TPU v7x, 32 devices: a whole 2x2x4 slice. The times are simulated.
32 devices in a mesh: tok: 8 (over z, y), voc: 4 (over x, core).
Axes of the slice: x: 2, y: 2, z: 4, core: 2. Of those that a mesh axis runs over, the one named last changes fastest.
Arguments:
- hidden: bfloat16 [2048, 1536], P('tok'), may hold values from -1000 to 1000
- norm_gain: float32 [1536], replicated, may hold values from 0.1 to 1.9
- head_weight: bfloat16 [1536, 49152], P(None, ('tok', 'voc')), may hold values from -8 to 8
- targets: int32 [2048], P('tok'), may hold values from 0 to 49151
- lengths: int32 [8], replicated, may hold values from 1 to 256, 1280 in all
- prior_device: int32 [8], replicated, may hold values from 0 to 7, each once
- prior_row: int32 [8], replicated, may hold values from 0 to 255
Outputs:
- logprob: float32 [2048], P('tok')
- entropy: float32 [2048], P('tok')
Inputs may be any that keep to these rules, and one draw needn't show every extreme that they name: One turn's block is full, lengths[t] = 256. `prior_device`: every block index appears once.
All inputs are finite; a program needn't handle non-finite values.
Results may differ from a plain program's by a relative error of at most 0.0036.
Values may be sent and summed in bfloat16 or wider, within the bound.
No kernel may reach another device: no remote copies, remote signals or barrier semaphores. Data moves between devices by JAX's collectives and lax.ppermute only.
A program may use at most 192 MiB of HBM per device.

v0:
```python
import jax
import jax.numpy as jnp
from jax import lax
from jax.sharding import PartitionSpec as P

epsilon = 1e-05


def select_entry(table, wanted):
    positions = jnp.arange(table.shape[0], dtype=jnp.int32)
    return jnp.sum(jnp.where(positions == wanted, table, 0))


def combine(first, second):
    largest = jnp.maximum(first[0], second[0])
    later = jnp.exp(second[0] - largest)
    return (largest, second[1] * later, second[2] * later, second[3])


def block_size(total_rows):
    for candidate in (512, 384, 256, 128):
        if total_rows % candidate == 0:
            return candidate
    return total_rows


def block_stats(states, columns, target_col):
    total_rows = states.shape[0]
    block_rows = block_size(total_rows)
    block_count = total_rows // block_rows
    column_ids = jnp.arange(columns.shape[1], dtype=jnp.int32)

    def score_block(inputs):
        state_rows, wanted = inputs
        logits = jnp.dot(state_rows, columns, preferred_element_type=jnp.float32)
        maxima = jnp.max(logits, axis=1)
        weights = jnp.exp(logits - maxima[:, None])
        totals = jnp.sum(weights, axis=1)
        moments = jnp.sum(weights * logits, axis=1)
        picked = jnp.sum(jnp.where(column_ids[None, :] == wanted[:, None], logits, 0.0), axis=1)
        return (maxima, totals, moments, picked)

    results = lax.map(
        score_block,
        (
            states.reshape(block_count, block_rows, states.shape[1]),
            target_col.reshape(block_count, block_rows),
        ),
    )
    return tuple((member.reshape(total_rows) for member in results))


def body(hidden, norm_gain, head_weight, targets, lengths, prior_device, prior_row):
    row_count = hidden.shape[0]
    col_width = head_weight.shape[1]
    tok_index = lax.axis_index("tok")
    band_index = lax.axis_index("voc")
    voc_count = lax.axis_size("voc")
    asked_row = jnp.sum(jnp.where(prior_device == tok_index, prior_row, 0))
    outgoing = lax.dynamic_slice_in_dim(hidden, asked_row, 1, 0)
    incoming = lax.all_gather(outgoing, "tok", axis=0, tiled=True)
    source = select_entry(prior_device, tok_index)
    chosen = jnp.arange(incoming.shape[0], dtype=jnp.int32) == source
    fetched = jnp.sum(
        jnp.where(chosen[:, None], incoming.astype(jnp.float32), 0.0), axis=0, keepdims=True
    )
    scored = jnp.concatenate([fetched, hidden[:-1].astype(jnp.float32)], axis=0)
    normed = (
        scored
        * lax.rsqrt(jnp.mean(scored * scored, axis=1, keepdims=True) + epsilon)
        * norm_gain[None, :]
    ).astype(jnp.bfloat16)
    owner_block = targets // col_width
    target_col = jnp.where(
        owner_block % voc_count == band_index,
        owner_block // voc_count * col_width + targets % col_width,
        -1,
    )
    zeroes = jnp.zeros((row_count,), jnp.float32)
    initial = (jnp.full((row_count,), -1e30, jnp.float32), zeroes, zeroes, zeroes)
    maxima, totals, moments, picked = combine(
        initial,
        block_stats(normed, lax.all_gather(head_weight, "tok", axis=1, tiled=True), target_col),
    )
    largest = lax.pmax(maxima, "voc")
    factor = jnp.exp(maxima - largest)
    totals, moments, picked = lax.psum((totals * factor, moments * factor, picked), "voc")
    maxima = largest
    normalizer = maxima + jnp.log(totals)
    logprob = picked - normalizer
    entropy = normalizer - moments / totals
    live_count = select_entry(lengths, tok_index)
    valid = jnp.arange(row_count, dtype=jnp.int32) < live_count
    return (jnp.where(valid, logprob, 0.0), jnp.where(valid, entropy, 0.0))


def solution(mesh):
    in_specs = (P("tok", None), P(), P(None, ("tok", "voc")), P("tok"), P(), P(), P())
    out_specs = (P("tok"), P("tok"))
    return jax.shard_map(body, mesh=mesh, in_specs=in_specs, out_specs=out_specs, check_vma=False)
```

profile of v0, /device:TPU:0, one launch (start us, length us, event | category | flops | bytes accessed | tf_op | source)
XLA Modules:
  0.0 777.2 jit_solution(7191092788528426236)
XLA Ops:
  7.2 0.0 copy-start.2
  7.2 0.0 copy-start.3
  7.2 0.0 copy-start
  7.2 0.0 all-gather.3.cloned.1.call-start
  7.2 0.7 all-gather.3.cloned.1.call-update
  7.9 0.0 copy-start.5
  7.9 0.0 copy-start.1
  7.9 0.0 copy-start.4
  8.0 0.0 copy-done.2
  8.0 0.0 copy-done.3
  8.0 0.6 fusion.7
  10.6 0.0 copy-done
  10.6 80.7 %all-gather = bf16[8,1,1536]{2,1,0:T(2,128)(2,1)S(1)} all-gather(bf16[1,1,1536]{2,1,0:T(2,128)(2,1)S(1)} %dynamic-slice_bitcast_fusion), channel_id=1, replica_groups=mesh['tok'=8,'voc'=4] {'tok'}, dimensions={0}, use_global_device_ids=true | all-gather | bytes 27648 | tf_op jit(solution)/shard_map/all_gather | solution.py:61
  91.3 0.1 convert_element_type.12
  91.4 0.7 iota_compare_fusion.2
  92.0 0.1 fusion.4
  92.1 0.2 slice_convert_fusion
  92.3 0.3 multiply_reduce_fusion.1
  92.6 0.0 copy-done.5
  92.6 0.7 fusion.6
  93.3 0.0 copy-done.1
  93.3 636.2 %all-gather.3.cloned.1.call-done = bf16[1536,12288]{1,0:T(8,128)(2,1)} async-done(((bf16[1536,1536]{1,0:T(8,128)(2,1)}), bf16[1536,12288]{1,0:T(8,128)(2,1)}) %all-gather.3.cloned.1.call-update) | async-done | bytes 37748752 | tf_op jit(solution)/shard_map/all_gather | solution.py:83
  729.5 0.0 copy-done.4
  729.5 19.5 %fusion.10 = (f32[256]{0:T(256)S(1)}, f32[256,12288]{1,0:T(8,128)}) fusion(bf16[1536,12288]{1,0:T(8,128)(2,1)} %all-gather.3.cloned.1.call-done, f32[255,1536]{1,0:T(8,128)S(1)} %slice_convert_fusion, f32[1,1536]{1,0:T(1,128)S(1)} %broadcast_in_dim.57, f32[1536]{0:T(1024)S(1)} %copy-done.4, f32[256]{0:T(256)S(1)} %add_rsqrt_fusion), kind=kOutput, calls=%fused_computation.42 | convolution fusion | flops 9668395008 | bytes 51912704 | tf_op jit(solution)/shard_map/while/body/eval_jaxpr/dot_general | solution.py:35
  749.0 6.8 pmax.7
  755.8 7.4 multiply_reduce_fusion
  763.2 5.9 all-reduce
  769.2 1.2 subtract_select_fusion
  (6 shorter events, 0.1 us)
Async XLA Ops:
  7.2 0.8 copy-start.2
  7.2 0.8 copy-start.3
  7.2 3.4 copy-start
  7.2 722.3 %all-gather.3.cloned.1.call-start = ((), (), s32[]{:S(2)}) async-start(), calls=%async_computation | async-start | bytes 42467328 | tf_op jit(solution)/shard_map/all_gather | solution.py:83
  7.9 84.7 %copy-start.5 = (s32[8]{0:T(128)S(1)}, s32[8]{0:T(128)}, u32[]{:S(2)}) copy-start(s32[8]{0:T(128)} %param.11) | copy-start | bytes 100
  7.9 85.4 %copy-start.1 = (s32[256]{0:T(256)S(1)}, s32[256]{0:T(256)}, u32[]{:S(2)}) copy-start(s32[256]{0:T(256)} %param.10) | copy-start | bytes 3076
  7.9 721.5 %copy-start.4 = (f32[1536]{0:T(1024)S(1)}, f32[1536]{0:T(1024)}, u32[]{:S(2)}) copy-start(f32[1536]{0:T(1024)} %param.8) | copy-start | bytes 18436
Sparse Core Ops, SparseCore 0:
  9.6 719.8 all-gather.2
where the time goes:
time: 777 us
  waiting for transfers between devices  637 us (82%)
  blocking collectives  93.5 us (12%)
  matrix products  19.5 us (3%)
  between operations  16.1 us (2%)
  other arithmetic  11.2 us (1%)
    all_gather x1, waiting for transfers between devices, body(): lax.all_gather(head_weight, 'tok', axis=1, tiled=True)  636 us
    all_gather x1, blocking collectives, body(): incoming = lax.all_gather(outgoing, 'tok', axis=0, tiled=True)  80.7 us
    dot_general x1, matrix products, score_block(): logits = jnp.dot(state_rows, columns, preferred_element_type=jnp.float32)  19.5 us
  transfers between devices with their start and end apart: 1, of which 1 were waited for; matrix products, arithmetic and copies ran while one was open for 0% of the time, Pallas kernels for 0%

commit v1 on v0

v1 whole, which is shorter than its diff:
```python
import functools

import jax
import jax.numpy as jnp
from jax import lax
from jax.experimental import pallas as pl
from jax.experimental.pallas import tpu as pltpu
from jax.sharding import PartitionSpec as P

epsilon = 1e-05
LANES = 128
SUB = 16
AXES = ("tok", "voc")


def score_kernel(layout, rows, width, nblocks, table, first, turns, targets, gain, head, *rest):
    pieces = rest[: len(layout)]
    out, states, logits, part_max, part_sum, part_moment, part_pick = rest[len(layout) :]
    feats = states.shape[1]
    tiles = head.shape[1] // LANES
    scale = gain[...]

    slot = 0
    for ref, count in zip(pieces, layout):
        size = ref.shape[0] // count
        for piece in range(count):
            place = table[slot]
            slot += 1

            def norm_rows(step, _, ref=ref, piece=piece, size=size, place=place):
                at = pl.multiple_of(piece * size + step * SUB, SUB)
                to = pl.multiple_of(place + step * SUB, SUB)
                value = ref[pl.ds(at, SUB), :].astype(jnp.float32)
                mean = jnp.sum(value * value, axis=1, keepdims=True) * (1.0 / feats)
                states[pl.ds(to, SUB), :] = (value * lax.rsqrt(mean + epsilon) * scale).astype(jnp.bfloat16)
                return 0

            lax.fori_loop(0, size // SUB, norm_rows, 0, unroll=2)

    me, base = table[slot], table[slot + 1]
    total_rows = nblocks * rows
    logits[...] = jnp.dot(states[...], head[...], preferred_element_type=jnp.float32)

    lane = lax.broadcasted_iota(jnp.int32, (1, rows), 1)
    for block in range(nblocks):
        position = table[slot + 2] + block
        turn = me ^ position
        prior_target = jnp.int32(0)
        for u in range(turns.shape[0]):
            prior_target = jnp.where(turns[u] == turn, first[u ^ me], prior_target)
        own = targets[pl.ds(position, 1), :]
        shifted = jnp.concatenate([own[:, 1:], own[:, :1]], axis=1)
        wanted = jnp.where(lane == rows - 1, prior_target, shifted) - base
        column = jnp.broadcast_to(wanted.astype(jnp.float32), (LANES, rows)).T
        part_pick[pl.ds(block * rows, rows), :] = column

    lanes = lax.broadcasted_iota(jnp.int32, (SUB, LANES), 1)
    lanes_f = lanes.astype(jnp.float32)

    def stats_rows(step, _):
        at = pl.ds(pl.multiple_of(step * SUB, SUB), SUB)

        def tile_of(k):
            value = logits[at, k * LANES : (k + 1) * LANES]
            if (k + 1) * LANES > width:
                value = jnp.where(lanes < width - k * LANES, value, -1e30)
            return value

        top = tile_of(0)
        for k in range(1, tiles):
            top = jnp.maximum(top, tile_of(k))
        offset = part_pick[at, :] - lanes_f
        total = jnp.zeros((SUB, LANES), jnp.float32)
        moment = total
        picked = total
        for k in range(tiles):
            value = tile_of(k)
            weight = jnp.exp(value - top)
            total = total + weight
            moment = moment + weight * value
            picked = picked + jnp.where(offset == float(k * LANES), value, 0.0)
        part_max[at, :] = top
        part_sum[at, :] = total
        part_moment[at, :] = moment
        part_pick[at, :] = picked
        return 0

    lax.fori_loop(0, total_rows // SUB, stats_rows, 0, unroll=2)

    halves = rows // LANES
    for block in range(nblocks):
        for half in range(halves):
            at = pl.ds(block * rows + half * LANES, LANES)
            top = part_max[at, :].T
            largest = jnp.max(top, axis=0, keepdims=True)
            factor = jnp.exp(top - largest)
            out[block, half : half + 1, :] = largest
            out[block, halves + half : halves + half + 1, :] = jnp.sum(part_sum[at, :].T * factor, axis=0, keepdims=True)
            out[block, 2 * halves + half : 2 * halves + half + 1, :] = jnp.sum(
                part_moment[at, :].T * factor, axis=0, keepdims=True
            )
            out[block, 3 * halves + half : 3 * halves + half + 1, :] = jnp.sum(part_pick[at, :].T, axis=0, keepdims=True)


def score(pieces, layout, table, first, turns, targets, gain, head, rows, width, nblocks):
    total_rows = nblocks * rows
    feats = gain.shape[1]
    columns = head.shape[1]
    smem = pl.BlockSpec(memory_space=pltpu.SMEM)
    vmem = pl.BlockSpec(memory_space=pltpu.VMEM)
    return pl.pallas_call(
        functools.partial(score_kernel, layout, rows, width, nblocks),
        out_shape=jax.ShapeDtypeStruct((nblocks, 4 * (rows // LANES), LANES), jnp.float32),
        in_specs=[smem] * 3 + [vmem] * (3 + len(pieces)),
        out_specs=vmem,
        scratch_shapes=[
            pltpu.VMEM((total_rows, feats), jnp.bfloat16),
            pltpu.VMEM((total_rows, columns), jnp.float32),
        ]
        + [pltpu.VMEM((total_rows, LANES), jnp.float32)] * 4,
        compiler_params=pltpu.CompilerParams(vmem_limit_bytes=40 * 1024 * 1024),
        cost_estimate=pl.CostEstimate(
            flops=2 * total_rows * feats * columns,
            bytes_accessed=2 * feats * (total_rows + columns),
            transcendentals=total_rows * columns,
        ),
    )(table, first, turns, targets, gain, head, *pieces)


def collect_kernel(turn_count, voc_count, tail, table, turns, *rest):
    stats, out, held = rest[:-2], rest[-2], rest[-1]
    me = table[0]
    per = stats[0].shape[0]
    for index, ref in enumerate(stats):
        for block in range(per):
            held[(index * per + block) ^ me] = ref[block]
    shape = held.shape[1:]
    row = lax.broadcasted_iota(jnp.int32, shape, 0)
    lane = lax.broadcasted_iota(jnp.int32, shape, 1)
    swap = (lane == LANES - 1) & (row % tail == tail - 1)
    for turn in range(turn_count):
        value = jnp.where(swap, held[turns[turn]], held[turn])
        for copy in range(voc_count):
            out[turn * voc_count + copy] = value


def collect(stats, table, turns, turn_count, voc_count):
    smem = pl.BlockSpec(memory_space=pltpu.SMEM)
    vmem = pl.BlockSpec(memory_space=pltpu.VMEM)
    sublanes = stats[0].shape[1]
    return pl.pallas_call(
        functools.partial(collect_kernel, turn_count, voc_count, sublanes // 4),
        out_shape=jax.ShapeDtypeStruct((turn_count * voc_count, sublanes, LANES), jnp.float32),
        in_specs=[smem] * 2 + [vmem] * len(stats),
        out_specs=vmem,
        scratch_shapes=[pltpu.VMEM((turn_count, sublanes, LANES), jnp.float32)],
    )(table, turns, *stats)


def finish_kernel(table, lengths, received, logprob, entropy):
    halves = received.shape[1] // 4
    top = received[:, 0:halves, :]
    largest = jnp.max(top, axis=0)
    factor = jnp.exp(top - largest[None])
    total = jnp.sum(received[:, halves : 2 * halves, :] * factor, axis=0)
    moment = jnp.sum(received[:, 2 * halves : 3 * halves, :] * factor, axis=0)
    picked = jnp.sum(received[:, 3 * halves :, :], axis=0)
    normalizer = largest + jnp.log(total)
    half = lax.broadcasted_iota(jnp.int32, largest.shape, 0)
    lane = lax.broadcasted_iota(jnp.int32, largest.shape, 1)
    live = half * LANES + lane < lengths[table[0]]

    def by_scored_row(value):
        previous = jnp.concatenate([value[halves - 1 :], value[: halves - 1]], axis=0)
        rolled = jnp.concatenate([value[:, LANES - 1 :], value[:, : LANES - 1]], axis=1)
        rolled_previous = jnp.concatenate([previous[:, LANES - 1 :], previous[:, : LANES - 1]], axis=1)
        return jnp.where(live, jnp.where(lane == 0, rolled_previous, rolled), 0.0)

    logprob[...] = by_scored_row(picked - normalizer)
    entropy[...] = by_scored_row(normalizer - moment / total)


def finish(table, lengths, received):
    smem = pl.BlockSpec(memory_space=pltpu.SMEM)
    vmem = pl.BlockSpec(memory_space=pltpu.VMEM)
    halves = received.shape[1] // 4
    shape = jax.ShapeDtypeStruct((halves, LANES), jnp.float32)
    return pl.pallas_call(
        finish_kernel, out_shape=(shape, shape), in_specs=[smem, smem, vmem], out_specs=(vmem, vmem)
    )(table, lengths, received)


def after(value, *others):
    return lax.optimization_barrier((value,) + others)[0]


def body(hidden, norm_gain, head_weight, targets, lengths, prior_device, prior_row):
    rows, feats = hidden.shape
    width = head_weight.shape[1]
    tok_count, voc_count = lax.axis_size("tok"), lax.axis_size("voc")
    side = voc_count // 2
    depth = tok_count // side
    me, band = lax.axis_index("tok"), lax.axis_index("voc")
    core = band % 2
    quarter = rows // voc_count
    half = rows // 2

    def permute(value, move):
        pairs = []
        for t in range(tok_count):
            for v in range(voc_count):
                to_t, to_v = move(t, v)
                pairs.append((t * voc_count + v, to_t * voc_count + to_v))
        return lax.ppermute(value, AXES, pairs)

    def along_z(value, d):
        return permute(value, lambda t, v: (t ^ (d * side), v))

    def along_y(value, d):
        return permute(value, lambda t, v: (t ^ d, v))

    def across_cores(value):
        return permute(value, lambda t, v: (t, v ^ 1))

    def second_hop(value, d):
        return permute(value, lambda t, v: (t ^ d, v) if v % 2 == 0 else (t, v ^ (2 * d)))

    def third_hop(value, d):
        return permute(value, lambda t, v: (t, v ^ (2 * d)) if v % 2 == 0 else (t ^ d, v))

    asked = jnp.sum(jnp.where(prior_device == me, prior_row, 0))
    asked_state = lax.dynamic_slice_in_dim(hidden, asked, 1, 0)
    row_ids = lax.broadcasted_iota(jnp.int32, (rows, 1), 0)
    block = jnp.where(row_ids == rows - 1, asked_state, hidden)

    own_quarter = lax.dynamic_slice_in_dim(block, band * quarter, quarter, 0)
    own_half = lax.dynamic_slice_in_dim(block, core * half, half, 0)

    near = [along_y(own_half, d) for d in range(1, side)]
    arrived = {1: along_z(own_quarter, 1)}
    for d in range(2, depth):
        arrived[d] = along_z(own_quarter if d == 2 else after(own_quarter, arrived[d - 2]), d)

    known = targets.reshape(1, rows)
    step = 1
    while step < tok_count:
        moved = lax.ppermute(known, "tok", [(i, i ^ step) for i in range(tok_count)])
        known = jnp.concatenate([known, moved], axis=0)
        step *= 2
    first = known[:, 0]
    base = (me * voc_count + band) * width
    gain = norm_gain.reshape(1, feats)
    head = head_weight
    if width % LANES:
        head = jnp.pad(head_weight, ((0, 0), (0, LANES - width % LANES)))

    def places(core_id, band_id):
        result = []
        for d in range(side):
            y, x = jnp.where(core_id == 0, d, 0), jnp.where(core_id == 0, 0, d)
            result.append(y * rows + (band_id ^ (2 * x)) * quarter)
        for d in range(1, side):
            for e in range(side):
                y, x = jnp.where(core_id == 0, e, d), jnp.where(core_id == 0, d, e)
                result.append(y * rows + (band_id ^ (2 * x)) * quarter)
        return result

    common = [me, base]
    stats = []
    pieces = [block]
    where = [0]
    layout = [1]
    for d in range(1, side):
        pieces += [near[d - 1], across_cores(near[d - 1])]
        where += [d * rows + core * half, d * rows + (1 - core) * half]
        layout += [1, 1]
    table = jnp.stack([jnp.asarray(p, jnp.int32) for p in where + common + [0]])
    stats.append(score(pieces, layout, table, first, prior_device, known, gain, head, rows, width, side))

    where = places(core, band) + places(1 - core, band ^ 1)
    for d in range(1, depth):
        near_pieces = [arrived[d]] + [second_hop(arrived[d], e) for e in range(1, side)]
        gathered = jnp.concatenate(near_pieces, axis=0)
        far = [third_hop(gathered, e) for e in range(1, side)]
        pieces = [gathered] + far + [across_cores(gathered)] + [across_cores(f) for f in far]
        table = jnp.stack([jnp.asarray(p, jnp.int32) for p in where + common + [d * side]])
        stats.append(
            score(pieces, [side] * len(pieces), table, first, prior_device, known, gain, head, rows, width, side)
        )

    spot = jnp.reshape(me, (1,)).astype(jnp.int32)
    sent = collect(stats, spot, prior_device, tok_count, voc_count)
    received = lax.all_to_all(sent, AXES, 0, 0)
    logprob, entropy = finish(spot, lengths, received)
    return logprob.reshape(rows), entropy.reshape(rows)


def solution(mesh):
    in_specs = (P("tok", None), P(), P(None, ("tok", "voc")), P("tok"), P(), P(), P())
    out_specs = (P("tok"), P("tok"))
    return jax.shard_map(body, mesh=mesh, in_specs=in_specs, out_specs=out_specs, check_vma=False)
```

time: 777 us -> 90.8 us (0.12)
  waiting for transfers between devices: 637 us -> 14.1 us
  blocking collectives: 93.5 us -> 12.3 us
  Pallas kernels: 0 us -> 29.4 us
  starting transfers between devices: 0.04 us -> 21.5 us
  matrix products: 19.5 us -> 0 us
  between operations: 16.1 us -> 2.79 us
    all_gather x1 -> x0, waiting for transfers between devices: 636 us -> none  [body(): lax.all_gather(head_weight, 'tok', axis=1, tiled=True)]
    all_gather x1 -> x0, blocking collectives: 80.7 us -> none  [body(): incoming = lax.all_gather(outgoing, 'tok', axis=0, tiled=True)]
    pallas_call x0 -> x6, Pallas kernels: none -> 29.4 us  [the longest x4 26.3 us: score(): pl.pallas_call(functools.partial(score_kernel, layout, rows, width, nbloc...]
    ppermute x0 -> x20, starting transfers between devices: none -> 21.5 us  [the longest x17 18.2 us: permute(): return lax.ppermute(value, AXES, pairs)]
    dot_general x1 -> x0, matrix products: 19.5 us -> none  [score_block(): logits = jnp.dot(state_rows, columns, preferred_element_type=jnp.float32)]
    ppermute x0 -> x20, waiting for transfers between devices: none -> 14.1 us  [the longest x17 10.3 us: permute(): return lax.ppermute(value, AXES, pairs)]
    all_to_all x0 -> x1, blocking collectives: none -> 12.3 us  [body(): received = lax.all_to_all(sent, AXES, 0, 0)]
  transfers between devices with their start and end apart: 1 -> 20, of which waited for: 1 -> 5; matrix products, arithmetic and copies ran while one was open for 0% -> 3% of each run, Pallas kernels for 0% -> 22%
where the time goes in v1:
time: 90.8 us; the launch traced here: 90.3 us
  Pallas kernels  29.4 us (32%)
  starting transfers between devices  21.5 us (24%)
  waiting for transfers between devices  14.1 us (16%)
  blocking collectives  12.3 us (14%)
  local copies, waits for them, and re-layouts  6.17 us (7%)
  other arithmetic  3.96 us (4%)
  between operations  2.79 us (3%)
    pallas_call x4, Pallas kernels, score(): pl.pallas_call(functools.partial(score_kernel, layout, rows, width, nbloc...  26.3 us
    ppermute x17, starting transfers between devices, permute(): return lax.ppermute(value, AXES, pairs)  18.2 us
    all_to_all x1, blocking collectives, body(): received = lax.all_to_all(sent, AXES, 0, 0)  12.3 us
    ppermute x17, waiting for transfers between devices, permute(): return lax.ppermute(value, AXES, pairs)  10.3 us
    unnamed x17, local copies, waits for them, and re-layouts  4.15 us
    ppermute x3, waiting for transfers between devices, body(): lax.ppermute(known, 'tok', [(i, i ^ step) for i in range(tok_count)])  3.75 us
    ppermute x3, starting transfers between devices, body(): lax.ppermute(known, 'tok', [(i, i ^ step) for i in range(tok_count)])  3.28 us
  transfers between devices with their start and end apart: 20, of which 5 were waited for; matrix products, arithmetic and copies ran while one was open for 3% of the time, Pallas kernels for 22%

profile of v1, /device:TPU:0, one launch (start us, length us, event | category | flops | bytes accessed | tf_op | source)
XLA Modules:
  0.0 90.3 jit_solution(9112152590552553644)
XLA Ops:
  0.6 0.0 copy-start.4
  0.6 0.0 copy-start.6
  0.7 1.3 %fusion = s32[]{:T(128)} fusion(s32[8]{0:T(128)} %param.13, s32[8]{0:T(128)} %turns.9, s32[]{:T(128)} %axis_index.23), kind=kLoop, calls=%fused_computation.16 | loop fusion | flops 23 | bytes 72 | tf_op jit(solution)/shard_map/reduce_sum | solution.py:231
  3.9 0.8 dynamic-slice_reduce_fusion
  4.7 1.3 %broadcast_select_fusion.rest_0_ = bf16[256,1536]{1,0:T(8,128)(2,1)S(1)} fusion(bf16[256,1536]{1,0:T(8,128)(2,1)} %param.7, pred[256]{0:T(512)(128)(4,1)S(1)} %iota_compare_fusion, bf16[1536]{0:T(1024)(128)(2,1)S(1)} %dynamic-slice_reduce_fusion), kind=kLoop, calls=%fused_computation | loop fusion | flops 393216 | bytes 1576192 | tf_op jit(solution)/shard_map/jit(_where)/select_n | solution.py:234
  6.0 3.1 %collective-permute-start.5 = (bf16[64,1536]{1,0:T(8,128)(2,1)S(1)}, bf16[64,1536]{1,0:T(8,128)(2,1)S(1)}, u32[]{:S(2)}, u32[]{:S(2)}) collective-permute-start(bf16[64,1536]{1,0:T(8,128)(2,1)S(1)} %constant_dynamic-slice_fusion), channel_id=1, source_target_pairs={{0,8},{1,9},{2,10},{3,11},{4,12},{5,13},{6,14},{7,15},{8,0},{9,1},... | collective-permute-start | bytes 589832 | tf_op jit(solution)/shard_map/ppermute | solution.py:214
  9.1 2.6 %collective-permute-start.10 = (bf16[64,1536]{1,0:T(8,128)(2,1)S(1)}, bf16[64,1536]{1,0:T(8,128)(2,1)S(1)}, u32[]{:S(2)}, u32[]{:S(2)}) collective-permute-start(bf16[64,1536]{1,0:T(8,128)(2,1)S(1)} %constant_dynamic-slice_fusion), channel_id=1, source_target_pairs={{0,16},{1,17},{2,18},{3,19},{4,20},{5,21},{6,22},{7,23},{8,24},{9,... | collective-permute-start | bytes 589832 | tf_op jit(solution)/shard_map/ppermute | solution.py:214
  11.7 1.5 %collective-permute-start = (s32[1,256]{1,0:T(1,128)}, s32[1,256]{1,0:T(1,128)S(1)}, u32[]{:S(2)}, u32[]{:S(2)}) collective-permute-start(s32[1,256]{1,0:T(1,128)} %bitcast.15), channel_id=1, source_target_pairs={{0,4},{4,0},{8,12},{12,8},{16,20},{20,16},{24,28},{28,24},{1,5},{5... | collective-permute-start | bytes 3080 | tf_op jit(solution)/shard_map/ppermute | solution.py:247
  13.2 0.6 collective-permute-start.3
  13.8 1.7 %collective-permute-done = s32[1,256]{1,0:T(1,128)S(1)} collective-permute-done((s32[1,256]{1,0:T(1,128)}, s32[1,256]{1,0:T(1,128)S(1)}, u32[]{:S(2)}, u32[]{:S(2)}) %collective-permute-start) | collective-permute-done | bytes 1056 | tf_op jit(solution)/shard_map/ppermute | solution.py:247
  15.5 0.7 pad_add_fusion.2
  16.2 0.4 collective-permute-start.1
  16.6 0.7 reshape.26.gain
  17.3 0.1 stack.80.table
  17.4 0.1 stack.81.table
  17.5 0.1 stack.82.table
  17.6 0.1 stack.33.table
  17.7 2.1 %collective-permute-done.1 = s32[2,256]{1,0:T(2,128)S(1)} collective-permute-done((s32[2,256]{1,0:T(2,128)S(1)}, s32[2,256]{1,0:T(2,128)S(1)}, u32[]{:S(2)}, u32[]{:S(2)}) %collective-permute-start.1) | collective-permute-done | bytes 2080 | tf_op jit(solution)/shard_map/ppermute | solution.py:247
  19.7 0.7 pad_add_fusion.1
  20.4 1.3 %collective-permute-start.2 = (s32[4,256]{1,0:T(4,128)S(1)}, s32[4,256]{1,0:T(4,128)S(1)}, u32[]{:S(2)}, u32[]{:S(2)}) collective-permute-start(s32[4,256]{1,0:T(4,128)S(1)} %pad_add_fusion.1), channel_id=1, source_target_pairs={{0,16},{4,20},{8,24},{12,28},{16,0},{20,4},{24,8},{28,12},{1,17},{... | collective-permute-start | bytes 12296 | tf_op jit(solution)/shard_map/ppermute | solution.py:247
  21.7 0.0 collective-permute-done.5
  21.7 1.5 %collective-permute-start.15 = (bf16[64,1536]{1,0:T(8,128)(2,1)S(1)}, bf16[64,1536]{1,0:T(8,128)(2,1)S(1)}, u32[]{:S(2)}, u32[]{:S(2)}) collective-permute-start(bf16[64,1536]{1,0:T(8,128)(2,1)S(1)} %constant_dynamic-slice_fusion), channel_id=1, source_target_pairs={{0,24},{1,25},{2,26},{3,27},{4,28},{5,29},{6,30},{7,31},{8,16},{9,... | collective-permute-start | bytes 589832 | tf_op jit(solution)/shard_map/ppermute | solution.py:214
  23.2 1.6 %collective-permute-start.6 = (bf16[64,1536]{1,0:T(8,128)(2,1)S(1)}, bf16[64,1536]{1,0:T(8,128)(2,1)S(1)}, u32[]{:S(2)}, u32[]{:S(2)}) collective-permute-start(bf16[64,1536]{1,0:T(8,128)(2,1)S(1)} %collective-permute-done.5), channel_id=1, source_target_pairs={{0,4},{1,3},{2,6},{3,1},{4,0},{5,7},{6,2},{7,5},{8,12},{9,11},{10,... | collective-permute-start | bytes 589832 | tf_op jit(solution)/shard_map/ppermute | solution.py:214
  24.9 0.0 collective-permute-done.10
  24.9 0.5 collective-permute-start.11
  25.4 3.5 %collective-permute-done.6 = bf16[64,1536]{1,0:T(8,128)(2,1)S(1)} collective-permute-done((bf16[64,1536]{1,0:T(8,128)(2,1)S(1)}, bf16[64,1536]{1,0:T(8,128)(2,1)S(1)}, u32[]{:S(2)}, u32[]{:S(2)}) %collective-permute-start.6) | collective-permute-done | bytes 196640 | tf_op jit(solution)/shard_map/ppermute | solution.py:214
  28.9 1.6 %collective-permute-start.7 = (bf16[128,1536]{1,0:T(8,128)(2,1)S(1)}, bf16[128,1536]{1,0:T(8,128)(2,1)S(1)}, u32[]{:S(2)}, u32[]{:S(2)}) collective-permute-start(bf16[128,1536]{1,0:T(8,128)(2,1)S(1)} %constant_dynamic-update-slice_fusion.rest_0_), channel_id=1, source_target_pairs={{0,2},{1,5},{2,0},{3,7},{4,6},{5,1},{6,4},{7,3},{8,10},{9,13},{10,... | collective-permute-start | bytes 1179656 | tf_op jit(solution)/shard_map/ppermute | solution.py:214
  30.5 0.0 collective-permute-done.15
  30.5 0.0 collective-permute-start.8
  30.5 2.5 %collective-permute-done.11 = bf16[64,1536]{1,0:T(8,128)(2,1)S(1)} collective-permute-done((bf16[64,1536]{1,0:T(8,128)(2,1)S(1)}, bf16[64,1536]{1,0:T(8,128)(2,1)S(1)}, u32[]{:S(2)}, u32[]{:S(2)}) %collective-permute-start.11) | collective-permute-done | bytes 196640 | tf_op jit(solution)/shard_map/ppermute | solution.py:214
  33.0 1.9 %collective-permute-start.16 = (bf16[64,1536]{1,0:T(8,128)(2,1)S(1)}, bf16[64,1536]{1,0:T(8,128)(2,1)S(1)}, u32[]{:S(2)}, u32[]{:S(2)}) collective-permute-start(bf16[64,1536]{1,0:T(8,128)(2,1)S(1)} %collective-permute-done.15), channel_id=1, source_target_pairs={{0,4},{1,3},{2,6},{3,1},{4,0},{5,7},{6,2},{7,5},{8,12},{9,11},{10,... | collective-permute-start | bytes 589832 | tf_op jit(solution)/shard_map/ppermute | solution.py:214
  35.0 0.0 collective-permute-done.3.rest_1_
  35.0 1.6 %collective-permute-start.12 = (bf16[128,1536]{1,0:T(8,128)(2,1)S(1)}, bf16[128,1536]{1,0:T(8,128)(2,1)S(1)}, u32[]{:S(2)}, u32[]{:S(2)}) collective-permute-start(bf16[128,1536]{1,0:T(8,128)(2,1)S(1)} %constant_dynamic-update-slice_fusion.2.rest_0_), channel_id=1, source_target_pairs={{0,2},{1,5},{2,0},{3,7},{4,6},{5,1},{6,4},{7,3},{8,10},{9,13},{10,... | collective-permute-start | bytes 1179656 | tf_op jit(solution)/shard_map/ppermute | solution.py:214
  36.5 4.3 %collective-permute-done.16 = bf16[64,1536]{1,0:T(8,128)(2,1)S(1)} collective-permute-done((bf16[64,1536]{1,0:T(8,128)(2,1)S(1)}, bf16[64,1536]{1,0:T(8,128)(2,1)S(1)}, u32[]{:S(2)}, u32[]{:S(2)}) %collective-permute-start.16) | collective-permute-done | bytes 196640 | tf_op jit(solution)/shard_map/ppermute | solution.py:214
  40.8 0.0 collective-permute-start.4
  40.8 0.0 collective-permute-done.2
  40.9 1.6 %collective-permute-start.17 = (bf16[128,1536]{1,0:T(8,128)(2,1)S(1)}, bf16[128,1536]{1,0:T(8,128)(2,1)S(1)}, u32[]{:S(2)}, u32[]{:S(2)}) collective-permute-start(bf16[128,1536]{1,0:T(8,128)(2,1)S(1)} %constant_dynamic-update-slice_fusion.4.rest_0_), channel_id=1, source_target_pairs={{0,2},{1,5},{2,0},{3,7},{4,6},{5,1},{6,4},{7,3},{8,10},{9,13},{10,... | collective-permute-start | bytes 1179656 | tf_op jit(solution)/shard_map/ppermute | solution.py:214
  42.4 0.0 collective-permute-done.7.rest_1_
  42.4 0.7 collective-permute-start.9
  43.1 0.1 slice_reduce_fusion.first
  43.2 0.0 collective-permute-done.4.rest_2_
  43.2 0.1 collective-permute-start.13
  43.3 0.0 collective-permute-done.12.rest_1_
  43.3 0.5 collective-permute-start.14
  43.8 2.3 %copy-done.5 = bf16[1536,1536]{1,0:T(8,128)(2,1)S(1)} copy-done((bf16[1536,1536]{1,0:T(8,128)(2,1)S(1)}, bf16[1536,1536]{1,0:T(8,128)(2,1)}, u32[]{:S(2)}) %copy-start.5) | copy-done | bytes 4718616
  46.2 6.6 %shard_map.86.rest_0_ = f32[2,8,128]{2,1,0:T(8,128)S(1)} custom-call(s32[6]{0:T(128)S(1)} %stack.33.table, s32[8]{0:T(128)S(1)} %slice_reduce_fusion.first, s32[8]{0:T(128)S(1)} %copy-done.4, s32[8,256]{1,0:T(8,128)S(1)} %pad_add_fusion.targets, f32[1,1536]{1,0:T(1,128)S(1)} %reshape.26.gain, bf16[1536,1536]{1,0:T(8,128)(2,1)S(1)} %copy-done.5, ...), custom_call_target="tpu_custom_call" | custom-call | flops 2415919104 | bytes 6291456 | tf_op jit(solution)/shard_map/pallas_call | solution.py:111
  52.8 0.6 copy-done
  53.3 0.0 collective-permute-done.8.rest_2_
  53.3 0.1 collective-permute-start.18
  53.4 0.0 collective-permute-done.17.rest_1_
  53.4 0.4 collective-permute-start.19
  53.9 0.0 collective-permute-done.9.rest_3_
  53.9 6.6 %shard_map.87.rest_1_ = f32[2,8,128]{2,1,0:T(8,128)S(1)} custom-call(s32[11]{0:T(128)S(1)} %stack.80.table, s32[8]{0:T(128)S(1)} %slice_reduce_fusion.first, s32[8]{0:T(128)S(1)} %copy-done.4, s32[8,256]{1,0:T(8,128)S(1)} %pad_add_fusion.targets, f32[1,1536]{1,0:T(1,128)S(1)} %reshape.26.gain, bf16[1536,1536]{1,0:T(8,128)(2,1)S(1)} %copy-done.5, ...), custom_call_target="tpu_custom_call" | custom-call | flops 2415919104 | bytes 6291456 | tf_op jit(solution)/shard_map/pallas_call | solution.py:111
  60.5 0.0 collective-permute-done.13.rest_2_
  60.5 0.0 collective-permute-done.14.rest_3_
  60.5 6.6 %shard_map.88.rest_2_ = f32[2,8,128]{2,1,0:T(8,128)S(1)} custom-call(s32[11]{0:T(128)S(1)} %stack.81.table, s32[8]{0:T(128)S(1)} %slice_reduce_fusion.first, s32[8]{0:T(128)S(1)} %copy-done.4, s32[8,256]{1,0:T(8,128)S(1)} %pad_add_fusion.targets, f32[1,1536]{1,0:T(1,128)S(1)} %reshape.26.gain, bf16[1536,1536]{1,0:T(8,128)(2,1)S(1)} %copy-done.5, ...), custom_call_target="tpu_custom_call" | custom-call | flops 2415919104 | bytes 6291456 | tf_op jit(solution)/shard_map/pallas_call | solution.py:111
  67.1 0.6 copy-done.2
  67.7 0.0 collective-permute-done.18.rest_2_
  67.7 0.0 collective-permute-done.19.rest_3_
  67.7 6.6 %shard_map.89.rest_3_ = f32[2,8,128]{2,1,0:T(8,128)S(1)} custom-call(s32[11]{0:T(128)S(1)} %stack.82.table, s32[8]{0:T(128)S(1)} %slice_reduce_fusion.first, s32[8]{0:T(128)S(1)} %copy-done.4, s32[8,256]{1,0:T(8,128)S(1)} %pad_add_fusion.targets, f32[1,1536]{1,0:T(1,128)S(1)} %reshape.26.gain, bf16[1536,1536]{1,0:T(8,128)(2,1)S(1)} %copy-done.5, ...), custom_call_target="tpu_custom_call" | custom-call | flops 2415919104 | bytes 6291456 | tf_op jit(solution)/shard_map/pallas_call | solution.py:111
  74.3 0.6 copy-done.3
  74.8 1.5 %shard_map.90 = f32[32,8,128]{2,1,0:T(8,128)} custom-call(s32[1]{0:T(128)} %bitcast.table, s32[8]{0:T(128)} %turns.9, f32[2,8,128]{2,1,0:T(8,128)} %copy-done, f32[2,8,128]{2,1,0:T(8,128)} %copy-done.1, f32[2,8,128]{2,1,0:T(8,128)} %copy-done.2, f32[2,8,128]{2,1,0:T(8,128)} %copy-done.3), custom_call_target="tpu_custom_call" | custom-call | tf_op jit(solution)/shard_map/pallas_call | solution.py:151
  76.3 12.3 %all_to_all.5.received = f32[32,8,128]{2,1,0:T(8,128)} all-to-all(f32[32,8,128]{2,1,0:T(8,128)} %shard_map.90), channel_id=1, replica_groups=mesh['tok'=8,'voc'=4] {'tok','voc'}, dimensions={0} | all-to-all | bytes 262144 | tf_op jit(solution)/shard_map/all_to_all | solution.py:293
  88.7 1.6 %shard_map.91 = (f32[2,128]{1,0:T(2,128)}, f32[2,128]{1,0:T(2,128)}) custom-call(s32[1]{0:T(128)} %bitcast.table, s32[8]{0:T(128)} %lengths.1, f32[32,8,128]{2,1,0:T(8,128)} %all_to_all.5.received), custom_call_target="tpu_custom_call" | custom-call | tf_op jit(solution)/shard_map/pallas_call | solution.py:188
  (18 shorter events, 0.2 us)
Async XLA Ops:
  0.6 43.2 %copy-start.4 = (s32[8]{0:T(128)S(1)}, s32[8]{0:T(128)}, u32[]{:S(2)}) copy-start(s32[8]{0:T(128)} %turns.9) | copy-start | bytes 100
  0.6 42.5 %copy-start.6 = (s32[256]{0:T(256)S(1)}, s32[256]{0:T(256)}, u32[]{:S(2)}) copy-start(s32[256]{0:T(256)} %param.10) | copy-start | bytes 3076
  6.0 15.7 %collective-permute-start.5 = (bf16[64,1536]{1,0:T(8,128)(2,1)S(1)}, bf16[64,1536]{1,0:T(8,128)(2,1)S(1)}, u32[]{:S(2)}, u32[]{:S(2)}) collective-permute-start(bf16[64,1536]{1,0:T(8,128)(2,1)S(1)} %constant_dynamic-slice_fusion), channel_id=1, source_target_pairs={{0,8},{1,9},{2,10},{3,11},{4,12},{5,13},{6,14},{7,15},{8,0},{9,1},... | collective-permute-start | bytes 589832 | tf_op jit(solution)/shard_map/ppermute | solution.py:214
  9.1 15.8 %collective-permute-start.10 = (bf16[64,1536]{1,0:T(8,128)(2,1)S(1)}, bf16[64,1536]{1,0:T(8,128)(2,1)S(1)}, u32[]{:S(2)}, u32[]{:S(2)}) collective-permute-start(bf16[64,1536]{1,0:T(8,128)(2,1)S(1)} %constant_dynamic-slice_fusion), channel_id=1, source_target_pairs={{0,16},{1,17},{2,18},{3,19},{4,20},{5,21},{6,22},{7,23},{8,24},{9,... | collective-permute-start | bytes 589832 | tf_op jit(solution)/shard_map/ppermute | solution.py:214
  11.7 3.8 %collective-permute-start = (s32[1,256]{1,0:T(1,128)}, s32[1,256]{1,0:T(1,128)S(1)}, u32[]{:S(2)}, u32[]{:S(2)}) collective-permute-start(s32[1,256]{1,0:T(1,128)} %bitcast.15), channel_id=1, source_target_pairs={{0,4},{4,0},{8,12},{12,8},{16,20},{20,16},{24,28},{28,24},{1,5},{5... | collective-permute-start | bytes 3080 | tf_op jit(solution)/shard_map/ppermute | solution.py:247
  13.2 21.7 %collective-permute-start.3 = (bf16[128,1536]{1,0:T(8,128)(2,1)S(1)}, bf16[128,1536]{1,0:T(8,128)(2,1)S(1)}, u32[]{:S(2)}, u32[]{:S(2)}) collective-permute-start(bf16[128,1536]{1,0:T(8,128)(2,1)S(1)} %constant_dynamic-slice_fusion.1), channel_id=1, source_target_pairs={{0,4},{1,5},{2,6},{3,7},{4,0},{5,1},{6,2},{7,3},{8,12},{9,13},{10,... | collective-permute-start | bytes 1179656 | tf_op jit(solution)/shard_map/ppermute | solution.py:214
  16.2 3.6 %collective-permute-start.1 = (s32[2,256]{1,0:T(2,128)S(1)}, s32[2,256]{1,0:T(2,128)S(1)}, u32[]{:S(2)}, u32[]{:S(2)}) collective-permute-start(s32[2,256]{1,0:T(2,128)S(1)} %pad_add_fusion.2), channel_id=1, source_target_pairs={{0,8},{4,12},{8,0},{12,4},{16,24},{20,28},{24,16},{28,20},{1,9},{5... | collective-permute-start | bytes 6152 | tf_op jit(solution)/shard_map/ppermute | solution.py:247
  20.4 20.4 %collective-permute-start.2 = (s32[4,256]{1,0:T(4,128)S(1)}, s32[4,256]{1,0:T(4,128)S(1)}, u32[]{:S(2)}, u32[]{:S(2)}) collective-permute-start(s32[4,256]{1,0:T(4,128)S(1)} %pad_add_fusion.1), channel_id=1, source_target_pairs={{0,16},{4,20},{8,24},{12,28},{16,0},{20,4},{24,8},{28,12},{1,17},{... | collective-permute-start | bytes 12296 | tf_op jit(solution)/shard_map/ppermute | solution.py:247
  21.7 8.7 %collective-permute-start.15 = (bf16[64,1536]{1,0:T(8,128)(2,1)S(1)}, bf16[64,1536]{1,0:T(8,128)(2,1)S(1)}, u32[]{:S(2)}, u32[]{:S(2)}) collective-permute-start(bf16[64,1536]{1,0:T(8,128)(2,1)S(1)} %constant_dynamic-slice_fusion), channel_id=1, source_target_pairs={{0,24},{1,25},{2,26},{3,27},{4,28},{5,29},{6,30},{7,31},{8,16},{9,... | collective-permute-start | bytes 589832 | tf_op jit(solution)/shard_map/ppermute | solution.py:214
  23.2 5.7 %collective-permute-start.6 = (bf16[64,1536]{1,0:T(8,128)(2,1)S(1)}, bf16[64,1536]{1,0:T(8,128)(2,1)S(1)}, u32[]{:S(2)}, u32[]{:S(2)}) collective-permute-start(bf16[64,1536]{1,0:T(8,128)(2,1)S(1)} %collective-permute-done.5), channel_id=1, source_target_pairs={{0,4},{1,3},{2,6},{3,1},{4,0},{5,7},{6,2},{7,5},{8,12},{9,11},{10,... | collective-permute-start | bytes 589832 | tf_op jit(solution)/shard_map/ppermute | solution.py:214
  24.9 8.1 %collective-permute-start.11 = (bf16[64,1536]{1,0:T(8,128)(2,1)S(1)}, bf16[64,1536]{1,0:T(8,128)(2,1)S(1)}, u32[]{:S(2)}, u32[]{:S(2)}) collective-permute-start(bf16[64,1536]{1,0:T(8,128)(2,1)S(1)} %collective-permute-done.10), channel_id=1, source_target_pairs={{0,4},{1,3},{2,6},{3,1},{4,0},{5,7},{6,2},{7,5},{8,12},{9,11},{10,... | collective-permute-start | bytes 589832 | tf_op jit(solution)/shard_map/ppermute | solution.py:214
  28.9 13.5 %collective-permute-start.7 = (bf16[128,1536]{1,0:T(8,128)(2,1)S(1)}, bf16[128,1536]{1,0:T(8,128)(2,1)S(1)}, u32[]{:S(2)}, u32[]{:S(2)}) collective-permute-start(bf16[128,1536]{1,0:T(8,128)(2,1)S(1)} %constant_dynamic-update-slice_fusion.rest_0_), channel_id=1, source_target_pairs={{0,2},{1,5},{2,0},{3,7},{4,6},{5,1},{6,4},{7,3},{8,10},{9,13},{10,... | collective-permute-start | bytes 1179656 | tf_op jit(solution)/shard_map/ppermute | solution.py:214
  30.5 22.8 %collective-permute-start.8 = (bf16[128,1536]{1,0:T(8,128)(2,1)S(1)}, bf16[128,1536]{1,0:T(8,128)(2,1)S(1)}, u32[]{:S(2)}, u32[]{:S(2)}) collective-permute-start(bf16[128,1536]{1,0:T(8,128)(2,1)S(1)} %constant_dynamic-update-slice_fusion.rest_0_), channel_id=1, source_target_pairs={{0,1},{1,0},{2,3},{3,2},{4,5},{5,4},{6,7},{7,6},{8,9},{9,8},{10,11... | collective-permute-start | bytes 1179656 | tf_op jit(solution)/shard_map/ppermute | solution.py:214
  33.0 7.8 %collective-permute-start.16 = (bf16[64,1536]{1,0:T(8,128)(2,1)S(1)}, bf16[64,1536]{1,0:T(8,128)(2,1)S(1)}, u32[]{:S(2)}, u32[]{:S(2)}) collective-permute-start(bf16[64,1536]{1,0:T(8,128)(2,1)S(1)} %collective-permute-done.15), channel_id=1, source_target_pairs={{0,4},{1,3},{2,6},{3,1},{4,0},{5,7},{6,2},{7,5},{8,12},{9,11},{10,... | collective-permute-start | bytes 589832 | tf_op jit(solution)/shard_map/ppermute | solution.py:214
  35.0 8.4 %collective-permute-start.12 = (bf16[128,1536]{1,0:T(8,128)(2,1)S(1)}, bf16[128,1536]{1,0:T(8,128)(2,1)S(1)}, u32[]{:S(2)}, u32[]{:S(2)}) collective-permute-start(bf16[128,1536]{1,0:T(8,128)(2,1)S(1)} %constant_dynamic-update-slice_fusion.2.rest_0_), channel_id=1, source_target_pairs={{0,2},{1,5},{2,0},{3,7},{4,6},{5,1},{6,4},{7,3},{8,10},{9,13},{10,... | collective-permute-start | bytes 1179656 | tf_op jit(solution)/shard_map/ppermute | solution.py:214
  40.8 2.4 %collective-permute-start.4 = (bf16[128,1536]{1,0:T(8,128)(2,1)S(1)}, bf16[128,1536]{1,0:T(8,128)(2,1)S(1)}, u32[]{:S(2)}, u32[]{:S(2)}) collective-permute-start(bf16[128,1536]{1,0:T(8,128)(2,1)S(1)} %collective-permute-done.3.rest_1_), channel_id=1, source_target_pairs={{0,1},{1,0},{2,3},{3,2},{4,5},{5,4},{6,7},{7,6},{8,9},{9,8},{10,11... | collective-permute-start | bytes 1179656 | tf_op jit(solution)/shard_map/ppermute | solution.py:214
  40.9 12.6 %collective-permute-start.17 = (bf16[128,1536]{1,0:T(8,128)(2,1)S(1)}, bf16[128,1536]{1,0:T(8,128)(2,1)S(1)}, u32[]{:S(2)}, u32[]{:S(2)}) collective-permute-start(bf16[128,1536]{1,0:T(8,128)(2,1)S(1)} %constant_dynamic-update-slice_fusion.4.rest_0_), channel_id=1, source_target_pairs={{0,2},{1,5},{2,0},{3,7},{4,6},{5,1},{6,4},{7,3},{8,10},{9,13},{10,... | collective-permute-start | bytes 1179656 | tf_op jit(solution)/shard_map/ppermute | solution.py:214
  42.4 11.4 %collective-permute-start.9 = (bf16[128,1536]{1,0:T(8,128)(2,1)S(1)}, bf16[128,1536]{1,0:T(8,128)(2,1)S(1)}, u32[]{:S(2)}, u32[]{:S(2)}) collective-permute-start(bf16[128,1536]{1,0:T(8,128)(2,1)S(1)} %collective-permute-done.7.rest_1_), channel_id=1, source_target_pairs={{0,1},{1,0},{2,3},{3,2},{4,5},{5,4},{6,7},{7,6},{8,9},{9,8},{10,11... | collective-permute-start | bytes 1179656 | tf_op jit(solution)/shard_map/ppermute | solution.py:214
  43.2 17.2 %collective-permute-start.13 = (bf16[128,1536]{1,0:T(8,128)(2,1)S(1)}, bf16[128,1536]{1,0:T(8,128)(2,1)S(1)}, u32[]{:S(2)}, u32[]{:S(2)}) collective-permute-start(bf16[128,1536]{1,0:T(8,128)(2,1)S(1)} %constant_dynamic-update-slice_fusion.2.rest_0_), channel_id=1, source_target_pairs={{0,1},{1,0},{2,3},{3,2},{4,5},{5,4},{6,7},{7,6},{8,9},{9,8},{10,11... | collective-permute-start | bytes 1179656 | tf_op jit(solution)/shard_map/ppermute | solution.py:214
  43.3 17.1 %collective-permute-start.14 = (bf16[128,1536]{1,0:T(8,128)(2,1)S(1)}, bf16[128,1536]{1,0:T(8,128)(2,1)S(1)}, u32[]{:S(2)}, u32[]{:S(2)}) collective-permute-start(bf16[128,1536]{1,0:T(8,128)(2,1)S(1)} %collective-permute-done.12.rest_1_), channel_id=1, source_target_pairs={{0,1},{1,0},{2,3},{3,2},{4,5},{5,4},{6,7},{7,6},{8,9},{9,8},{10,11... | collective-permute-start | bytes 1179656 | tf_op jit(solution)/shard_map/ppermute | solution.py:214
  43.8 2.3 %copy-start.5 = (bf16[1536,1536]{1,0:T(8,128)(2,1)S(1)}, bf16[1536,1536]{1,0:T(8,128)(2,1)}, u32[]{:S(2)}) copy-start(bf16[1536,1536]{1,0:T(8,128)(2,1)} %head.7) | copy-start | bytes 14155780
  52.7 0.6 copy-start
  53.3 14.3 %collective-permute-start.18 = (bf16[128,1536]{1,0:T(8,128)(2,1)S(1)}, bf16[128,1536]{1,0:T(8,128)(2,1)S(1)}, u32[]{:S(2)}, u32[]{:S(2)}) collective-permute-start(bf16[128,1536]{1,0:T(8,128)(2,1)S(1)} %constant_dynamic-update-slice_fusion.4.rest_0_), channel_id=1, source_target_pairs={{0,1},{1,0},{2,3},{3,2},{4,5},{5,4},{6,7},{7,6},{8,9},{9,8},{10,11... | collective-permute-start | bytes 1179656 | tf_op jit(solution)/shard_map/ppermute | solution.py:214
  53.4 14.2 %collective-permute-start.19 = (bf16[128,1536]{1,0:T(8,128)(2,1)S(1)}, bf16[128,1536]{1,0:T(8,128)(2,1)S(1)}, u32[]{:S(2)}, u32[]{:S(2)}) collective-permute-start(bf16[128,1536]{1,0:T(8,128)(2,1)S(1)} %collective-permute-done.17.rest_1_), channel_id=1, source_target_pairs={{0,1},{1,0},{2,3},{3,2},{4,5},{5,4},{6,7},{7,6},{8,9},{9,8},{10,11... | collective-permute-start | bytes 1179656 | tf_op jit(solution)/shard_map/ppermute | solution.py:214
  60.4 7.2 %copy-start.1 = (f32[2,8,128]{2,1,0:T(8,128)}, f32[2,8,128]{2,1,0:T(8,128)S(1)}, u32[]{:S(2)}) copy-start(f32[2,8,128]{2,1,0:T(8,128)S(1)} %shard_map.87.rest_1_) | copy-start | bytes 24580
  67.1 0.6 copy-start.2
  74.3 0.6 copy-start.3

commit v2 on v0

v2 whole, which is shorter than its diff:
```python
import functools

import jax
import jax.numpy as jnp
from jax import lax
from jax.experimental import pallas as pl
from jax.experimental.pallas import tpu as pltpu
from jax.sharding import PartitionSpec as P

epsilon = 1e-05
LANES = 128
SUB = 16
GROUP = 32
DIGIT = 256
AXES = ("tok", "voc")
VMEM_LIMIT = 24 * 1024 * 1024


def prepare_kernel(spot, *refs):
    sources, (block, quarter, half, table), held, arrivals = refs[:6], refs[6:10], refs[10:16], refs[16]
    fetches = [pltpu.make_async_copy(sources[i], held[i], arrivals.at[i]) for i in range(6)]
    for fetch in fetches:
        fetch.start()
    for fetch in fetches:
        fetch.wait()
    hidden, gain, targets, lengths, turns, prior_rows = held
    rows, feats = hidden.shape
    me, band = spot[0], spot[1]
    scale = gain[...].reshape(1, feats)
    table[0] = me
    table[1] = band
    for u in range(turns.shape[0]):
        table[2 + u] = turns[u]
        table[2 + turns.shape[0] + u] = lengths[u]

    own = targets[...].reshape(1, rows).astype(jnp.float32)
    own = jnp.concatenate([own[:, 1:], own[:, :1]], axis=1)
    high = jnp.floor(own * (1.0 / DIGIT))
    low = own - high * DIGIT
    lane = lax.broadcasted_iota(jnp.int32, (LANES, LANES), 1)
    first_high = jnp.broadcast_to(high[:, rows - 1 :], (LANES, LANES))
    first_low = jnp.broadcast_to(low[:, rows - 1 :], (LANES, LANES))
    for start in range(0, rows, LANES):
        at = slice(start, start + LANES)
        own_high = jnp.broadcast_to(high[:, at], (LANES, LANES)).T
        own_low = jnp.broadcast_to(low[:, at], (LANES, LANES)).T
        digits = jnp.where(
            lane < LANES // 2,
            jnp.where(lane < LANES // 4, own_high, own_low),
            jnp.where(lane < 3 * LANES // 4, first_high, first_low),
        )
        block[at, feats:] = digits.astype(jnp.bfloat16)

    def norm_rows(step, _):
        at = pl.ds(pl.multiple_of(step * SUB, SUB), SUB)
        value = hidden[at, :].astype(jnp.float32)
        mean = jnp.sum(value * value, axis=1, keepdims=True) * (1.0 / feats)
        block[at, 0:feats] = (value * lax.rsqrt(mean + epsilon) * scale).astype(jnp.bfloat16)
        return 0

    lax.fori_loop(0, rows // SUB, norm_rows, 0, unroll=4)
    asked = jnp.int32(0)
    for u in range(turns.shape[0]):
        asked = jnp.where(turns[u] == me, prior_rows[u], asked)
    end = lengths[me] - 1
    sub = lax.broadcasted_iota(jnp.int32, (SUB, 1), 0)
    values = block[pl.ds(pl.multiple_of(asked // SUB * SUB, SUB), SUB), 0:feats].astype(jnp.float32)
    value = jnp.sum(jnp.where(sub == asked % SUB, values, 0.0), axis=0, keepdims=True)
    at = pl.ds(pl.multiple_of(end // SUB * SUB, SUB), SUB)
    present = block[at, 0:feats].astype(jnp.float32)
    block[at, 0:feats] = jnp.where(sub == end % SUB, value, present).astype(jnp.bfloat16)
    quarter[...] = block[pl.ds(pl.multiple_of(band * quarter.shape[0], SUB), quarter.shape[0]), :]
    half[...] = block[pl.ds(pl.multiple_of(band % 2 * half.shape[0], SUB), half.shape[0]), :]


def prepare(spot, hidden, gain, targets, lengths, turns, prior_rows, voc_count):
    rows, feats = hidden.shape
    sources = (hidden, gain, targets, lengths, turns, prior_rows)
    sources = [pltpu.with_memory_space_constraint(a, pltpu.HBM) for a in sources]
    smem, vmem = pl.BlockSpec(memory_space=pltpu.SMEM), pl.BlockSpec(memory_space=pltpu.VMEM)
    shapes = [jax.ShapeDtypeStruct((n, feats + LANES), hidden.dtype) for n in (rows, rows // voc_count, rows // 2)]
    shapes.append(jax.ShapeDtypeStruct((2 + 2 * turns.shape[0],), jnp.int32))
    held = [pltpu.VMEM(a.shape, a.dtype) for a in sources[:3]] + [pltpu.SMEM(a.shape, a.dtype) for a in sources[3:]]
    return pl.pallas_call(
        prepare_kernel,
        out_shape=shapes,
        in_specs=[smem] + [pl.BlockSpec(memory_space=pltpu.HBM)] * 6,
        out_specs=[vmem] * 3 + [smem],
        scratch_shapes=held + [pltpu.SemaphoreType.DMA((6,))],
        compiler_params=pltpu.CompilerParams(vmem_limit_bytes=VMEM_LIMIT),
    )(spot, *sources)


def place_of(kind, core, band, rows, side, voc_count):
    name, d, e = kind
    if name == "own":
        return 0
    if name == "near":
        return d * rows + (core if e == 0 else 1 - core) * (rows // 2)
    if name == "other":
        core, band = 1 - core, band ^ 1
    y, x = jnp.where(core == 0, e, d), jnp.where(core == 0, d, e)
    return y * rows + (band ^ (2 * x)) * (rows // voc_count)


def score_kernel(
    layout, position, rows, width, nblocks, turn_count, voc_count, spans, collects, loads, table, head, *rest
):
    pieces, rest = rest[: len(layout)], rest[len(layout) :]
    earlier, rest = rest[: 2 * len(spans)], rest[2 * len(spans) :]
    out, rest = rest[0], rest[1:]
    if not collects:
        ends, rest = rest[0], rest[1:]
    if loads:
        stored, head, arrival, rest = head, rest[0], rest[1], rest[2:]
        fetch = pltpu.make_async_copy(stored, head, arrival)
        fetch.start()
    if collects:
        held, rest = rest[0], rest[1:]
    states, even, odd, lines, kept, edges = rest
    feats = head.shape[0]
    tiles = head.shape[1] // LANES
    halves = rows // LANES
    side = voc_count // 2
    turns, lengths = 2, 2 + turn_count
    me, band = table[0], table[1]
    core = band % 2
    base = (me * voc_count + band) * width

    offsets = []
    live = []
    offset = jnp.int32(0)
    for block in range(nblocks):
        length = table[lengths + (me ^ (position + block))]
        offsets.append(offset)
        live.append(length)
        offset = offset + (length + GROUP - 1) // GROUP * GROUP
    total_rows = offset + GROUP if collects else offset
    count = (total_rows + LANES - 1) // LANES

    for ref, parts in zip(pieces, layout):
        size = ref.shape[0] // len(parts)
        for index, (kind, start_block) in enumerate(parts):
            place = place_of(kind, core, band, rows, side, voc_count)
            block = start_block + place // rows
            row = place % rows
            to, length = offsets[0], live[0]
            for b in range(1, nblocks):
                to = jnp.where(block == b, offsets[b], to)
                length = jnp.where(block == b, live[b], length)
            for step in range(0, size, GROUP):

                @pl.when(row + step < length)
                def _(ref=ref, start=index * size + step, to=to + row + step):
                    states[pl.ds(pl.multiple_of(to, GROUP), GROUP), :] = ref[start : start + GROUP, :]

    sub = lax.broadcasted_iota(jnp.int32, (SUB, 1), 0)
    sub_group = lax.broadcasted_iota(jnp.int32, (GROUP, 1), 0)
    edge = jnp.zeros(edges.shape, jnp.float32)
    for ref in earlier[1::2]:
        edge = edge + ref[...].astype(jnp.float32)
    edges[...] = edge
    for block in range(nblocks):
        end = offsets[block] + live[block] - 1
        values = states[pl.ds(pl.multiple_of(end // SUB * SUB, SUB), SUB), 0:feats].astype(jnp.float32)
        line = position + block
        edges[line : line + 1, 0:feats] = jnp.sum(jnp.where(sub == end % SUB, values, 0.0), axis=0, keepdims=True)
        values = states[pl.ds(pl.multiple_of(offsets[block], SUB), SUB), feats:].astype(jnp.float32)
        edges[line : line + 1, feats:] = values[0:1, :]
    if collects:
        group = pl.ds(pl.multiple_of(offset, GROUP), GROUP)
        states[group, 0:feats] = edges[:, 0:feats].astype(jnp.bfloat16)
        digits = jnp.zeros((GROUP, LANES), jnp.float32)
        for line in range(turn_count):
            asked = me ^ table[turns + (me ^ line)]
            digits = digits + jnp.where(sub_group == asked, edges[line : line + 1, feats:], 0.0)
        states[group, feats:] = pltpu.roll(digits, LANES // 2, 1).astype(jnp.bfloat16)
    else:
        ends[...] = edges[...].astype(jnp.bfloat16)

    lanes = lax.broadcasted_iota(jnp.int32, (SUB, LANES), 1)
    lanes_f = lanes.astype(jnp.float32)
    base_f = base.astype(jnp.float32)

    def multiply(tile, into):
        at = pl.ds(pl.multiple_of(tile * LANES, LANES), LANES)
        into[...] = jnp.dot(states[at, 0:feats], head[...], preferred_element_type=jnp.float32)

    def reduce(tile, logits):
        for row in range(0, LANES, SUB):
            at = slice(row, row + SUB)

            def part(k, at=at):
                value = logits[at, k * LANES : (k + 1) * LANES]
                if (k + 1) * LANES > width:
                    value = jnp.where(lanes < width - k * LANES, value, -1e30)
                return value

            top = part(0)
            for k in range(1, tiles):
                top = jnp.maximum(top, part(k))
            here = pl.ds(pl.multiple_of(tile * LANES + row, SUB), SUB)
            digits = states[here, feats:].astype(jnp.float32)
            digits = jnp.where(lanes < LANES // 4, digits * DIGIT, jnp.where(lanes < LANES // 2, digits, 0.0))
            digits = digits + pltpu.roll(digits, LANES // 2, 1)
            offset = digits + pltpu.roll(digits, LANES // 4, 1) - base_f - lanes_f
            total = jnp.zeros((SUB, LANES), jnp.float32)
            moment = total
            picked = total
            for k in range(tiles):
                value = part(k)
                weight = jnp.exp(value - top)
                total = total + weight
                moment = moment + weight * value
                picked = picked + jnp.where(offset == float(k * LANES), value, 0.0)
            kept[0, at, :] = top
            kept[1, at, :] = total
            kept[2, at, :] = moment
            kept[3, at, :] = picked
        top = kept[0].T
        largest = jnp.max(top, axis=0, keepdims=True)
        factor = jnp.exp(top - largest)
        lines[tile, 0:1, :] = largest
        lines[tile, 1:2, :] = jnp.sum(kept[1].T * factor, axis=0, keepdims=True)
        lines[tile, 2:3, :] = jnp.sum(kept[2].T * factor, axis=0, keepdims=True)
        lines[tile, 3:4, :] = jnp.sum(kept[3].T, axis=0, keepdims=True)

    if loads:
        fetch.wait()
    multiply(0, even)

    def two_tiles(step, _):
        multiply(2 * step + 1, odd)
        reduce(2 * step, even)
        multiply(2 * step + 2, even)
        reduce(2 * step + 1, odd)
        return 0

    lax.fori_loop(0, (count - 1) // 2, two_tiles, 0)

    @pl.when(count % 2 == 0)
    def _():
        multiply(count - 1, odd)
        reduce(count - 2, even)
        reduce(count - 1, odd)

    @pl.when(count % 2 == 1)
    def _():
        reduce(count - 1, even)

    def line_of(block_offset, half):
        tile, turned = block_offset // LANES + half, block_offset % LANES
        back = (LANES - turned) % LANES
        here, next_one = pltpu.roll(lines[tile], back, 1), pltpu.roll(lines[tile + 1], back, 1)
        return jnp.where(lax.broadcasted_iota(jnp.int32, here.shape, 1) < LANES - turned, here, next_one)

    high = 4 * halves
    for block in range(nblocks):
        to = held.at[me ^ (position + block)] if collects else out.at[block]
        for half in range(halves):
            to[4 * half : 4 * half + 4, :] = line_of(offsets[block], half)[0:4, :]

    if collects:
        for start, ref in zip(spans, earlier[0::2]):
            for block in range(ref.shape[0]):
                held[me ^ (start + block)] = ref[block]
        line = lax.broadcasted_iota(jnp.int32, (high, LANES), 0)
        lane = lax.broadcasted_iota(jnp.int32, (high, LANES), 1)
        swap = (lane == LANES - 1) & (line >= high - 4)
        edge_lines = jnp.concatenate([lines[offset // LANES, 0:4, :]] * halves, axis=0)
        for turn in range(turn_count):
            at = offset % LANES + (me ^ table[turns + turn])
            prior = pltpu.roll(edge_lines, LANES - 1 - at, 1)
            value = jnp.where(swap, prior, held[turn])
            for copy in range(voc_count):
                out[turn * voc_count + copy] = value


def score(pieces, layout, table, position, head, rows, width, nblocks, turn_count, voc_count, earlier=(), spans=(), loads=False):
    collects = bool(spans) or nblocks == turn_count
    total_rows = nblocks * rows + LANES
    feats, columns = head.shape
    high = 4 * (rows // LANES)
    smem = pl.BlockSpec(memory_space=pltpu.SMEM)
    vmem = pl.BlockSpec(memory_space=pltpu.VMEM)
    where_head = vmem
    blocks = turn_count * voc_count if collects else nblocks
    result = [jax.ShapeDtypeStruct((blocks, high, LANES), jnp.float32)]
    scratch = []
    if not collects:
        result.append(jax.ShapeDtypeStruct((GROUP, feats + LANES), jnp.bfloat16))
    if loads:
        head = pltpu.with_memory_space_constraint(head, pltpu.HBM)
        where_head = pl.BlockSpec(memory_space=pltpu.HBM)
        result.append(pltpu.VMEM((feats, columns), head.dtype))
        scratch.append(pltpu.SemaphoreType.DMA)
    if collects:
        scratch.append(pltpu.VMEM((turn_count, high, LANES), jnp.float32))
    return pl.pallas_call(
        functools.partial(
            score_kernel, layout, position, rows, width, nblocks, turn_count, voc_count, spans, collects, loads
        ),
        out_shape=result,
        in_specs=[smem, where_head] + [vmem] * (len(pieces) + len(earlier)),
        out_specs=[vmem] * len(result),
        scratch_shapes=scratch
        + [
            pltpu.VMEM((total_rows, feats + LANES), jnp.bfloat16),
            pltpu.VMEM((LANES, columns), jnp.float32),
            pltpu.VMEM((LANES, columns), jnp.float32),
            pltpu.VMEM((total_rows // LANES + 1, 8, LANES), jnp.float32),
            pltpu.VMEM((4, LANES, LANES), jnp.float32),
            pltpu.VMEM((GROUP, feats + LANES), jnp.float32),
        ],
        compiler_params=pltpu.CompilerParams(vmem_limit_bytes=VMEM_LIMIT),
        cost_estimate=pl.CostEstimate(
            flops=2 * total_rows * feats * columns,
            bytes_accessed=2 * feats * (total_rows + columns),
            transcendentals=total_rows * columns,
        ),
    )(table, head, *pieces, *earlier)


def finish_kernel(spot, lengths, received, logprob, entropy):
    halves = received.shape[1] // 4

    def kind_of(kind):
        return jnp.concatenate([received[:, 4 * h + kind : 4 * h + kind + 1, :] for h in range(halves)], axis=1)

    top = kind_of(0)
    largest = jnp.max(top, axis=0)
    factor = jnp.exp(top - largest[None])
    total = jnp.sum(kind_of(1) * factor, axis=0)
    moment = jnp.sum(kind_of(2) * factor, axis=0)
    picked = jnp.sum(kind_of(3), axis=0)
    normalizer = largest + jnp.log(total)
    half = lax.broadcasted_iota(jnp.int32, largest.shape, 0)
    lane = lax.broadcasted_iota(jnp.int32, largest.shape, 1)
    live = half * LANES + lane < lengths[spot[0]]

    def by_scored_row(value):
        previous = jnp.concatenate([value[halves - 1 :], value[: halves - 1]], axis=0)
        rolled = jnp.concatenate([value[:, LANES - 1 :], value[:, : LANES - 1]], axis=1)
        rolled_previous = jnp.concatenate([previous[:, LANES - 1 :], previous[:, : LANES - 1]], axis=1)
        return jnp.where(live, jnp.where(lane == 0, rolled_previous, rolled), 0.0)

    logprob[...] = by_scored_row(picked - normalizer)
    entropy[...] = by_scored_row(normalizer - moment / total)


def finish(spot, lengths, received):
    smem = pl.BlockSpec(memory_space=pltpu.SMEM)
    vmem = pl.BlockSpec(memory_space=pltpu.VMEM)
    halves = received.shape[1] // 4
    shape = jax.ShapeDtypeStruct((halves, LANES), jnp.float32)
    return pl.pallas_call(
        finish_kernel, out_shape=(shape, shape), in_specs=[smem, smem, vmem], out_specs=(vmem, vmem)
    )(spot, lengths, received)


def after(value, *others):
    return lax.optimization_barrier((value,) + others)[0]


def body(hidden, norm_gain, head_weight, targets, lengths, prior_device, prior_row):
    rows, feats = hidden.shape
    width = head_weight.shape[1]
    tok_count, voc_count = lax.axis_size("tok"), lax.axis_size("voc")
    side = voc_count // 2
    depth = tok_count // side
    me, band = lax.axis_index("tok"), lax.axis_index("voc")
    core = band % 2
    quarter = rows // voc_count
    half = rows // 2

    def permute(value, move):
        pairs = []
        for t in range(tok_count):
            for v in range(voc_count):
                to_t, to_v = move(t, v)
                pairs.append((t * voc_count + v, to_t * voc_count + to_v))
        return lax.ppermute(value, AXES, pairs)

    def along_z(value, d):
        return permute(value, lambda t, v: (t ^ (d * side), v))

    def along_y(value, d):
        return permute(value, lambda t, v: (t ^ d, v))

    def across_cores(value):
        return permute(value, lambda t, v: (t, v ^ 1))

    def second_hop(value, d):
        return permute(value, lambda t, v: (t ^ d, v) if v % 2 == 0 else (t, v ^ (2 * d)))

    def third_hop(value, d):
        return permute(value, lambda t, v: (t, v ^ (2 * d)) if v % 2 == 0 else (t ^ d, v))

    spot = jnp.stack([me, band]).astype(jnp.int32)
    block, own_quarter, own_half, table = prepare(
        spot, hidden, norm_gain, targets, lengths, prior_device, prior_row, voc_count
    )
    near = [along_y(own_half, d) for d in range(1, side)]
    arrived = {1: along_z(own_quarter, 1)}
    for d in range(2, depth):
        high = 1 << (d.bit_length() - 1)
        arrived[d] = along_z(after(arrived[high], arrived[1]) if d > high else own_quarter, d % high or high)
    near_far = [across_cores(n) for n in near]

    head = head_weight
    if width % LANES:
        head = jnp.pad(head_weight, ((0, 0), (0, LANES - width % LANES)))

    pieces, layout = [block], [((("own", 0, 0), 0),)]
    for d in range(1, side):
        pieces += [near[d - 1], near_far[d - 1]]
        layout += [((("near", d, 0), 0),), ((("near", d, 1), 0),)]
    groups = [(pieces, layout)]
    sizes = (rows, width, 2 * side, tok_count, voc_count)
    second, third = {}, {}
    for d in range(1, depth):
        start = after(arrived[d], arrived[1]) if d > 1 else arrived[d]
        second[d] = [second_hop(start, e) for e in range(1, side)]
        gathered = jnp.concatenate([start] + second[d], axis=0)
        if d > 1:
            gathered = after(gathered, *third[1])
        third[d] = [third_hop(gathered, e) for e in range(1, side)]
        far = list(third[d])
        if d == depth - 1:
            joined = [sum(parts, []) for parts in zip(*groups[:2])]
            first_stats, first_ends, head = score(*joined, table, 0, head, *sizes, loads=True)
            far = [after(f, first_stats) for f in far]
        pieces = [gathered, across_cores(gathered)]
        for f in far:
            pieces += [f, across_cores(f)]
        first_block = (d * side) % (2 * side) if d > 1 else side
        layout = []
        for e in range(side):
            for name in ("same", "other"):
                layout.append(tuple(((name, e, i), first_block) for i in range(side)))
        groups.append((pieces, layout))

    joined = [sum(parts, []) for parts in zip(*groups[2:])]
    (sent,) = score(*joined, table, 2 * side, head, *sizes, earlier=(first_stats, first_ends), spans=(0,))
    received = lax.all_to_all(sent, AXES, 0, 0)
    logprob, entropy = finish(spot, lengths, received)
    return logprob.reshape(rows), entropy.reshape(rows)


def solution(mesh):
    in_specs = (P("tok", None), P(), P(None, ("tok", "voc")), P("tok"), P(), P(), P())
    out_specs = (P("tok"), P("tok"))
    return jax.shard_map(body, mesh=mesh, in_specs=in_specs, out_specs=out_specs, check_vma=False)
```

time: 777 us -> 70.9 us (0.09)
  waiting for transfers between devices: 637 us -> 21.7 us
  blocking collectives: 93.5 us -> 10.7 us
  Pallas kernels: 0 us -> 19.9 us
  matrix products: 19.5 us -> 0 us
  starting transfers between devices: 0.04 us -> 17.4 us
  between operations: 16.1 us -> 0.71 us
  other arithmetic: 11.2 us -> 0.14 us
    all_gather x1 -> x0, waiting for transfers between devices: 636 us -> none  [body(): lax.all_gather(head_weight, 'tok', axis=1, tiled=True)]
    all_gather x1 -> x0, blocking collectives: 80.7 us -> none  [body(): incoming = lax.all_gather(outgoing, 'tok', axis=0, tiled=True)]
    ppermute x0 -> x17, waiting for transfers between devices: none -> 21.7 us  [permute(): return lax.ppermute(value, AXES, pairs)]
    pallas_call x0 -> x4, Pallas kernels: none -> 19.9 us  [the longest x2 15.1 us: score(): pl.pallas_call(functools.partial(score_kernel, layout, position, rows, wi...]
    dot_general x1 -> x0, matrix products: 19.5 us -> none  [score_block(): logits = jnp.dot(state_rows, columns, preferred_element_type=jnp.float32)]
    ppermute x0 -> x17, starting transfers between devices: none -> 17.4 us  [permute(): return lax.ppermute(value, AXES, pairs)]
    all_to_all x0 -> x1, blocking collectives: none -> 10.7 us  [body(): received = lax.all_to_all(sent, AXES, 0, 0)]
    reduce_sum x5 -> x0, other arithmetic: 9.05 us -> none  [the longest x1 7.37 us: score_block(): moments = jnp.sum(weights * logits, axis=1)]
  transfers between devices with their start and end apart: 1 -> 17, of which waited for: 1 -> 7; matrix products, arithmetic and copies ran while one was open for 0% -> 0% of each run, Pallas kernels for 0% -> 11%
where the time goes in v2:
time: 70.9 us; the launch traced here: 70.6 us
  waiting for transfers between devices  21.7 us (31%)
  Pallas kernels  19.9 us (28%)
  starting transfers between devices  17.4 us (25%)
  blocking collectives  10.7 us (15%)
  between operations  0.71 us (1%)
    ppermute x17, waiting for transfers between devices, permute(): return lax.ppermute(value, AXES, pairs)  21.7 us
    ppermute x17, starting transfers between devices, permute(): return lax.ppermute(value, AXES, pairs)  17.4 us
    pallas_call x2, Pallas kernels, score(): pl.pallas_call(functools.partial(score_kernel, layout, position, rows, wi...  15.1 us
    all_to_all x1, blocking collectives, body(): received = lax.all_to_all(sent, AXES, 0, 0)  10.7 us
    pallas_call x1, Pallas kernels, prepare(): pl.pallas_call(prepare_kernel, out_shape=shapes, in_specs=[smem] + [pl.Bl...  3.12 us
    pallas_call x1, Pallas kernels, finish(): pl.pallas_call(finish_kernel, out_shape=(shape, shape), in_specs=[smem, s...  1.66 us
  transfers between devices with their start and end apart: 17, of which 7 were waited for; matrix products, arithmetic and copies ran while one was open for 0% of the time, Pallas kernels for 11%

profile of v2, /device:TPU:0, one launch (start us, length us, event | category | flops | bytes accessed | tf_op | source)
XLA Modules:
  0.0 70.6 jit_solution(4549846351880210019)
XLA Ops:
  0.6 0.1 pad_add_fusion.spot
  0.7 0.0 copy-start
  0.7 3.1 %shard_map.86 = (bf16[256,1664]{1,0:T(8,128)(2,1)S(1)}, bf16[64,1664]{1,0:T(8,128)(2,1)S(1)}, bf16[128,1664]{1,0:T(8,128)(2,1)S(1)}, s32[18]{0:T(128)S(1)}) custom-call(s32[2]{0:T(128)S(1)} %pad_add_fusion.spot, bf16[256,1536]{1,0:T(8,128)(2,1)} %refs_0_.1, f32[1536]{0:T(1024)} %refs_1_.1, s32[256]{0:T(256)} %refs_2_.1, s32[8]{0:T(128)} %lengths.1, ...), custom_call_target="tpu_custom_call" | custom-call | tf_op jit(solution)/shard_map/pallas_call | solution.py:84
  3.8 3.1 %collective-permute-start.2 = (bf16[64,1664]{1,0:T(8,128)(2,1)S(1)}, bf16[64,1664]{1,0:T(8,128)(2,1)S(1)}, u32[]{:S(2)}, u32[]{:S(2)}) collective-permute-start(bf16[64,1664]{1,0:T(8,128)(2,1)S(1)} %get-tuple-element.19), channel_id=1, source_target_pairs={{0,8},{1,9},{2,10},{3,11},{4,12},{5,13},{6,14},{7,15},{8,0},{9,1},... | collective-permute-start | bytes 638984 | tf_op jit(solution)/shard_map/ppermute | solution.py:382
  6.9 2.6 %collective-permute-start.7 = (bf16[64,1664]{1,0:T(8,128)(2,1)S(1)}, bf16[64,1664]{1,0:T(8,128)(2,1)S(1)}, u32[]{:S(2)}, u32[]{:S(2)}) collective-permute-start(bf16[64,1664]{1,0:T(8,128)(2,1)S(1)} %get-tuple-element.19), channel_id=1, source_target_pairs={{0,16},{1,17},{2,18},{3,19},{4,20},{5,21},{6,22},{7,23},{8,24},{9,... | collective-permute-start | bytes 638984 | tf_op jit(solution)/shard_map/ppermute | solution.py:382
  9.5 1.5 %collective-permute-start = (bf16[128,1664]{1,0:T(8,128)(2,1)S(1)}, bf16[128,1664]{1,0:T(8,128)(2,1)S(1)}, u32[]{:S(2)}, u32[]{:S(2)}) collective-permute-start(bf16[128,1664]{1,0:T(8,128)(2,1)S(1)} %get-tuple-element.18), channel_id=1, source_target_pairs={{0,4},{1,5},{2,6},{3,7},{4,0},{5,1},{6,2},{7,3},{8,12},{9,13},{10,... | collective-permute-start | bytes 1277960 | tf_op jit(solution)/shard_map/ppermute | solution.py:382
  11.0 5.6 %collective-permute-done.2 = bf16[64,1664]{1,0:T(8,128)(2,1)S(1)} collective-permute-done((bf16[64,1664]{1,0:T(8,128)(2,1)S(1)}, bf16[64,1664]{1,0:T(8,128)(2,1)S(1)}, u32[]{:S(2)}, u32[]{:S(2)}) %collective-permute-start.2) | collective-permute-done | bytes 213024 | tf_op jit(solution)/shard_map/ppermute | solution.py:382
  16.6 1.7 %collective-permute-start.3 = (bf16[64,1664]{1,0:T(8,128)(2,1)S(1)}, bf16[64,1664]{1,0:T(8,128)(2,1)S(1)}, u32[]{:S(2)}, u32[]{:S(2)}) collective-permute-start(bf16[64,1664]{1,0:T(8,128)(2,1)S(1)} %collective-permute-done.2), channel_id=1, source_target_pairs={{0,4},{1,3},{2,6},{3,1},{4,0},{5,7},{6,2},{7,5},{8,12},{9,11},{10,... | collective-permute-start | bytes 638984 | tf_op jit(solution)/shard_map/ppermute | solution.py:382
  18.3 4.5 %collective-permute-done.3 = bf16[64,1664]{1,0:T(8,128)(2,1)S(1)} collective-permute-done((bf16[64,1664]{1,0:T(8,128)(2,1)S(1)}, bf16[64,1664]{1,0:T(8,128)(2,1)S(1)}, u32[]{:S(2)}, u32[]{:S(2)}) %collective-permute-start.3) | collective-permute-done | bytes 213024 | tf_op jit(solution)/shard_map/ppermute | solution.py:382
  22.8 1.6 %collective-permute-start.5 = (bf16[128,1664]{1,0:T(8,128)(2,1)S(1)}, bf16[128,1664]{1,0:T(8,128)(2,1)S(1)}, u32[]{:S(2)}, u32[]{:S(2)}) collective-permute-start(bf16[128,1664]{1,0:T(8,128)(2,1)S(1)} %constant_dynamic-update-slice_fusion.rest_3_), channel_id=1, source_target_pairs={{0,2},{1,5},{2,0},{3,7},{4,6},{5,1},{6,4},{7,3},{8,10},{9,13},{10,... | collective-permute-start | bytes 1277960 | tf_op jit(solution)/shard_map/ppermute | solution.py:382
  24.4 0.0 collective-permute-done.7
  24.4 1.2 %collective-permute-start.12 = (bf16[64,1664]{1,0:T(8,128)(2,1)S(1)}, bf16[64,1664]{1,0:T(8,128)(2,1)S(1)}, u32[]{:S(2)}, u32[]{:S(2)}) collective-permute-start(bf16[64,1664]{1,0:T(8,128)(2,1)S(1)} %collective-permute-done.7), channel_id=1, source_target_pairs={{0,8},{1,9},{2,10},{3,11},{4,12},{5,13},{6,14},{7,15},{8,0},{9,1},... | collective-permute-start | bytes 638984 | tf_op jit(solution)/shard_map/ppermute | solution.py:382
  25.6 1.5 %collective-permute-start.8 = (bf16[64,1664]{1,0:T(8,128)(2,1)S(1)}, bf16[64,1664]{1,0:T(8,128)(2,1)S(1)}, u32[]{:S(2)}, u32[]{:S(2)}) collective-permute-start(bf16[64,1664]{1,0:T(8,128)(2,1)S(1)} %collective-permute-done.7), channel_id=1, source_target_pairs={{0,4},{1,3},{2,6},{3,1},{4,0},{5,7},{6,2},{7,5},{8,12},{9,11},{10,... | collective-permute-start | bytes 638984 | tf_op jit(solution)/shard_map/ppermute | solution.py:382
  27.1 0.0 collective-permute-start.4
  27.1 3.1 %collective-permute-done.12 = bf16[64,1664]{1,0:T(8,128)(2,1)S(1)} collective-permute-done((bf16[64,1664]{1,0:T(8,128)(2,1)S(1)}, bf16[64,1664]{1,0:T(8,128)(2,1)S(1)}, u32[]{:S(2)}, u32[]{:S(2)}) %collective-permute-start.12) | collective-permute-done | bytes 213024 | tf_op jit(solution)/shard_map/ppermute | solution.py:382
  30.2 1.5 %collective-permute-start.13 = (bf16[64,1664]{1,0:T(8,128)(2,1)S(1)}, bf16[64,1664]{1,0:T(8,128)(2,1)S(1)}, u32[]{:S(2)}, u32[]{:S(2)}) collective-permute-start(bf16[64,1664]{1,0:T(8,128)(2,1)S(1)} %collective-permute-done.12), channel_id=1, source_target_pairs={{0,4},{1,3},{2,6},{3,1},{4,0},{5,7},{6,2},{7,5},{8,12},{9,11},{10,... | collective-permute-start | bytes 638984 | tf_op jit(solution)/shard_map/ppermute | solution.py:382
  31.7 0.0 collective-permute-done.rest_1_
  31.8 0.0 collective-permute-start.1
  31.8 1.0 %collective-permute-done.5.rest_5_ = bf16[128,1664]{1,0:T(8,128)(2,1)S(1)} collective-permute-done((bf16[128,1664]{1,0:T(8,128)(2,1)S(1)}, bf16[128,1664]{1,0:T(8,128)(2,1)S(1)}, u32[]{:S(2)}, u32[]{:S(2)}) %collective-permute-start.5) | collective-permute-done | bytes 426016 | tf_op jit(solution)/shard_map/ppermute | solution.py:382
  32.7 0.0 collective-permute-start.6
  32.7 0.0 collective-permute-done.8
  32.8 3.3 %collective-permute-done.13 = bf16[64,1664]{1,0:T(8,128)(2,1)S(1)} collective-permute-done((bf16[64,1664]{1,0:T(8,128)(2,1)S(1)}, bf16[64,1664]{1,0:T(8,128)(2,1)S(1)}, u32[]{:S(2)}, u32[]{:S(2)}) %collective-permute-start.13) | collective-permute-done | bytes 213024 | tf_op jit(solution)/shard_map/ppermute | solution.py:382
  36.1 0.6 collective-permute-start.15
  36.7 0.0 collective-permute-start.14
  36.7 0.0 collective-permute-done.4.rest_4_
  36.7 1.5 %collective-permute-start.10 = (bf16[128,1664]{1,0:T(8,128)(2,1)S(1)}, bf16[128,1664]{1,0:T(8,128)(2,1)S(1)}, u32[]{:S(2)}, u32[]{:S(2)}) collective-permute-start(bf16[128,1664]{1,0:T(8,128)(2,1)S(1)} %pad_maximum_fusion.rest_0_), channel_id=1, source_target_pairs={{0,2},{1,5},{2,0},{3,7},{4,6},{5,1},{6,4},{7,3},{8,10},{9,13},{10,... | collective-permute-start | bytes 1277960 | tf_op jit(solution)/shard_map/ppermute | solution.py:382
  38.2 0.0 collective-permute-done.1.rest_2_
  38.2 0.3 collective-permute-start.9
  38.5 0.0 collective-permute-done.6.rest_6_
  38.5 7.5 %shard_map.87 = (f32[4,8,128]{2,1,0:T(8,128)S(1)}, bf16[32,1664]{1,0:T(8,128)(2,1)S(1)}, bf16[1536,1536]{1,0:T(8,128)(2,1)S(1)}) custom-call(s32[18]{0:T(128)S(1)} %get-tuple-element.16.table, bf16[1536,1536]{1,0:T(8,128)(2,1)} %head.1, bf16[256,1664]{1,0:T(8,128)(2,1)S(1)} %get-tuple-element.17.rest_0_, bf16[128,1664]{1,0:T(8,128)(2,1)S(1)} %collective-permute-done.rest_1_, ...), custom_call_target="tpu_custom_call" | custom-call | flops 5435817984 | bytes 8257536 | tf_op jit(solution)/shard_map/pallas_call | solution.py:299
  46.0 0.0 copy-done
  46.0 0.0 collective-permute-done.15.rest_6_
  46.0 0.3 collective-permute-start.16
  46.3 2.5 %collective-permute-done.10.rest_2_ = bf16[128,1664]{1,0:T(8,128)(2,1)S(1)} collective-permute-done((bf16[128,1664]{1,0:T(8,128)(2,1)S(1)}, bf16[128,1664]{1,0:T(8,128)(2,1)S(1)}, u32[]{:S(2)}, u32[]{:S(2)}) %collective-permute-start.10) | collective-permute-done | bytes 426016 | tf_op jit(solution)/shard_map/ppermute | solution.py:382
  48.9 0.0 collective-permute-start.11
  48.9 0.0 collective-permute-done.14.rest_5_
  48.9 0.0 collective-permute-done.9.rest_1_
  48.9 0.0 collective-permute-done.16.rest_7_
  48.9 1.7 %collective-permute-done.11.rest_3_ = bf16[128,1664]{1,0:T(8,128)(2,1)S(1)} collective-permute-done((bf16[128,1664]{1,0:T(8,128)(2,1)S(1)}, bf16[128,1664]{1,0:T(8,128)(2,1)S(1)}, u32[]{:S(2)}, u32[]{:S(2)}) %collective-permute-start.11) | collective-permute-done | bytes 426016 | tf_op jit(solution)/shard_map/ppermute | solution.py:382
  50.6 7.6 %shard_map.88 = f32[32,8,128]{2,1,0:T(8,128)S(1)} custom-call(s32[18]{0:T(128)S(1)} %get-tuple-element.16.table, bf16[1536,1536]{1,0:T(8,128)(2,1)S(1)} %get-tuple-element.20.head, bf16[128,1664]{1,0:T(8,128)(2,1)S(1)} %pad_maximum_fusion.rest_0_, bf16[128,1664]{1,0:T(8,128)(2,1)S(1)} %collective-permute-done.9.rest_1_, ...), custom_call_target="tpu_custom_call" | custom-call | flops 5435817984 | bytes 8257536 | tf_op jit(solution)/shard_map/pallas_call | solution.py:299
  58.2 10.7 %all_to_all.5.received = f32[32,8,128]{2,1,0:T(8,128)} all-to-all(f32[32,8,128]{2,1,0:T(8,128)S(1)} %shard_map.88), channel_id=1, replica_groups=mesh['tok'=8,'voc'=4] {'tok','voc'}, dimensions={0} | all-to-all | bytes 262144 | tf_op jit(solution)/shard_map/all_to_all | solution.py:445
  68.9 1.7 %shard_map.89 = (f32[2,128]{1,0:T(2,128)}, f32[2,128]{1,0:T(2,128)}) custom-call(s32[2]{0:T(128)} %copy-done, s32[8]{0:T(128)} %lengths.1, f32[32,8,128]{2,1,0:T(8,128)} %all_to_all.5.received), custom_call_target="tpu_custom_call" | custom-call | tf_op jit(solution)/shard_map/pallas_call | solution.py:356
  (4 shorter events, 0.1 us)
Async XLA Ops:
  0.7 45.3 %copy-start = (s32[2]{0:T(128)}, s32[2]{0:T(128)S(1)}, u32[]{:S(2)}) copy-start(s32[2]{0:T(128)S(1)} %pad_add_fusion.spot) | copy-start | bytes 28
  3.8 12.8 %collective-permute-start.2 = (bf16[64,1664]{1,0:T(8,128)(2,1)S(1)}, bf16[64,1664]{1,0:T(8,128)(2,1)S(1)}, u32[]{:S(2)}, u32[]{:S(2)}) collective-permute-start(bf16[64,1664]{1,0:T(8,128)(2,1)S(1)} %get-tuple-element.19), channel_id=1, source_target_pairs={{0,8},{1,9},{2,10},{3,11},{4,12},{5,13},{6,14},{7,15},{8,0},{9,1},... | collective-permute-start | bytes 638984 | tf_op jit(solution)/shard_map/ppermute | solution.py:382
  6.9 17.5 %collective-permute-start.7 = (bf16[64,1664]{1,0:T(8,128)(2,1)S(1)}, bf16[64,1664]{1,0:T(8,128)(2,1)S(1)}, u32[]{:S(2)}, u32[]{:S(2)}) collective-permute-start(bf16[64,1664]{1,0:T(8,128)(2,1)S(1)} %get-tuple-element.19), channel_id=1, source_target_pairs={{0,16},{1,17},{2,18},{3,19},{4,20},{5,21},{6,22},{7,23},{8,24},{9,... | collective-permute-start | bytes 638984 | tf_op jit(solution)/shard_map/ppermute | solution.py:382
  9.5 22.2 %collective-permute-start = (bf16[128,1664]{1,0:T(8,128)(2,1)S(1)}, bf16[128,1664]{1,0:T(8,128)(2,1)S(1)}, u32[]{:S(2)}, u32[]{:S(2)}) collective-permute-start(bf16[128,1664]{1,0:T(8,128)(2,1)S(1)} %get-tuple-element.18), channel_id=1, source_target_pairs={{0,4},{1,5},{2,6},{3,7},{4,0},{5,1},{6,2},{7,3},{8,12},{9,13},{10,... | collective-permute-start | bytes 1277960 | tf_op jit(solution)/shard_map/ppermute | solution.py:382
  16.6 6.2 %collective-permute-start.3 = (bf16[64,1664]{1,0:T(8,128)(2,1)S(1)}, bf16[64,1664]{1,0:T(8,128)(2,1)S(1)}, u32[]{:S(2)}, u32[]{:S(2)}) collective-permute-start(bf16[64,1664]{1,0:T(8,128)(2,1)S(1)} %collective-permute-done.2), channel_id=1, source_target_pairs={{0,4},{1,3},{2,6},{3,1},{4,0},{5,7},{6,2},{7,5},{8,12},{9,11},{10,... | collective-permute-start | bytes 638984 | tf_op jit(solution)/shard_map/ppermute | solution.py:382
  22.8 9.9 %collective-permute-start.5 = (bf16[128,1664]{1,0:T(8,128)(2,1)S(1)}, bf16[128,1664]{1,0:T(8,128)(2,1)S(1)}, u32[]{:S(2)}, u32[]{:S(2)}) collective-permute-start(bf16[128,1664]{1,0:T(8,128)(2,1)S(1)} %constant_dynamic-update-slice_fusion.rest_3_), channel_id=1, source_target_pairs={{0,2},{1,5},{2,0},{3,7},{4,6},{5,1},{6,4},{7,3},{8,10},{9,13},{10,... | collective-permute-start | bytes 1277960 | tf_op jit(solution)/shard_map/ppermute | solution.py:382
  24.4 5.8 %collective-permute-start.12 = (bf16[64,1664]{1,0:T(8,128)(2,1)S(1)}, bf16[64,1664]{1,0:T(8,128)(2,1)S(1)}, u32[]{:S(2)}, u32[]{:S(2)}) collective-permute-start(bf16[64,1664]{1,0:T(8,128)(2,1)S(1)} %collective-permute-done.7), channel_id=1, source_target_pairs={{0,8},{1,9},{2,10},{3,11},{4,12},{5,13},{6,14},{7,15},{8,0},{9,1},... | collective-permute-start | bytes 638984 | tf_op jit(solution)/shard_map/ppermute | solution.py:382
  25.6 7.1 %collective-permute-start.8 = (bf16[64,1664]{1,0:T(8,128)(2,1)S(1)}, bf16[64,1664]{1,0:T(8,128)(2,1)S(1)}, u32[]{:S(2)}, u32[]{:S(2)}) collective-permute-start(bf16[64,1664]{1,0:T(8,128)(2,1)S(1)} %collective-permute-done.7), channel_id=1, source_target_pairs={{0,4},{1,3},{2,6},{3,1},{4,0},{5,7},{6,2},{7,5},{8,12},{9,11},{10,... | collective-permute-start | bytes 638984 | tf_op jit(solution)/shard_map/ppermute | solution.py:382
  27.1 9.6 %collective-permute-start.4 = (bf16[128,1664]{1,0:T(8,128)(2,1)S(1)}, bf16[128,1664]{1,0:T(8,128)(2,1)S(1)}, u32[]{:S(2)}, u32[]{:S(2)}) collective-permute-start(bf16[128,1664]{1,0:T(8,128)(2,1)S(1)} %constant_dynamic-update-slice_fusion.rest_3_), channel_id=1, source_target_pairs={{0,1},{1,0},{2,3},{3,2},{4,5},{5,4},{6,7},{7,6},{8,9},{9,8},{10,11... | collective-permute-start | bytes 1277960 | tf_op jit(solution)/shard_map/ppermute | solution.py:382
  30.2 5.8 %collective-permute-start.13 = (bf16[64,1664]{1,0:T(8,128)(2,1)S(1)}, bf16[64,1664]{1,0:T(8,128)(2,1)S(1)}, u32[]{:S(2)}, u32[]{:S(2)}) collective-permute-start(bf16[64,1664]{1,0:T(8,128)(2,1)S(1)} %collective-permute-done.12), channel_id=1, source_target_pairs={{0,4},{1,3},{2,6},{3,1},{4,0},{5,7},{6,2},{7,5},{8,12},{9,11},{10,... | collective-permute-start | bytes 638984 | tf_op jit(solution)/shard_map/ppermute | solution.py:382
  31.8 6.5 %collective-permute-start.1 = (bf16[128,1664]{1,0:T(8,128)(2,1)S(1)}, bf16[128,1664]{1,0:T(8,128)(2,1)S(1)}, u32[]{:S(2)}, u32[]{:S(2)}) collective-permute-start(bf16[128,1664]{1,0:T(8,128)(2,1)S(1)} %collective-permute-done.rest_1_), channel_id=1, source_target_pairs={{0,1},{1,0},{2,3},{3,2},{4,5},{5,4},{6,7},{7,6},{8,9},{9,8},{10,11... | collective-permute-start | bytes 1277960 | tf_op jit(solution)/shard_map/ppermute | solution.py:382
  32.7 5.7 %collective-permute-start.6 = (bf16[128,1664]{1,0:T(8,128)(2,1)S(1)}, bf16[128,1664]{1,0:T(8,128)(2,1)S(1)}, u32[]{:S(2)}, u32[]{:S(2)}) collective-permute-start(bf16[128,1664]{1,0:T(8,128)(2,1)S(1)} %collective-permute-done.5.rest_5_), channel_id=1, source_target_pairs={{0,1},{1,0},{2,3},{3,2},{4,5},{5,4},{6,7},{7,6},{8,9},{9,8},{10,11... | collective-permute-start | bytes 1277960 | tf_op jit(solution)/shard_map/ppermute | solution.py:382
  36.1 9.9 %collective-permute-start.15 = (bf16[128,1664]{1,0:T(8,128)(2,1)S(1)}, bf16[128,1664]{1,0:T(8,128)(2,1)S(1)}, u32[]{:S(2)}, u32[]{:S(2)}) collective-permute-start(bf16[128,1664]{1,0:T(8,128)(2,1)S(1)} %pad_maximum_fusion.1.rest_4_), channel_id=1, source_target_pairs={{0,2},{1,5},{2,0},{3,7},{4,6},{5,1},{6,4},{7,3},{8,10},{9,13},{10,... | collective-permute-start | bytes 1277960 | tf_op jit(solution)/shard_map/ppermute | solution.py:382
  36.7 12.2 %collective-permute-start.14 = (bf16[128,1664]{1,0:T(8,128)(2,1)S(1)}, bf16[128,1664]{1,0:T(8,128)(2,1)S(1)}, u32[]{:S(2)}, u32[]{:S(2)}) collective-permute-start(bf16[128,1664]{1,0:T(8,128)(2,1)S(1)} %pad_maximum_fusion.1.rest_4_), channel_id=1, source_target_pairs={{0,1},{1,0},{2,3},{3,2},{4,5},{5,4},{6,7},{7,6},{8,9},{9,8},{10,11... | collective-permute-start | bytes 1277960 | tf_op jit(solution)/shard_map/ppermute | solution.py:382
  36.7 12.2 %collective-permute-start.10 = (bf16[128,1664]{1,0:T(8,128)(2,1)S(1)}, bf16[128,1664]{1,0:T(8,128)(2,1)S(1)}, u32[]{:S(2)}, u32[]{:S(2)}) collective-permute-start(bf16[128,1664]{1,0:T(8,128)(2,1)S(1)} %pad_maximum_fusion.rest_0_), channel_id=1, source_target_pairs={{0,2},{1,5},{2,0},{3,7},{4,6},{5,1},{6,4},{7,3},{8,10},{9,13},{10,... | collective-permute-start | bytes 1277960 | tf_op jit(solution)/shard_map/ppermute | solution.py:382
  38.2 10.7 %collective-permute-start.9 = (bf16[128,1664]{1,0:T(8,128)(2,1)S(1)}, bf16[128,1664]{1,0:T(8,128)(2,1)S(1)}, u32[]{:S(2)}, u32[]{:S(2)}) collective-permute-start(bf16[128,1664]{1,0:T(8,128)(2,1)S(1)} %pad_maximum_fusion.rest_0_), channel_id=1, source_target_pairs={{0,1},{1,0},{2,3},{3,2},{4,5},{5,4},{6,7},{7,6},{8,9},{9,8},{10,11... | collective-permute-start | bytes 1277960 | tf_op jit(solution)/shard_map/ppermute | solution.py:382
  46.0 2.9 %collective-permute-start.16 = (bf16[128,1664]{1,0:T(8,128)(2,1)S(1)}, bf16[128,1664]{1,0:T(8,128)(2,1)S(1)}, u32[]{:S(2)}, u32[]{:S(2)}) collective-permute-start(bf16[128,1664]{1,0:T(8,128)(2,1)S(1)} %collective-permute-done.15.rest_6_), channel_id=1, source_target_pairs={{0,1},{1,0},{2,3},{3,2},{4,5},{5,4},{6,7},{7,6},{8,9},{9,8},{10,11... | collective-permute-start | bytes 1277960 | tf_op jit(solution)/shard_map/ppermute | solution.py:382
  48.9 1.8 %collective-permute-start.11 = (bf16[128,1664]{1,0:T(8,128)(2,1)S(1)}, bf16[128,1664]{1,0:T(8,128)(2,1)S(1)}, u32[]{:S(2)}, u32[]{:S(2)}) collective-permute-start(bf16[128,1664]{1,0:T(8,128)(2,1)S(1)} %collective-permute-done.10.rest_2_), channel_id=1, source_target_pairs={{0,1},{1,0},{2,3},{3,2},{4,5},{5,4},{6,7},{7,6},{8,9},{9,8},{10,11... | collective-permute-start | bytes 1277960 | tf_op jit(solution)/shard_map/ppermute | solution.py:382

commit v3 on v2

--- a/solution.py
+++ b/solution.py
@@ -92,81 +92,83 @@
 
 
 def place_of(kind, core, band, rows, side, voc_count):
-    name, d, e = kind
+    name, d, e, index = kind
+    quarter = rows // voc_count
     if name == "own":
-        return 0
+        return index * quarter
     if name == "near":
-        return d * rows + (core if e == 0 else 1 - core) * (rows // 2)
+        return d * rows + (core if e == 0 else 1 - core) * (rows // 2) + index * quarter
     if name == "other":
         core, band = 1 - core, band ^ 1
-    y, x = jnp.where(core == 0, e, d), jnp.where(core == 0, d, e)
-    return y * rows + (band ^ (2 * x)) * (rows // voc_count)
-
-
-def score_kernel(
-    layout, position, rows, width, nblocks, turn_count, voc_count, spans, collects, loads, table, head, *rest
-):
+    y, x = jnp.where(core == 0, index, d), jnp.where(core == 0, d, index)
+    return y * rows + (band ^ (2 * x)) * quarter
+
+
+def score_kernel(layout, rows, width, turn_count, voc_count, collects, loads, table, head, *rest):
     pieces, rest = rest[: len(layout)], rest[len(layout) :]
-    earlier, rest = rest[: 2 * len(spans)], rest[2 * len(spans) :]
-    out, rest = rest[0], rest[1:]
-    if not collects:
-        ends, rest = rest[0], rest[1:]
+    if collects:
+        earlier, earlier_ends, rest = rest[0], rest[1], rest[2:]
+        out, rest = rest[0], rest[1:]
+    else:
+        out, ends, rest = rest[0], rest[1], rest[2:]
     if loads:
         stored, head, arrival, rest = head, rest[0], rest[1], rest[2:]
         fetch = pltpu.make_async_copy(stored, head, arrival)
         fetch.start()
-    if collects:
-        held, rest = rest[0], rest[1:]
+    found = out
+    if collects:
+        found, rest = rest[0], rest[1:]
     states, even, odd, lines, kept, edges = rest
     feats = head.shape[0]
     tiles = head.shape[1] // LANES
     halves = rows // LANES
     side = voc_count // 2
+    size = rows // voc_count
     turns, lengths = 2, 2 + turn_count
     me, band = table[0], table[1]
     core = band % 2
     base = (me * voc_count + band) * width
 
-    offsets = []
-    live = []
     offset = jnp.int32(0)
-    for block in range(nblocks):
-        length = table[lengths + (me ^ (position + block))]
-        offsets.append(offset)
-        live.append(length)
-        offset = offset + (length + GROUP - 1) // GROUP * GROUP
+    moved = []
+    present = set()
+    for ref, parts in zip(pieces, layout):
+        for index, (kind, start_block) in enumerate(parts):
+            present.update(range(start_block, start_block + side))
+            place = jnp.asarray(place_of(kind, core, band, rows, side, voc_count), jnp.int32)
+            block = start_block + place // rows
+            row = place % rows
+            live = jnp.clip(table[lengths + (me ^ block)] - row, 0, size)
+            for step in range(0, size, GROUP):
+
+                @pl.when(step < live)
+                def _(ref=ref, start=index * size + step, to=offset + step):
+                    states[pl.ds(pl.multiple_of(to, GROUP), GROUP), :] = ref[start : start + GROUP, :]
+
+            moved.append((start_block, block, row, offset))
+            offset = offset + (live + GROUP - 1) // GROUP * GROUP
     total_rows = offset + GROUP if collects else offset
     count = (total_rows + LANES - 1) // LANES
 
-    for ref, parts in zip(pieces, layout):
-        size = ref.shape[0] // len(parts)
-        for index, (kind, start_block) in enumerate(parts):
-            place = place_of(kind, core, band, rows, side, voc_count)
-            block = start_block + place // rows
-            row = place % rows
-            to, length = offsets[0], live[0]
-            for b in range(1, nblocks):
-                to = jnp.where(block == b, offsets[b], to)
-                length = jnp.where(block == b, live[b], length)
-            for step in range(0, size, GROUP):
-
-                @pl.when(row + step < length)
-                def _(ref=ref, start=index * size + step, to=to + row + step):
-                    states[pl.ds(pl.multiple_of(to, GROUP), GROUP), :] = ref[start : start + GROUP, :]
-
     sub = lax.broadcasted_iota(jnp.int32, (SUB, 1), 0)
     sub_group = lax.broadcasted_iota(jnp.int32, (GROUP, 1), 0)
-    edge = jnp.zeros(edges.shape, jnp.float32)
-    for ref in earlier[1::2]:
-        edge = edge + ref[...].astype(jnp.float32)
-    edges[...] = edge
-    for block in range(nblocks):
-        end = offsets[block] + live[block] - 1
-        values = states[pl.ds(pl.multiple_of(end // SUB * SUB, SUB), SUB), 0:feats].astype(jnp.float32)
-        line = position + block
-        edges[line : line + 1, 0:feats] = jnp.sum(jnp.where(sub == end % SUB, values, 0.0), axis=0, keepdims=True)
-        values = states[pl.ds(pl.multiple_of(offsets[block], SUB), SUB), feats:].astype(jnp.float32)
-        edges[line : line + 1, feats:] = values[0:1, :]
+    edges[...] = earlier_ends[...].astype(jnp.float32) if collects else jnp.zeros(edges.shape, jnp.float32)
+    for line in sorted(present):
+        end = table[lengths + (me ^ line)] - 1
+        end_row = end // size * size
+        at_end, at_first = jnp.int32(-1), jnp.int32(-1)
+        for start_block, block, row, to in moved:
+            if start_block <= line < start_block + side:
+                at_end = jnp.where((block == line) & (row == end_row), to + end % size, at_end)
+                at_first = jnp.where((block == line) & (row == 0), to, at_first)
+
+        def row_at(at, columns):
+            group = pl.ds(pl.multiple_of(jnp.maximum(at, 0) // SUB * SUB, SUB), SUB)
+            values = states[group, columns].astype(jnp.float32)
+            return jnp.sum(jnp.where((sub == at % SUB) & (at >= 0), values, 0.0), axis=0, keepdims=True)
+
+        for at, columns in ((at_end, slice(0, feats)), (at_first, slice(feats, feats + LANES))):
+            edges[line : line + 1, columns] = edges[line : line + 1, columns] + row_at(at, columns)
     if collects:
         group = pl.ds(pl.multiple_of(offset, GROUP), GROUP)
         states[group, 0:feats] = edges[:, 0:feats].astype(jnp.bfloat16)
@@ -248,22 +250,19 @@
     def _():
         reduce(count - 1, even)
 
-    def line_of(block_offset, half):
-        tile, turned = block_offset // LANES + half, block_offset % LANES
+    lane = lax.broadcasted_iota(jnp.int32, (8, LANES), 1)
+    if collects:
+        found[...] = earlier[...]
+    for _, block, row, to in moved:
+        tile, turned, shift = to // LANES, to % LANES, row % LANES
         back = (LANES - turned) % LANES
-        here, next_one = pltpu.roll(lines[tile], back, 1), pltpu.roll(lines[tile + 1], back, 1)
-        return jnp.where(lax.broadcasted_iota(jnp.int32, here.shape, 1) < LANES - turned, here, next_one)
-
-    high = 4 * halves
-    for block in range(nblocks):
-        to = held.at[me ^ (position + block)] if collects else out.at[block]
-        for half in range(halves):
-            to[4 * half : 4 * half + 4, :] = line_of(offsets[block], half)[0:4, :]
-
-    if collects:
-        for start, ref in zip(spans, earlier[0::2]):
-            for block in range(ref.shape[0]):
-                held[me ^ (start + block)] = ref[block]
+        here, following = pltpu.roll(lines[tile], back, 1), pltpu.roll(lines[tile + 1], back, 1)
+        value = pltpu.roll(jnp.where(lane < LANES - turned, here, following), shift, 1)
+        inside = (lane >= shift) & (lane < shift + size)
+        found[block, row // LANES] = jnp.where(inside, value, found[block, row // LANES])
+
+    if collects:
+        high = 4 * halves
         line = lax.broadcasted_iota(jnp.int32, (high, LANES), 0)
         lane = lax.broadcasted_iota(jnp.int32, (high, LANES), 1)
         swap = (lane == LANES - 1) & (line >= high - 4)
@@ -271,23 +270,26 @@
         for turn in range(turn_count):
             at = offset % LANES + (me ^ table[turns + turn])
             prior = pltpu.roll(edge_lines, LANES - 1 - at, 1)
-            value = jnp.where(swap, prior, held[turn])
+            own = jnp.concatenate([found[me ^ turn, half][0:4, :] for half in range(halves)], axis=0)
+            value = jnp.where(swap, prior, own)
             for copy in range(voc_count):
                 out[turn * voc_count + copy] = value
 
 
-def score(pieces, layout, table, position, head, rows, width, nblocks, turn_count, voc_count, earlier=(), spans=(), loads=False):
-    collects = bool(spans) or nblocks == turn_count
-    total_rows = nblocks * rows + LANES
+def score(pieces, layout, table, head, rows, width, turn_count, voc_count, earlier=(), loads=False):
+    collects = bool(earlier)
+    raw_rows = sum(piece.shape[0] for piece in pieces)
     feats, columns = head.shape
-    high = 4 * (rows // LANES)
+    halves = rows // LANES
     smem = pl.BlockSpec(memory_space=pltpu.SMEM)
     vmem = pl.BlockSpec(memory_space=pltpu.VMEM)
     where_head = vmem
-    blocks = turn_count * voc_count if collects else nblocks
-    result = [jax.ShapeDtypeStruct((blocks, high, LANES), jnp.float32)]
+    by_block = (turn_count, halves, 8, LANES)
     scratch = []
-    if not collects:
+    if collects:
+        result = [jax.ShapeDtypeStruct((turn_count * voc_count, 4 * halves, LANES), jnp.float32)]
+    else:
+        result = [jax.ShapeDtypeStruct(by_block, jnp.float32)]
         result.append(jax.ShapeDtypeStruct((GROUP, feats + LANES), jnp.bfloat16))
     if loads:
         head = pltpu.with_memory_space_constraint(head, pltpu.HBM)
@@ -295,28 +297,26 @@
         result.append(pltpu.VMEM((feats, columns), head.dtype))
         scratch.append(pltpu.SemaphoreType.DMA)
     if collects:
-        scratch.append(pltpu.VMEM((turn_count, high, LANES), jnp.float32))
+        scratch.append(pltpu.VMEM(by_block, jnp.float32))
     return pl.pallas_call(
-        functools.partial(
-            score_kernel, layout, position, rows, width, nblocks, turn_count, voc_count, spans, collects, loads
-        ),
+        functools.partial(score_kernel, layout, rows, width, turn_count, voc_count, collects, loads),
         out_shape=result,
         in_specs=[smem, where_head] + [vmem] * (len(pieces) + len(earlier)),
         out_specs=[vmem] * len(result),
         scratch_shapes=scratch
         + [
-            pltpu.VMEM((total_rows, feats + LANES), jnp.bfloat16),
+            pltpu.VMEM((raw_rows + LANES, feats + LANES), jnp.bfloat16),
             pltpu.VMEM((LANES, columns), jnp.float32),
             pltpu.VMEM((LANES, columns), jnp.float32),
-            pltpu.VMEM((total_rows // LANES + 1, 8, LANES), jnp.float32),
+            pltpu.VMEM((raw_rows // LANES + 2, 8, LANES), jnp.float32),
             pltpu.VMEM((4, LANES, LANES), jnp.float32),
             pltpu.VMEM((GROUP, feats + LANES), jnp.float32),
         ],
         compiler_params=pltpu.CompilerParams(vmem_limit_bytes=VMEM_LIMIT),
         cost_estimate=pl.CostEstimate(
-            flops=2 * total_rows * feats * columns,
-            bytes_accessed=2 * feats * (total_rows + columns),
-            transcendentals=total_rows * columns,
+            flops=2 * raw_rows * feats * columns,
+            bytes_accessed=2 * feats * (raw_rows + columns),
+            transcendentals=raw_rows * columns,
         ),
     )(table, head, *pieces, *earlier)
 
@@ -402,46 +402,48 @@
     )
     near = [along_y(own_half, d) for d in range(1, side)]
     arrived = {1: along_z(own_quarter, 1)}
+    second = {1: [second_hop(arrived[1], e) for e in range(1, side)]}
     for d in range(2, depth):
         high = 1 << (d.bit_length() - 1)
-        arrived[d] = along_z(after(arrived[high], arrived[1]) if d > high else own_quarter, d % high or high)
+        arrived[d] = along_z(after(arrived[high], arrived[1], *near) if d > high else own_quarter, d % high or high)
     near_far = [across_cores(n) for n in near]
 
     head = head_weight
     if width % LANES:
         head = jnp.pad(head_weight, ((0, 0), (0, LANES - width % LANES)))
 
-    pieces, layout = [block], [((("own", 0, 0), 0),)]
+    pieces, layout = [block], [tuple((("own", 0, 0, i), 0) for i in range(voc_count))]
     for d in range(1, side):
         pieces += [near[d - 1], near_far[d - 1]]
-        layout += [((("near", d, 0), 0),), ((("near", d, 1), 0),)]
-    groups = [(pieces, layout)]
-    sizes = (rows, width, 2 * side, tok_count, voc_count)
-    second, third = {}, {}
+        layout += [tuple((("near", d, e, i), 0) for i in range(voc_count // 2)) for e in range(2)]
+    sizes = (rows, width, tok_count, voc_count)
+    third, late, late_layout = {}, [], []
     for d in range(1, depth):
-        start = after(arrived[d], arrived[1]) if d > 1 else arrived[d]
-        second[d] = [second_hop(start, e) for e in range(1, side)]
+        start = arrived[d]
+        if d > 1:
+            start = after(start, arrived[1], *near)
+            second[d] = [second_hop(start, e) for e in range(1, side)]
         gathered = jnp.concatenate([start] + second[d], axis=0)
         if d > 1:
             gathered = after(gathered, *third[1])
         third[d] = [third_hop(gathered, e) for e in range(1, side)]
+        pieces += [gathered, across_cores(gathered)]
+        layouts = [[tuple(((n, e, 0, i), d * side) for i in range(side)) for n in ("same", "other")] for e in range(side)]
+        layout += layouts[0]
         far = list(third[d])
         if d == depth - 1:
-            joined = [sum(parts, []) for parts in zip(*groups[:2])]
-            first_stats, first_ends, head = score(*joined, table, 0, head, *sizes, loads=True)
+            first_stats, first_ends, head = score(pieces, layout, table, head, *sizes, loads=True)
             far = [after(f, first_stats) for f in far]
-        pieces = [gathered, across_cores(gathered)]
-        for f in far:
-            pieces += [f, across_cores(f)]
-        first_block = (d * side) % (2 * side) if d > 1 else side
-        layout = []
-        for e in range(side):
-            for name in ("same", "other"):
-                layout.append(tuple(((name, e, i), first_block) for i in range(side)))
-        groups.append((pieces, layout))
-
-    joined = [sum(parts, []) for parts in zip(*groups[2:])]
-    (sent,) = score(*joined, table, 2 * side, head, *sizes, earlier=(first_stats, first_ends), spans=(0,))
+        for e in range(1, side):
+            sent_on = [far[e - 1], across_cores(far[e - 1])]
+            if d == 1:
+                pieces += sent_on
+                layout += layouts[e]
+            else:
+                late += sent_on
+                late_layout += layouts[e]
+
+    (sent,) = score(late, late_layout, table, head, *sizes, earlier=(first_stats, first_ends))
     received = lax.all_to_all(sent, AXES, 0, 0)
     logprob, entropy = finish(spot, lengths, received)
     return logprob.reshape(rows), entropy.reshape(rows)

time: 70.9 us -> 68.4 us (0.965)
  waiting for transfers between devices: 21.7 us -> 17.4 us
  blocking collectives: 10.7 us -> 13.6 us
  starting transfers between devices: 17.4 us -> 16.5 us
    ppermute x17, waiting for transfers between devices: 21.7 us -> 17.4 us  [permute(): return lax.ppermute(value, AXES, pairs)]
    all_to_all x1, blocking collectives: 10.7 us -> 13.6 us  [body(): received = lax.all_to_all(sent, AXES, 0, 0)]
    ppermute x17, starting transfers between devices: 17.4 us -> 16.5 us  [permute(): return lax.ppermute(value, AXES, pairs)]
  transfers between devices with their start and end apart: 17 -> 17, of which waited for: 7 -> 10; matrix products, arithmetic and copies ran while one was open for 0% -> 0% of each run, Pallas kernels for 11% -> 18%
where the time goes in v3:
time: 68.4 us; the launch traced here: 68.3 us
  Pallas kernels  19.9 us (29%)
  waiting for transfers between devices  17.4 us (25%)
  starting transfers between devices  16.5 us (24%)
  blocking collectives  13.6 us (20%)
  between operations  0.7 us (1%)
    ppermute x17, waiting for transfers between devices, permute(): return lax.ppermute(value, AXES, pairs)  17.4 us
    ppermute x17, starting transfers between devices, permute(): return lax.ppermute(value, AXES, pairs)  16.5 us
    pallas_call x2, Pallas kernels, score(): pl.pallas_call(functools.partial(score_kernel, layout, rows, width, turn_...  15.1 us
    all_to_all x1, blocking collectives, body(): received = lax.all_to_all(sent, AXES, 0, 0)  13.6 us
    pallas_call x1, Pallas kernels, prepare(): pl.pallas_call(prepare_kernel, out_shape=shapes, in_specs=[smem] + [pl.Bl...  3.12 us
    pallas_call x1, Pallas kernels, finish(): pl.pallas_call(finish_kernel, out_shape=(shape, shape), in_specs=[smem, s...  1.66 us
  transfers between devices with their start and end apart: 17, of which 10 were waited for; matrix products, arithmetic and copies ran while one was open for 0% of the time, Pallas kernels for 18%

profile of v3, /device:TPU:0, one launch (start us, length us, event | category | flops | bytes accessed | tf_op | source)
XLA Modules:
  0.0 68.3 jit_solution(13919929193777813688)
XLA Ops:
  0.6 0.1 pad_add_fusion.spot
  0.7 0.0 copy-start
  0.7 3.1 %shard_map.86 = (bf16[256,1664]{1,0:T(8,128)(2,1)S(1)}, bf16[64,1664]{1,0:T(8,128)(2,1)S(1)}, bf16[128,1664]{1,0:T(8,128)(2,1)S(1)}, s32[18]{0:T(128)S(1)}) custom-call(s32[2]{0:T(128)S(1)} %pad_add_fusion.spot, bf16[256,1536]{1,0:T(8,128)(2,1)} %refs_0_.1, f32[1536]{0:T(1024)} %refs_1_.1, s32[256]{0:T(256)} %refs_2_.1, s32[8]{0:T(128)} %lengths.1, ...), custom_call_target="tpu_custom_call" | custom-call | tf_op jit(solution)/shard_map/pallas_call | solution.py:84
  3.8 3.1 %collective-permute-start.2 = (bf16[64,1664]{1,0:T(8,128)(2,1)S(1)}, bf16[64,1664]{1,0:T(8,128)(2,1)S(1)}, u32[]{:S(2)}, u32[]{:S(2)}) collective-permute-start(bf16[64,1664]{1,0:T(8,128)(2,1)S(1)} %get-tuple-element.19), channel_id=1, source_target_pairs={{0,8},{1,9},{2,10},{3,11},{4,12},{5,13},{6,14},{7,15},{8,0},{9,1},... | collective-permute-start | bytes 638984 | tf_op jit(solution)/shard_map/ppermute | solution.py:382
  6.9 1.5 %collective-permute-start = (bf16[128,1664]{1,0:T(8,128)(2,1)S(1)}, bf16[128,1664]{1,0:T(8,128)(2,1)S(1)}, u32[]{:S(2)}, u32[]{:S(2)}) collective-permute-start(bf16[128,1664]{1,0:T(8,128)(2,1)S(1)} %get-tuple-element.18), channel_id=1, source_target_pairs={{0,4},{1,5},{2,6},{3,7},{4,0},{5,1},{6,2},{7,3},{8,12},{9,13},{10,... | collective-permute-start | bytes 1277960 | tf_op jit(solution)/shard_map/ppermute | solution.py:382
  8.5 2.6 %collective-permute-start.7 = (bf16[64,1664]{1,0:T(8,128)(2,1)S(1)}, bf16[64,1664]{1,0:T(8,128)(2,1)S(1)}, u32[]{:S(2)}, u32[]{:S(2)}) collective-permute-start(bf16[64,1664]{1,0:T(8,128)(2,1)S(1)} %get-tuple-element.19), channel_id=1, source_target_pairs={{0,16},{1,17},{2,18},{3,19},{4,20},{5,21},{6,22},{7,23},{8,24},{9,... | collective-permute-start | bytes 638984 | tf_op jit(solution)/shard_map/ppermute | solution.py:382
  11.0 4.0 %collective-permute-done.2 = bf16[64,1664]{1,0:T(8,128)(2,1)S(1)} collective-permute-done((bf16[64,1664]{1,0:T(8,128)(2,1)S(1)}, bf16[64,1664]{1,0:T(8,128)(2,1)S(1)}, u32[]{:S(2)}, u32[]{:S(2)}) %collective-permute-start.2) | collective-permute-done | bytes 213024 | tf_op jit(solution)/shard_map/ppermute | solution.py:382
  15.1 3.0 %collective-permute-start.3 = (bf16[64,1664]{1,0:T(8,128)(2,1)S(1)}, bf16[64,1664]{1,0:T(8,128)(2,1)S(1)}, u32[]{:S(2)}, u32[]{:S(2)}) collective-permute-start(bf16[64,1664]{1,0:T(8,128)(2,1)S(1)} %collective-permute-done.2), channel_id=1, source_target_pairs={{0,4},{1,3},{2,6},{3,1},{4,0},{5,7},{6,2},{7,5},{8,12},{9,11},{10,... | collective-permute-start | bytes 638984 | tf_op jit(solution)/shard_map/ppermute | solution.py:382
  18.1 2.4 %collective-permute-done.7 = bf16[64,1664]{1,0:T(8,128)(2,1)S(1)} collective-permute-done((bf16[64,1664]{1,0:T(8,128)(2,1)S(1)}, bf16[64,1664]{1,0:T(8,128)(2,1)S(1)}, u32[]{:S(2)}, u32[]{:S(2)}) %collective-permute-start.7) | collective-permute-done | bytes 213024 | tf_op jit(solution)/shard_map/ppermute | solution.py:382
  20.5 0.0 collective-permute-done.rest_1_
  20.5 0.0 collective-permute-start.10
  20.5 0.6 collective-permute-start.8
  21.1 0.8 %collective-permute-done.3 = bf16[64,1664]{1,0:T(8,128)(2,1)S(1)} collective-permute-done((bf16[64,1664]{1,0:T(8,128)(2,1)S(1)}, bf16[64,1664]{1,0:T(8,128)(2,1)S(1)}, u32[]{:S(2)}, u32[]{:S(2)}) %collective-permute-start.3) | collective-permute-done | bytes 213024 | tf_op jit(solution)/shard_map/ppermute | solution.py:382
  21.9 1.6 %collective-permute-start.5 = (bf16[128,1664]{1,0:T(8,128)(2,1)S(1)}, bf16[128,1664]{1,0:T(8,128)(2,1)S(1)}, u32[]{:S(2)}, u32[]{:S(2)}) collective-permute-start(bf16[128,1664]{1,0:T(8,128)(2,1)S(1)} %constant_dynamic-update-slice_fusion.rest_3_), channel_id=1, source_target_pairs={{0,2},{1,5},{2,0},{3,7},{4,6},{5,1},{6,4},{7,3},{8,10},{9,13},{10,... | collective-permute-start | bytes 1277960 | tf_op jit(solution)/shard_map/ppermute | solution.py:382
  23.5 0.0 collective-permute-start.4
  23.5 0.5 collective-permute-start.1
  24.0 2.3 %collective-permute-done.10 = bf16[64,1664]{1,0:T(8,128)(2,1)S(1)} collective-permute-done((bf16[64,1664]{1,0:T(8,128)(2,1)S(1)}, bf16[64,1664]{1,0:T(8,128)(2,1)S(1)}, u32[]{:S(2)}, u32[]{:S(2)}) %collective-permute-start.10) | collective-permute-done | bytes 213024 | tf_op jit(solution)/shard_map/ppermute | solution.py:382
  26.3 0.4 collective-permute-start.11
  26.7 1.9 %collective-permute-done.8 = bf16[64,1664]{1,0:T(8,128)(2,1)S(1)} collective-permute-done((bf16[64,1664]{1,0:T(8,128)(2,1)S(1)}, bf16[64,1664]{1,0:T(8,128)(2,1)S(1)}, u32[]{:S(2)}, u32[]{:S(2)}) %collective-permute-start.8) | collective-permute-done | bytes 213024 | tf_op jit(solution)/shard_map/ppermute | solution.py:382
  28.7 3.5 %collective-permute-done.11 = bf16[64,1664]{1,0:T(8,128)(2,1)S(1)} collective-permute-done((bf16[64,1664]{1,0:T(8,128)(2,1)S(1)}, bf16[64,1664]{1,0:T(8,128)(2,1)S(1)}, u32[]{:S(2)}, u32[]{:S(2)}) %collective-permute-start.11) | collective-permute-done | bytes 213024 | tf_op jit(solution)/shard_map/ppermute | solution.py:382
  32.2 0.2 collective-permute-done.5.rest_5_
  32.4 0.0 collective-permute-start.12
  32.4 0.5 collective-permute-start.9
  32.9 0.0 collective-permute-start.6
  32.9 0.0 collective-permute-done.4.rest_4_
  32.9 1.5 %collective-permute-start.15 = (bf16[128,1664]{1,0:T(8,128)(2,1)S(1)}, bf16[128,1664]{1,0:T(8,128)(2,1)S(1)}, u32[]{:S(2)}, u32[]{:S(2)}) collective-permute-start(bf16[128,1664]{1,0:T(8,128)(2,1)S(1)} %pad_maximum_fusion.1.rest_9_), channel_id=1, source_target_pairs={{0,2},{1,5},{2,0},{3,7},{4,6},{5,1},{6,4},{7,3},{8,10},{9,13},{10,... | collective-permute-start | bytes 1277960 | tf_op jit(solution)/shard_map/ppermute | solution.py:382
  34.4 0.0 collective-permute-done.1.rest_2_
  34.4 0.5 collective-permute-start.13
  35.0 0.0 collective-permute-done.12.rest_10_
  35.0 0.0 collective-permute-done.9.rest_8_
  35.0 0.4 collective-permute-done.6.rest_6_
  35.4 12.0 %shard_map.87 = (f32[8,2,8,128]{3,2,1,0:T(8,128)S(1)}, bf16[32,1664]{1,0:T(8,128)(2,1)S(1)}, bf16[1536,1536]{1,0:T(8,128)(2,1)S(1)}) custom-call(s32[18]{0:T(128)S(1)} %get-tuple-element.16.table, bf16[1536,1536]{1,0:T(8,128)(2,1)} %head.1, bf16[256,1664]{1,0:T(8,128)(2,1)S(1)} %get-tuple-element.17.rest_0_, ...), custom_call_target="tpu_custom_call" | custom-call | flops 7247757312 | bytes 9437184 | tf_op jit(solution)/shard_map/pallas_call | solution.py:301
  47.4 0.0 copy-done
  47.4 0.0 collective-permute-done.15.rest_2_
  47.5 0.2 collective-permute-start.16
  47.7 0.0 collective-permute-done.13.rest_0_
  47.7 0.4 collective-permute-start.14
  48.0 1.3 %collective-permute-done.16.rest_3_ = bf16[128,1664]{1,0:T(8,128)(2,1)S(1)} collective-permute-done((bf16[128,1664]{1,0:T(8,128)(2,1)S(1)}, bf16[128,1664]{1,0:T(8,128)(2,1)S(1)}, u32[]{:S(2)}, u32[]{:S(2)}) %collective-permute-start.16) | collective-permute-done | bytes 426016 | tf_op jit(solution)/shard_map/ppermute | solution.py:382
  49.3 0.6 collective-permute-done.14.rest_1_
  49.9 3.1 %shard_map.88 = f32[32,8,128]{2,1,0:T(8,128)S(1)} custom-call(s32[18]{0:T(128)S(1)} %get-tuple-element.16.table, bf16[1536,1536]{1,0:T(8,128)(2,1)S(1)} %get-tuple-element.24.head, bf16[128,1664]{1,0:T(8,128)(2,1)S(1)} %collective-permute-done.13.rest_0_, bf16[128,1664]{1,0:T(8,128)(2,1)S(1)} %collective-permute-done.14.rest_1_, ...), custom_call_target="tpu_custom_call" | custom-call | flops 2415919104 | bytes 6291456 | tf_op jit(solution)/shard_map/pallas_call | solution.py:301
  53.0 13.6 %all_to_all.5.received = f32[32,8,128]{2,1,0:T(8,128)} all-to-all(f32[32,8,128]{2,1,0:T(8,128)S(1)} %shard_map.88), channel_id=1, replica_groups=mesh['tok'=8,'voc'=4] {'tok','voc'}, dimensions={0} | all-to-all | bytes 262144 | tf_op jit(solution)/shard_map/all_to_all | solution.py:447
  66.6 1.7 %shard_map.89 = (f32[2,128]{1,0:T(2,128)}, f32[2,128]{1,0:T(2,128)}) custom-call(s32[2]{0:T(128)} %copy-done, s32[8]{0:T(128)} %lengths.1, f32[32,8,128]{2,1,0:T(8,128)} %all_to_all.5.received), custom_call_target="tpu_custom_call" | custom-call | tf_op jit(solution)/shard_map/pallas_call | solution.py:356
  (4 shorter events, 0.1 us)
Async XLA Ops:
  0.7 46.7 %copy-start = (s32[2]{0:T(128)}, s32[2]{0:T(128)S(1)}, u32[]{:S(2)}) copy-start(s32[2]{0:T(128)S(1)} %pad_add_fusion.spot) | copy-start | bytes 28
  3.8 11.2 %collective-permute-start.2 = (bf16[64,1664]{1,0:T(8,128)(2,1)S(1)}, bf16[64,1664]{1,0:T(8,128)(2,1)S(1)}, u32[]{:S(2)}, u32[]{:S(2)}) collective-permute-start(bf16[64,1664]{1,0:T(8,128)(2,1)S(1)} %get-tuple-element.19), channel_id=1, source_target_pairs={{0,8},{1,9},{2,10},{3,11},{4,12},{5,13},{6,14},{7,15},{8,0},{9,1},... | collective-permute-start | bytes 638984 | tf_op jit(solution)/shard_map/ppermute | solution.py:382
  6.9 13.5 %collective-permute-start = (bf16[128,1664]{1,0:T(8,128)(2,1)S(1)}, bf16[128,1664]{1,0:T(8,128)(2,1)S(1)}, u32[]{:S(2)}, u32[]{:S(2)}) collective-permute-start(bf16[128,1664]{1,0:T(8,128)(2,1)S(1)} %get-tuple-element.18), channel_id=1, source_target_pairs={{0,4},{1,5},{2,6},{3,7},{4,0},{5,1},{6,2},{7,3},{8,12},{9,13},{10,... | collective-permute-start | bytes 1277960 | tf_op jit(solution)/shard_map/ppermute | solution.py:382
  8.5 12.0 %collective-permute-start.7 = (bf16[64,1664]{1,0:T(8,128)(2,1)S(1)}, bf16[64,1664]{1,0:T(8,128)(2,1)S(1)}, u32[]{:S(2)}, u32[]{:S(2)}) collective-permute-start(bf16[64,1664]{1,0:T(8,128)(2,1)S(1)} %get-tuple-element.19), channel_id=1, source_target_pairs={{0,16},{1,17},{2,18},{3,19},{4,20},{5,21},{6,22},{7,23},{8,24},{9,... | collective-permute-start | bytes 638984 | tf_op jit(solution)/shard_map/ppermute | solution.py:382
  15.1 6.9 %collective-permute-start.3 = (bf16[64,1664]{1,0:T(8,128)(2,1)S(1)}, bf16[64,1664]{1,0:T(8,128)(2,1)S(1)}, u32[]{:S(2)}, u32[]{:S(2)}) collective-permute-start(bf16[64,1664]{1,0:T(8,128)(2,1)S(1)} %collective-permute-done.2), channel_id=1, source_target_pairs={{0,4},{1,3},{2,6},{3,1},{4,0},{5,7},{6,2},{7,5},{8,12},{9,11},{10,... | collective-permute-start | bytes 638984 | tf_op jit(solution)/shard_map/ppermute | solution.py:382
  20.5 5.8 %collective-permute-start.10 = (bf16[64,1664]{1,0:T(8,128)(2,1)S(1)}, bf16[64,1664]{1,0:T(8,128)(2,1)S(1)}, u32[]{:S(2)}, u32[]{:S(2)}) collective-permute-start(bf16[64,1664]{1,0:T(8,128)(2,1)S(1)} %collective-permute-done.7), channel_id=1, source_target_pairs={{0,8},{1,9},{2,10},{3,11},{4,12},{5,13},{6,14},{7,15},{8,0},{9,1},... | collective-permute-start | bytes 638984 | tf_op jit(solution)/shard_map/ppermute | solution.py:382
  20.5 8.2 %collective-permute-start.8 = (bf16[64,1664]{1,0:T(8,128)(2,1)S(1)}, bf16[64,1664]{1,0:T(8,128)(2,1)S(1)}, u32[]{:S(2)}, u32[]{:S(2)}) collective-permute-start(bf16[64,1664]{1,0:T(8,128)(2,1)S(1)} %collective-permute-done.7), channel_id=1, source_target_pairs={{0,4},{1,3},{2,6},{3,1},{4,0},{5,7},{6,2},{7,5},{8,12},{9,11},{10,... | collective-permute-start | bytes 638984 | tf_op jit(solution)/shard_map/ppermute | solution.py:382
  21.9 10.5 %collective-permute-start.5 = (bf16[128,1664]{1,0:T(8,128)(2,1)S(1)}, bf16[128,1664]{1,0:T(8,128)(2,1)S(1)}, u32[]{:S(2)}, u32[]{:S(2)}) collective-permute-start(bf16[128,1664]{1,0:T(8,128)(2,1)S(1)} %constant_dynamic-update-slice_fusion.rest_3_), channel_id=1, source_target_pairs={{0,2},{1,5},{2,0},{3,7},{4,6},{5,1},{6,4},{7,3},{8,10},{9,13},{10,... | collective-permute-start | bytes 1277960 | tf_op jit(solution)/shard_map/ppermute | solution.py:382
  23.5 9.4 %collective-permute-start.4 = (bf16[128,1664]{1,0:T(8,128)(2,1)S(1)}, bf16[128,1664]{1,0:T(8,128)(2,1)S(1)}, u32[]{:S(2)}, u32[]{:S(2)}) collective-permute-start(bf16[128,1664]{1,0:T(8,128)(2,1)S(1)} %constant_dynamic-update-slice_fusion.rest_3_), channel_id=1, source_target_pairs={{0,1},{1,0},{2,3},{3,2},{4,5},{5,4},{6,7},{7,6},{8,9},{9,8},{10,11... | collective-permute-start | bytes 1277960 | tf_op jit(solution)/shard_map/ppermute | solution.py:382
  23.5 10.9 %collective-permute-start.1 = (bf16[128,1664]{1,0:T(8,128)(2,1)S(1)}, bf16[128,1664]{1,0:T(8,128)(2,1)S(1)}, u32[]{:S(2)}, u32[]{:S(2)}) collective-permute-start(bf16[128,1664]{1,0:T(8,128)(2,1)S(1)} %collective-permute-done.rest_1_), channel_id=1, source_target_pairs={{0,1},{1,0},{2,3},{3,2},{4,5},{5,4},{6,7},{7,6},{8,9},{9,8},{10,11... | collective-permute-start | bytes 1277960 | tf_op jit(solution)/shard_map/ppermute | solution.py:382
  26.3 5.8 %collective-permute-start.11 = (bf16[64,1664]{1,0:T(8,128)(2,1)S(1)}, bf16[64,1664]{1,0:T(8,128)(2,1)S(1)}, u32[]{:S(2)}, u32[]{:S(2)}) collective-permute-start(bf16[64,1664]{1,0:T(8,128)(2,1)S(1)} %collective-permute-done.10), channel_id=1, source_target_pairs={{0,4},{1,3},{2,6},{3,1},{4,0},{5,7},{6,2},{7,5},{8,12},{9,11},{10,... | collective-permute-start | bytes 638984 | tf_op jit(solution)/shard_map/ppermute | solution.py:382
  32.4 2.6 %collective-permute-start.12 = (bf16[128,1664]{1,0:T(8,128)(2,1)S(1)}, bf16[128,1664]{1,0:T(8,128)(2,1)S(1)}, u32[]{:S(2)}, u32[]{:S(2)}) collective-permute-start(bf16[128,1664]{1,0:T(8,128)(2,1)S(1)} %pad_maximum_fusion.1.rest_9_), channel_id=1, source_target_pairs={{0,1},{1,0},{2,3},{3,2},{4,5},{5,4},{6,7},{7,6},{8,9},{9,8},{10,11... | collective-permute-start | bytes 1277960 | tf_op jit(solution)/shard_map/ppermute | solution.py:382
  32.4 2.6 %collective-permute-start.9 = (bf16[128,1664]{1,0:T(8,128)(2,1)S(1)}, bf16[128,1664]{1,0:T(8,128)(2,1)S(1)}, u32[]{:S(2)}, u32[]{:S(2)}) collective-permute-start(bf16[128,1664]{1,0:T(8,128)(2,1)S(1)} %pad_maximum_fusion.rest_7_), channel_id=1, source_target_pairs={{0,1},{1,0},{2,3},{3,2},{4,5},{5,4},{6,7},{7,6},{8,9},{9,8},{10,11... | collective-permute-start | bytes 1277960 | tf_op jit(solution)/shard_map/ppermute | solution.py:382
  32.9 2.5 %collective-permute-start.6 = (bf16[128,1664]{1,0:T(8,128)(2,1)S(1)}, bf16[128,1664]{1,0:T(8,128)(2,1)S(1)}, u32[]{:S(2)}, u32[]{:S(2)}) collective-permute-start(bf16[128,1664]{1,0:T(8,128)(2,1)S(1)} %collective-permute-done.5.rest_5_), channel_id=1, source_target_pairs={{0,1},{1,0},{2,3},{3,2},{4,5},{5,4},{6,7},{7,6},{8,9},{9,8},{10,11... | collective-permute-start | bytes 1277960 | tf_op jit(solution)/shard_map/ppermute | solution.py:382
  32.9 14.5 %collective-permute-start.15 = (bf16[128,1664]{1,0:T(8,128)(2,1)S(1)}, bf16[128,1664]{1,0:T(8,128)(2,1)S(1)}, u32[]{:S(2)}, u32[]{:S(2)}) collective-permute-start(bf16[128,1664]{1,0:T(8,128)(2,1)S(1)} %pad_maximum_fusion.1.rest_9_), channel_id=1, source_target_pairs={{0,2},{1,5},{2,0},{3,7},{4,6},{5,1},{6,4},{7,3},{8,10},{9,13},{10,... | collective-permute-start | bytes 1277960 | tf_op jit(solution)/shard_map/ppermute | solution.py:382
  34.4 13.2 %collective-permute-start.13 = (bf16[128,1664]{1,0:T(8,128)(2,1)S(1)}, bf16[128,1664]{1,0:T(8,128)(2,1)S(1)}, u32[]{:S(2)}, u32[]{:S(2)}) collective-permute-start(bf16[128,1664]{1,0:T(8,128)(2,1)S(1)} %pad_maximum_fusion.rest_7_), channel_id=1, source_target_pairs={{0,2},{1,5},{2,0},{3,7},{4,6},{5,1},{6,4},{7,3},{8,10},{9,13},{10,... | collective-permute-start | bytes 1277960 | tf_op jit(solution)/shard_map/ppermute | solution.py:382
  47.5 1.8 %collective-permute-start.16 = (bf16[128,1664]{1,0:T(8,128)(2,1)S(1)}, bf16[128,1664]{1,0:T(8,128)(2,1)S(1)}, u32[]{:S(2)}, u32[]{:S(2)}) collective-permute-start(bf16[128,1664]{1,0:T(8,128)(2,1)S(1)} %collective-permute-done.15.rest_2_), channel_id=1, source_target_pairs={{0,1},{1,0},{2,3},{3,2},{4,5},{5,4},{6,7},{7,6},{8,9},{9,8},{10,11... | collective-permute-start | bytes 1277960 | tf_op jit(solution)/shard_map/ppermute | solution.py:382
  47.7 2.2 %collective-permute-start.14 = (bf16[128,1664]{1,0:T(8,128)(2,1)S(1)}, bf16[128,1664]{1,0:T(8,128)(2,1)S(1)}, u32[]{:S(2)}, u32[]{:S(2)}) collective-permute-start(bf16[128,1664]{1,0:T(8,128)(2,1)S(1)} %collective-permute-done.13.rest_0_), channel_id=1, source_target_pairs={{0,1},{1,0},{2,3},{3,2},{4,5},{5,4},{6,7},{7,6},{8,9},{9,8},{10,11... | collective-permute-start | bytes 1277960 | tf_op jit(solution)/shard_map/ppermute | solution.py:382

commit v4 on v3

--- a/solution.py
+++ b/solution.py
@@ -21,12 +21,11 @@
     fetches = [pltpu.make_async_copy(sources[i], held[i], arrivals.at[i]) for i in range(6)]
     for fetch in fetches:
         fetch.start()
-    for fetch in fetches:
+    for fetch in fetches[2:]:
         fetch.wait()
     hidden, gain, targets, lengths, turns, prior_rows = held
     rows, feats = hidden.shape
     me, band = spot[0], spot[1]
-    scale = gain[...].reshape(1, feats)
     table[0] = me
     table[1] = band
     for u in range(turns.shape[0]):
@@ -51,6 +50,10 @@
         )
         block[at, feats:] = digits.astype(jnp.bfloat16)
 
+    for fetch in fetches[:2]:
+        fetch.wait()
+    scale = gain[...].reshape(1, feats)
+
     def norm_rows(step, _):
         at = pl.ds(pl.multiple_of(step * SUB, SUB), SUB)
         value = hidden[at, :].astype(jnp.float32)
@@ -91,6 +94,24 @@
     )(spot, *sources)
 
 
+def load_kernel(stored, head, arrival):
+    fetch = pltpu.make_async_copy(stored, head, arrival)
+    fetch.start()
+    fetch.wait()
+
+
+def load(head):
+    return pl.pallas_call(
+        load_kernel,
+        out_shape=pltpu.VMEM(head.shape, head.dtype),
+        in_specs=[pl.BlockSpec(memory_space=pltpu.HBM)],
+        out_specs=pl.BlockSpec(memory_space=pltpu.VMEM),
+        scratch_shapes=[pltpu.SemaphoreType.DMA],
+        compiler_params=pltpu.CompilerParams(vmem_limit_bytes=VMEM_LIMIT),
+        cost_estimate=pl.CostEstimate(flops=0, bytes_accessed=2 * head.size * head.dtype.itemsize, transcendentals=0),
+    )(pltpu.with_memory_space_constraint(head, pltpu.HBM))
+
+
 def place_of(kind, core, band, rows, side, voc_count):
     name, d, e, index = kind
     quarter = rows // voc_count
@@ -104,17 +125,13 @@
     return y * rows + (band ^ (2 * x)) * quarter
 
 
-def score_kernel(layout, rows, width, turn_count, voc_count, collects, loads, table, head, *rest):
+def score_kernel(layout, rows, width, turn_count, voc_count, collects, table, head, *rest):
     pieces, rest = rest[: len(layout)], rest[len(layout) :]
     if collects:
         earlier, earlier_ends, rest = rest[0], rest[1], rest[2:]
         out, rest = rest[0], rest[1:]
     else:
         out, ends, rest = rest[0], rest[1], rest[2:]
-    if loads:
-        stored, head, arrival, rest = head, rest[0], rest[1], rest[2:]
-        fetch = pltpu.make_async_copy(stored, head, arrival)
-        fetch.start()
     found = out
     if collects:
         found, rest = rest[0], rest[1:]
@@ -227,8 +244,6 @@
         lines[tile, 2:3, :] = jnp.sum(kept[2].T * factor, axis=0, keepdims=True)
         lines[tile, 3:4, :] = jnp.sum(kept[3].T, axis=0, keepdims=True)
 
-    if loads:
-        fetch.wait()
     multiply(0, even)
 
     def two_tiles(step, _):
@@ -276,14 +291,13 @@
                 out[turn * voc_count + copy] = value
 
 
-def score(pieces, layout, table, head, rows, width, turn_count, voc_count, earlier=(), loads=False):
+def score(pieces, layout, table, head, rows, width, turn_count, voc_count, earlier=()):
     collects = bool(earlier)
     raw_rows = sum(piece.shape[0] for piece in pieces)
     feats, columns = head.shape
     halves = rows // LANES
     smem = pl.BlockSpec(memory_space=pltpu.SMEM)
     vmem = pl.BlockSpec(memory_space=pltpu.VMEM)
-    where_head = vmem
     by_block = (turn_count, halves, 8, LANES)
     scratch = []
     if collects:
@@ -291,17 +305,12 @@
     else:
         result = [jax.ShapeDtypeStruct(by_block, jnp.float32)]
         result.append(jax.ShapeDtypeStruct((GROUP, feats + LANES), jnp.bfloat16))
-    if loads:
-        head = pltpu.with_memory_space_constraint(head, pltpu.HBM)
-        where_head = pl.BlockSpec(memory_space=pltpu.HBM)
-        result.append(pltpu.VMEM((feats, columns), head.dtype))
-        scratch.append(pltpu.SemaphoreType.DMA)
     if collects:
         scratch.append(pltpu.VMEM(by_block, jnp.float32))
     return pl.pallas_call(
-        functools.partial(score_kernel, layout, rows, width, turn_count, voc_count, collects, loads),
+        functools.partial(score_kernel, layout, rows, width, turn_count, voc_count, collects),
         out_shape=result,
-        in_specs=[smem, where_head] + [vmem] * (len(pieces) + len(earlier)),
+        in_specs=[smem] + [vmem] * (1 + len(pieces) + len(earlier)),
         out_specs=[vmem] * len(result),
         scratch_shapes=scratch
         + [
@@ -402,15 +411,16 @@
     )
     near = [along_y(own_half, d) for d in range(1, side)]
     arrived = {1: along_z(own_quarter, 1)}
-    second = {1: [second_hop(arrived[1], e) for e in range(1, side)]}
+    head = head_weight
+    if width % LANES:
+        head = jnp.pad(head_weight, ((0, 0), (0, LANES - width % LANES)))
+    head = load(head)
+    second = {1: [second_hop(after(arrived[1], head), e) for e in range(1, side)]}
     for d in range(2, depth):
         high = 1 << (d.bit_length() - 1)
         arrived[d] = along_z(after(arrived[high], arrived[1], *near) if d > high else own_quarter, d % high or high)
     near_far = [across_cores(n) for n in near]
 
-    head = head_weight
-    if width % LANES:
-        head = jnp.pad(head_weight, ((0, 0), (0, LANES - width % LANES)))
 
     pieces, layout = [block], [tuple((("own", 0, 0, i), 0) for i in range(voc_count))]
     for d in range(1, side):
@@ -432,7 +442,7 @@
         layout += layouts[0]
         far = list(third[d])
         if d == depth - 1:
-            first_stats, first_ends, head = score(pieces, layout, table, head, *sizes, loads=True)
+            first_stats, first_ends = score(pieces, layout, table, head, *sizes)
             far = [after(f, first_stats) for f in far]
         for e in range(1, side):
             sent_on = [far[e - 1], across_cores(far[e - 1])]

time: 68.4 us -> 67.6 us (0.988)
  waiting for transfers between devices: 17.4 us -> 15 us
  Pallas kernels: 19.9 us -> 21.7 us
    ppermute x17, waiting for transfers between devices: 17.4 us -> 15 us  [permute(): return lax.ppermute(value, AXES, pairs)]
    pallas_call x0 -> x1, Pallas kernels: none -> 2.34 us  [load(): pl.pallas_call(load_kernel, out_shape=pltpu.VMEM(head.shape, head.dtype),...]
  transfers between devices with their start and end apart: 17 -> 17, of which waited for: 10 -> 10; matrix products, arithmetic and copies ran while one was open for 0% -> 0% of each run, Pallas kernels for 18% -> 19%
where the time goes in v4:
time: 67.6 us; the launch traced here: 67.4 us
  Pallas kernels  21.7 us (32%)
  starting transfers between devices  16.4 us (24%)
  waiting for transfers between devices  15 us (22%)
  blocking collectives  13.3 us (20%)
  between operations  0.7 us (1%)
    ppermute x17, starting transfers between devices, permute(): return lax.ppermute(value, AXES, pairs)  16.4 us
    ppermute x17, waiting for transfers between devices, permute(): return lax.ppermute(value, AXES, pairs)  15 us
    pallas_call x2, Pallas kernels, score(): pl.pallas_call(functools.partial(score_kernel, layout, rows, width, turn_...  14.8 us
    all_to_all x1, blocking collectives, body(): received = lax.all_to_all(sent, AXES, 0, 0)  13.3 us
    pallas_call x1, Pallas kernels, prepare(): pl.pallas_call(prepare_kernel, out_shape=shapes, in_specs=[smem] + [pl.Bl...  2.92 us
    pallas_call x1, Pallas kernels, load(): pl.pallas_call(load_kernel, out_shape=pltpu.VMEM(head.shape, head.dtype),...  2.34 us
    pallas_call x1, Pallas kernels, finish(): pl.pallas_call(finish_kernel, out_shape=(shape, shape), in_specs=[smem, s...  1.66 us
  transfers between devices with their start and end apart: 17, of which 10 were waited for; matrix products, arithmetic and copies ran while one was open for 0% of the time, Pallas kernels for 19%

profile of v4, /device:TPU:0, one launch (start us, length us, event | category | flops | bytes accessed | tf_op | source)
XLA Modules:
  0.0 67.4 jit_solution(9939924984855529136)
XLA Ops:
  0.6 0.1 pad_add_fusion.spot
  0.7 0.0 copy-start
  0.7 2.9 %shard_map.86 = (bf16[256,1664]{1,0:T(8,128)(2,1)S(1)}, bf16[64,1664]{1,0:T(8,128)(2,1)S(1)}, bf16[128,1664]{1,0:T(8,128)(2,1)S(1)}, s32[18]{0:T(128)S(1)}) custom-call(s32[2]{0:T(128)S(1)} %pad_add_fusion.spot, bf16[256,1536]{1,0:T(8,128)(2,1)} %refs_0_.1, f32[1536]{0:T(1024)} %refs_1_.1, s32[256]{0:T(256)} %refs_2_.1, s32[8]{0:T(128)} %lengths.1, ...), custom_call_target="tpu_custom_call" | custom-call | tf_op jit(solution)/shard_map/pallas_call | solution.py:87
  3.6 3.1 %collective-permute-start.1 = (bf16[64,1664]{1,0:T(8,128)(2,1)S(1)}, bf16[64,1664]{1,0:T(8,128)(2,1)S(1)}, u32[]{:S(2)}, u32[]{:S(2)}) collective-permute-start(bf16[64,1664]{1,0:T(8,128)(2,1)S(1)} %get-tuple-element.17), channel_id=1, source_target_pairs={{0,8},{1,9},{2,10},{3,11},{4,12},{5,13},{6,14},{7,15},{8,0},{9,1},... | collective-permute-start | bytes 638984 | tf_op jit(solution)/shard_map/ppermute | solution.py:391
  6.7 1.5 %collective-permute-start.2 = (bf16[128,1664]{1,0:T(8,128)(2,1)S(1)}, bf16[128,1664]{1,0:T(8,128)(2,1)S(1)}, u32[]{:S(2)}, u32[]{:S(2)}) collective-permute-start(bf16[128,1664]{1,0:T(8,128)(2,1)S(1)} %get-tuple-element.18), channel_id=1, source_target_pairs={{0,4},{1,5},{2,6},{3,7},{4,0},{5,1},{6,2},{7,3},{8,12},{9,13},{10,... | collective-permute-start | bytes 1277960 | tf_op jit(solution)/shard_map/ppermute | solution.py:391
  8.3 2.6 %collective-permute-start = (bf16[64,1664]{1,0:T(8,128)(2,1)S(1)}, bf16[64,1664]{1,0:T(8,128)(2,1)S(1)}, u32[]{:S(2)}, u32[]{:S(2)}) collective-permute-start(bf16[64,1664]{1,0:T(8,128)(2,1)S(1)} %get-tuple-element.17), channel_id=1, source_target_pairs={{0,16},{1,17},{2,18},{3,19},{4,20},{5,21},{6,22},{7,23},{8,24},{9,... | collective-permute-start | bytes 638984 | tf_op jit(solution)/shard_map/ppermute | solution.py:391
  10.8 2.3 %shard_map.87.head = bf16[1536,1536]{1,0:T(8,128)(2,1)S(1)} custom-call(bf16[1536,1536]{1,0:T(8,128)(2,1)} %stored.1), custom_call_target="tpu_custom_call" | custom-call | bytes 9437184 | tf_op jit(solution)/shard_map/pallas_call | solution.py:104
  13.2 0.0 copy-done
  13.2 1.7 %collective-permute-done.1 = bf16[64,1664]{1,0:T(8,128)(2,1)S(1)} collective-permute-done((bf16[64,1664]{1,0:T(8,128)(2,1)S(1)}, bf16[64,1664]{1,0:T(8,128)(2,1)S(1)}, u32[]{:S(2)}, u32[]{:S(2)}) %collective-permute-start.1) | collective-permute-done | bytes 213024 | tf_op jit(solution)/shard_map/ppermute | solution.py:391
  14.9 3.0 %collective-permute-start.4 = (bf16[64,1664]{1,0:T(8,128)(2,1)S(1)}, bf16[64,1664]{1,0:T(8,128)(2,1)S(1)}, u32[]{:S(2)}, u32[]{:S(2)}) collective-permute-start(bf16[64,1664]{1,0:T(8,128)(2,1)S(1)} %collective-permute-done.1), channel_id=1, source_target_pairs={{0,4},{1,3},{2,6},{3,1},{4,0},{5,7},{6,2},{7,5},{8,12},{9,11},{10,... | collective-permute-start | bytes 638984 | tf_op jit(solution)/shard_map/ppermute | solution.py:391
  17.9 2.4 %collective-permute-done = bf16[64,1664]{1,0:T(8,128)(2,1)S(1)} collective-permute-done((bf16[64,1664]{1,0:T(8,128)(2,1)S(1)}, bf16[64,1664]{1,0:T(8,128)(2,1)S(1)}, u32[]{:S(2)}, u32[]{:S(2)}) %collective-permute-start) | collective-permute-done | bytes 213024 | tf_op jit(solution)/shard_map/ppermute | solution.py:391
  20.3 0.0 collective-permute-done.2.rest_1_
  20.3 0.0 collective-permute-start.8
  20.3 0.6 collective-permute-start.3
  20.9 0.8 %collective-permute-done.4 = bf16[64,1664]{1,0:T(8,128)(2,1)S(1)} collective-permute-done((bf16[64,1664]{1,0:T(8,128)(2,1)S(1)}, bf16[64,1664]{1,0:T(8,128)(2,1)S(1)}, u32[]{:S(2)}, u32[]{:S(2)}) %collective-permute-start.4) | collective-permute-done | bytes 213024 | tf_op jit(solution)/shard_map/ppermute | solution.py:391
  21.7 1.6 %collective-permute-start.5 = (bf16[128,1664]{1,0:T(8,128)(2,1)S(1)}, bf16[128,1664]{1,0:T(8,128)(2,1)S(1)}, u32[]{:S(2)}, u32[]{:S(2)}) collective-permute-start(bf16[128,1664]{1,0:T(8,128)(2,1)S(1)} %constant_dynamic-update-slice_fusion.rest_3_), channel_id=1, source_target_pairs={{0,2},{1,5},{2,0},{3,7},{4,6},{5,1},{6,4},{7,3},{8,10},{9,13},{10,... | collective-permute-start | bytes 1277960 | tf_op jit(solution)/shard_map/ppermute | solution.py:391
  23.3 0.0 collective-permute-start.12
  23.3 0.5 collective-permute-start.11
  23.8 2.3 %collective-permute-done.8 = bf16[64,1664]{1,0:T(8,128)(2,1)S(1)} collective-permute-done((bf16[64,1664]{1,0:T(8,128)(2,1)S(1)}, bf16[64,1664]{1,0:T(8,128)(2,1)S(1)}, u32[]{:S(2)}, u32[]{:S(2)}) %collective-permute-start.8) | collective-permute-done | bytes 213024 | tf_op jit(solution)/shard_map/ppermute | solution.py:391
  26.1 0.4 collective-permute-start.9
  26.6 1.9 %collective-permute-done.3 = bf16[64,1664]{1,0:T(8,128)(2,1)S(1)} collective-permute-done((bf16[64,1664]{1,0:T(8,128)(2,1)S(1)}, bf16[64,1664]{1,0:T(8,128)(2,1)S(1)}, u32[]{:S(2)}, u32[]{:S(2)}) %collective-permute-start.3) | collective-permute-done | bytes 213024 | tf_op jit(solution)/shard_map/ppermute | solution.py:391
  28.5 3.5 %collective-permute-done.9 = bf16[64,1664]{1,0:T(8,128)(2,1)S(1)} collective-permute-done((bf16[64,1664]{1,0:T(8,128)(2,1)S(1)}, bf16[64,1664]{1,0:T(8,128)(2,1)S(1)}, u32[]{:S(2)}, u32[]{:S(2)}) %collective-permute-start.9) | collective-permute-done | bytes 213024 | tf_op jit(solution)/shard_map/ppermute | solution.py:391
  32.0 0.2 collective-permute-done.5.rest_5_
  32.2 0.0 collective-permute-start.15
  32.2 0.5 collective-permute-start.14
  32.7 0.0 collective-permute-start.13
  32.7 0.0 collective-permute-done.12.rest_4_
  32.7 1.5 %collective-permute-start.10 = (bf16[128,1664]{1,0:T(8,128)(2,1)S(1)}, bf16[128,1664]{1,0:T(8,128)(2,1)S(1)}, u32[]{:S(2)}, u32[]{:S(2)}) collective-permute-start(bf16[128,1664]{1,0:T(8,128)(2,1)S(1)} %pad_maximum_fusion.1.rest_9_), channel_id=1, source_target_pairs={{0,2},{1,5},{2,0},{3,7},{4,6},{5,1},{6,4},{7,3},{8,10},{9,13},{10,... | collective-permute-start | bytes 1277960 | tf_op jit(solution)/shard_map/ppermute | solution.py:391
  34.2 0.0 collective-permute-done.11.rest_2_
  34.2 0.5 collective-permute-start.6
  34.8 0.0 collective-permute-done.15.rest_10_
  34.8 0.0 collective-permute-done.14.rest_8_
  34.8 0.4 collective-permute-done.13.rest_6_
  35.2 10.5 %shard_map.88 = (f32[8,2,8,128]{3,2,1,0:T(8,128)S(1)}, bf16[32,1664]{1,0:T(8,128)(2,1)S(1)}) custom-call(s32[18]{0:T(128)S(1)} %get-tuple-element.16.table, bf16[1536,1536]{1,0:T(8,128)(2,1)S(1)} %shard_map.87.head, bf16[256,1664]{1,0:T(8,128)(2,1)S(1)} %get-tuple-element.24.rest_0_, bf16[128,1664]{1,0:T(8,128)(2,1)S(1)} %collective-permute-done.2.rest_1_, ...), custom_call_target="tpu_custom_call" | custom-call | flops 7247757312 | bytes 9437184 | tf_op jit(solution)/shard_map/pallas_call | solution.py:310
  45.7 0.0 collective-permute-done.10.rest_2_
  45.7 0.2 collective-permute-start.16
  45.9 0.0 collective-permute-done.6.rest_0_
  45.9 0.4 collective-permute-start.7
  46.3 1.3 %collective-permute-done.16.rest_3_ = bf16[128,1664]{1,0:T(8,128)(2,1)S(1)} collective-permute-done((bf16[128,1664]{1,0:T(8,128)(2,1)S(1)}, bf16[128,1664]{1,0:T(8,128)(2,1)S(1)}, u32[]{:S(2)}, u32[]{:S(2)}) %collective-permute-start.16) | collective-permute-done | bytes 426016 | tf_op jit(solution)/shard_map/ppermute | solution.py:391
  47.5 0.6 collective-permute-done.7.rest_1_
  48.1 4.3 %shard_map.89 = f32[32,8,128]{2,1,0:T(8,128)S(1)} custom-call(s32[18]{0:T(128)S(1)} %get-tuple-element.16.table, bf16[1536,1536]{1,0:T(8,128)(2,1)S(1)} %shard_map.87.head, bf16[128,1664]{1,0:T(8,128)(2,1)S(1)} %collective-permute-done.6.rest_0_, bf16[128,1664]{1,0:T(8,128)(2,1)S(1)} %collective-permute-done.7.rest_1_, ...), custom_call_target="tpu_custom_call" | custom-call | flops 2415919104 | bytes 6291456 | tf_op jit(solution)/shard_map/pallas_call | solution.py:310
  52.4 13.3 %all_to_all.5.received = f32[32,8,128]{2,1,0:T(8,128)} all-to-all(f32[32,8,128]{2,1,0:T(8,128)S(1)} %shard_map.89), channel_id=1, replica_groups=mesh['tok'=8,'voc'=4] {'tok','voc'}, dimensions={0} | all-to-all | bytes 262144 | tf_op jit(solution)/shard_map/all_to_all | solution.py:457
  65.8 1.7 %shard_map.90 = (f32[2,128]{1,0:T(2,128)}, f32[2,128]{1,0:T(2,128)}) custom-call(s32[2]{0:T(128)} %copy-done, s32[8]{0:T(128)} %lengths.1, f32[32,8,128]{2,1,0:T(8,128)} %all_to_all.5.received), custom_call_target="tpu_custom_call" | custom-call | tf_op jit(solution)/shard_map/pallas_call | solution.py:365
  (4 shorter events, 0.1 us)
Async XLA Ops:
  0.7 12.5 %copy-start = (s32[2]{0:T(128)}, s32[2]{0:T(128)S(1)}, u32[]{:S(2)}) copy-start(s32[2]{0:T(128)S(1)} %pad_add_fusion.spot) | copy-start | bytes 28
  3.6 11.2 %collective-permute-start.1 = (bf16[64,1664]{1,0:T(8,128)(2,1)S(1)}, bf16[64,1664]{1,0:T(8,128)(2,1)S(1)}, u32[]{:S(2)}, u32[]{:S(2)}) collective-permute-start(bf16[64,1664]{1,0:T(8,128)(2,1)S(1)} %get-tuple-element.17), channel_id=1, source_target_pairs={{0,8},{1,9},{2,10},{3,11},{4,12},{5,13},{6,14},{7,15},{8,0},{9,1},... | collective-permute-start | bytes 638984 | tf_op jit(solution)/shard_map/ppermute | solution.py:391
  6.7 13.5 %collective-permute-start.2 = (bf16[128,1664]{1,0:T(8,128)(2,1)S(1)}, bf16[128,1664]{1,0:T(8,128)(2,1)S(1)}, u32[]{:S(2)}, u32[]{:S(2)}) collective-permute-start(bf16[128,1664]{1,0:T(8,128)(2,1)S(1)} %get-tuple-element.18), channel_id=1, source_target_pairs={{0,4},{1,5},{2,6},{3,7},{4,0},{5,1},{6,2},{7,3},{8,12},{9,13},{10,... | collective-permute-start | bytes 1277960 | tf_op jit(solution)/shard_map/ppermute | solution.py:391
  8.3 12.0 %collective-permute-start = (bf16[64,1664]{1,0:T(8,128)(2,1)S(1)}, bf16[64,1664]{1,0:T(8,128)(2,1)S(1)}, u32[]{:S(2)}, u32[]{:S(2)}) collective-permute-start(bf16[64,1664]{1,0:T(8,128)(2,1)S(1)} %get-tuple-element.17), channel_id=1, source_target_pairs={{0,16},{1,17},{2,18},{3,19},{4,20},{5,21},{6,22},{7,23},{8,24},{9,... | collective-permute-start | bytes 638984 | tf_op jit(solution)/shard_map/ppermute | solution.py:391
  14.9 6.9 %collective-permute-start.4 = (bf16[64,1664]{1,0:T(8,128)(2,1)S(1)}, bf16[64,1664]{1,0:T(8,128)(2,1)S(1)}, u32[]{:S(2)}, u32[]{:S(2)}) collective-permute-start(bf16[64,1664]{1,0:T(8,128)(2,1)S(1)} %collective-permute-done.1), channel_id=1, source_target_pairs={{0,4},{1,3},{2,6},{3,1},{4,0},{5,7},{6,2},{7,5},{8,12},{9,11},{10,... | collective-permute-start | bytes 638984 | tf_op jit(solution)/shard_map/ppermute | solution.py:391
  20.3 5.8 %collective-permute-start.8 = (bf16[64,1664]{1,0:T(8,128)(2,1)S(1)}, bf16[64,1664]{1,0:T(8,128)(2,1)S(1)}, u32[]{:S(2)}, u32[]{:S(2)}) collective-permute-start(bf16[64,1664]{1,0:T(8,128)(2,1)S(1)} %collective-permute-done), channel_id=1, source_target_pairs={{0,8},{1,9},{2,10},{3,11},{4,12},{5,13},{6,14},{7,15},{8,0},{9,1},... | collective-permute-start | bytes 638984 | tf_op jit(solution)/shard_map/ppermute | solution.py:391
  20.3 8.2 %collective-permute-start.3 = (bf16[64,1664]{1,0:T(8,128)(2,1)S(1)}, bf16[64,1664]{1,0:T(8,128)(2,1)S(1)}, u32[]{:S(2)}, u32[]{:S(2)}) collective-permute-start(bf16[64,1664]{1,0:T(8,128)(2,1)S(1)} %collective-permute-done), channel_id=1, source_target_pairs={{0,4},{1,3},{2,6},{3,1},{4,0},{5,7},{6,2},{7,5},{8,12},{9,11},{10,... | collective-permute-start | bytes 638984 | tf_op jit(solution)/shard_map/ppermute | solution.py:391
  21.7 10.5 %collective-permute-start.5 = (bf16[128,1664]{1,0:T(8,128)(2,1)S(1)}, bf16[128,1664]{1,0:T(8,128)(2,1)S(1)}, u32[]{:S(2)}, u32[]{:S(2)}) collective-permute-start(bf16[128,1664]{1,0:T(8,128)(2,1)S(1)} %constant_dynamic-update-slice_fusion.rest_3_), channel_id=1, source_target_pairs={{0,2},{1,5},{2,0},{3,7},{4,6},{5,1},{6,4},{7,3},{8,10},{9,13},{10,... | collective-permute-start | bytes 1277960 | tf_op jit(solution)/shard_map/ppermute | solution.py:391
  23.3 9.4 %collective-permute-start.12 = (bf16[128,1664]{1,0:T(8,128)(2,1)S(1)}, bf16[128,1664]{1,0:T(8,128)(2,1)S(1)}, u32[]{:S(2)}, u32[]{:S(2)}) collective-permute-start(bf16[128,1664]{1,0:T(8,128)(2,1)S(1)} %constant_dynamic-update-slice_fusion.rest_3_), channel_id=1, source_target_pairs={{0,1},{1,0},{2,3},{3,2},{4,5},{5,4},{6,7},{7,6},{8,9},{9,8},{10,11... | collective-permute-start | bytes 1277960 | tf_op jit(solution)/shard_map/ppermute | solution.py:391
  23.3 10.9 %collective-permute-start.11 = (bf16[128,1664]{1,0:T(8,128)(2,1)S(1)}, bf16[128,1664]{1,0:T(8,128)(2,1)S(1)}, u32[]{:S(2)}, u32[]{:S(2)}) collective-permute-start(bf16[128,1664]{1,0:T(8,128)(2,1)S(1)} %collective-permute-done.2.rest_1_), channel_id=1, source_target_pairs={{0,1},{1,0},{2,3},{3,2},{4,5},{5,4},{6,7},{7,6},{8,9},{9,8},{10,11... | collective-permute-start | bytes 1277960 | tf_op jit(solution)/shard_map/ppermute | solution.py:391
  26.1 5.8 %collective-permute-start.9 = (bf16[64,1664]{1,0:T(8,128)(2,1)S(1)}, bf16[64,1664]{1,0:T(8,128)(2,1)S(1)}, u32[]{:S(2)}, u32[]{:S(2)}) collective-permute-start(bf16[64,1664]{1,0:T(8,128)(2,1)S(1)} %collective-permute-done.8), channel_id=1, source_target_pairs={{0,4},{1,3},{2,6},{3,1},{4,0},{5,7},{6,2},{7,5},{8,12},{9,11},{10,... | collective-permute-start | bytes 638984 | tf_op jit(solution)/shard_map/ppermute | solution.py:391
  32.2 2.6 %collective-permute-start.15 = (bf16[128,1664]{1,0:T(8,128)(2,1)S(1)}, bf16[128,1664]{1,0:T(8,128)(2,1)S(1)}, u32[]{:S(2)}, u32[]{:S(2)}) collective-permute-start(bf16[128,1664]{1,0:T(8,128)(2,1)S(1)} %pad_maximum_fusion.1.rest_9_), channel_id=1, source_target_pairs={{0,1},{1,0},{2,3},{3,2},{4,5},{5,4},{6,7},{7,6},{8,9},{9,8},{10,11... | collective-permute-start | bytes 1277960 | tf_op jit(solution)/shard_map/ppermute | solution.py:391
  32.2 2.6 %collective-permute-start.14 = (bf16[128,1664]{1,0:T(8,128)(2,1)S(1)}, bf16[128,1664]{1,0:T(8,128)(2,1)S(1)}, u32[]{:S(2)}, u32[]{:S(2)}) collective-permute-start(bf16[128,1664]{1,0:T(8,128)(2,1)S(1)} %pad_maximum_fusion.rest_7_), channel_id=1, source_target_pairs={{0,1},{1,0},{2,3},{3,2},{4,5},{5,4},{6,7},{7,6},{8,9},{9,8},{10,11... | collective-permute-start | bytes 1277960 | tf_op jit(solution)/shard_map/ppermute | solution.py:391
  32.7 2.5 %collective-permute-start.13 = (bf16[128,1664]{1,0:T(8,128)(2,1)S(1)}, bf16[128,1664]{1,0:T(8,128)(2,1)S(1)}, u32[]{:S(2)}, u32[]{:S(2)}) collective-permute-start(bf16[128,1664]{1,0:T(8,128)(2,1)S(1)} %collective-permute-done.5.rest_5_), channel_id=1, source_target_pairs={{0,1},{1,0},{2,3},{3,2},{4,5},{5,4},{6,7},{7,6},{8,9},{9,8},{10,11... | collective-permute-start | bytes 1277960 | tf_op jit(solution)/shard_map/ppermute | solution.py:391
  32.7 13.0 %collective-permute-start.10 = (bf16[128,1664]{1,0:T(8,128)(2,1)S(1)}, bf16[128,1664]{1,0:T(8,128)(2,1)S(1)}, u32[]{:S(2)}, u32[]{:S(2)}) collective-permute-start(bf16[128,1664]{1,0:T(8,128)(2,1)S(1)} %pad_maximum_fusion.1.rest_9_), channel_id=1, source_target_pairs={{0,2},{1,5},{2,0},{3,7},{4,6},{5,1},{6,4},{7,3},{8,10},{9,13},{10,... | collective-permute-start | bytes 1277960 | tf_op jit(solution)/shard_map/ppermute | solution.py:391
  34.2 11.7 %collective-permute-start.6 = (bf16[128,1664]{1,0:T(8,128)(2,1)S(1)}, bf16[128,1664]{1,0:T(8,128)(2,1)S(1)}, u32[]{:S(2)}, u32[]{:S(2)}) collective-permute-start(bf16[128,1664]{1,0:T(8,128)(2,1)S(1)} %pad_maximum_fusion.rest_7_), channel_id=1, source_target_pairs={{0,2},{1,5},{2,0},{3,7},{4,6},{5,1},{6,4},{7,3},{8,10},{9,13},{10,... | collective-permute-start | bytes 1277960 | tf_op jit(solution)/shard_map/ppermute | solution.py:391
  45.7 1.8 %collective-permute-start.16 = (bf16[128,1664]{1,0:T(8,128)(2,1)S(1)}, bf16[128,1664]{1,0:T(8,128)(2,1)S(1)}, u32[]{:S(2)}, u32[]{:S(2)}) collective-permute-start(bf16[128,1664]{1,0:T(8,128)(2,1)S(1)} %collective-permute-done.10.rest_2_), channel_id=1, source_target_pairs={{0,1},{1,0},{2,3},{3,2},{4,5},{5,4},{6,7},{7,6},{8,9},{9,8},{10,11... | collective-permute-start | bytes 1277960 | tf_op jit(solution)/shard_map/ppermute | solution.py:391
  45.9 2.2 %collective-permute-start.7 = (bf16[128,1664]{1,0:T(8,128)(2,1)S(1)}, bf16[128,1664]{1,0:T(8,128)(2,1)S(1)}, u32[]{:S(2)}, u32[]{:S(2)}) collective-permute-start(bf16[128,1664]{1,0:T(8,128)(2,1)S(1)} %collective-permute-done.6.rest_0_), channel_id=1, source_target_pairs={{0,1},{1,0},{2,3},{3,2},{4,5},{5,4},{6,7},{7,6},{8,9},{9,8},{10,11... | collective-permute-start | bytes 1277960 | tf_op jit(solution)/shard_map/ppermute | solution.py:391

commit v5 on v4

--- a/solution.py
+++ b/solution.py
@@ -434,7 +434,7 @@
             start = after(start, arrived[1], *near)
             second[d] = [second_hop(start, e) for e in range(1, side)]
         gathered = jnp.concatenate([start] + second[d], axis=0)
-        if d > 1:
+        if d == 2:
             gathered = after(gathered, *third[1])
         third[d] = [third_hop(gathered, e) for e in range(1, side)]
         pieces += [gathered, across_cores(gathered)]

time: 67.6 us -> 67.7 us (level); the launches traced: 67.4 us -> 66.5 us
  blocking collectives: 13.3 us -> 12.6 us
    all_to_all x1, blocking collectives: 13.3 us -> 12.6 us  [body(): received = lax.all_to_all(sent, AXES, 0, 0)]
where the time goes in v5:
time: 67.7 us; the launch traced here: 66.5 us
  Pallas kernels  21.7 us (32%)
  starting transfers between devices  16.5 us (24%)
  waiting for transfers between devices  14.8 us (22%)
  blocking collectives  12.6 us (19%)
  between operations  0.71 us (1%)
    ppermute x17, starting transfers between devices, permute(): return lax.ppermute(value, AXES, pairs)  16.5 us
    pallas_call x2, Pallas kernels, score(): pl.pallas_call(functools.partial(score_kernel, layout, rows, width, turn_...  14.8 us
    ppermute x17, waiting for transfers between devices, permute(): return lax.ppermute(value, AXES, pairs)  14.8 us
    all_to_all x1, blocking collectives, body(): received = lax.all_to_all(sent, AXES, 0, 0)  12.6 us
    pallas_call x1, Pallas kernels, prepare(): pl.pallas_call(prepare_kernel, out_shape=shapes, in_specs=[smem] + [pl.Bl...  2.92 us
    pallas_call x1, Pallas kernels, load(): pl.pallas_call(load_kernel, out_shape=pltpu.VMEM(head.shape, head.dtype),...  2.34 us
    pallas_call x1, Pallas kernels, finish(): pl.pallas_call(finish_kernel, out_shape=(shape, shape), in_specs=[smem, s...  1.66 us
  transfers between devices with their start and end apart: 17, of which 10 were waited for; matrix products, arithmetic and copies ran while one was open for 0% of the time, Pallas kernels for 19%

profile of v5, /device:TPU:0, one launch (start us, length us, event | category | flops | bytes accessed | tf_op | source)
XLA Modules:
  0.0 66.5 jit_solution(2515028295921667946)
XLA Ops:
  0.6 0.1 pad_add_fusion.spot
  0.7 0.0 copy-start
  0.7 2.9 %shard_map.86 = (bf16[256,1664]{1,0:T(8,128)(2,1)S(1)}, bf16[64,1664]{1,0:T(8,128)(2,1)S(1)}, bf16[128,1664]{1,0:T(8,128)(2,1)S(1)}, s32[18]{0:T(128)S(1)}) custom-call(s32[2]{0:T(128)S(1)} %pad_add_fusion.spot, bf16[256,1536]{1,0:T(8,128)(2,1)} %refs_0_.1, f32[1536]{0:T(1024)} %refs_1_.1, s32[256]{0:T(256)} %refs_2_.1, s32[8]{0:T(128)} %lengths.1, ...), custom_call_target="tpu_custom_call" | custom-call | tf_op jit(solution)/shard_map/pallas_call | solution.py:87
  3.6 3.1 %collective-permute-start.1 = (bf16[64,1664]{1,0:T(8,128)(2,1)S(1)}, bf16[64,1664]{1,0:T(8,128)(2,1)S(1)}, u32[]{:S(2)}, u32[]{:S(2)}) collective-permute-start(bf16[64,1664]{1,0:T(8,128)(2,1)S(1)} %get-tuple-element.16), channel_id=1, source_target_pairs={{0,8},{1,9},{2,10},{3,11},{4,12},{5,13},{6,14},{7,15},{8,0},{9,1},... | collective-permute-start | bytes 638984 | tf_op jit(solution)/shard_map/ppermute | solution.py:391
  6.7 1.5 %collective-permute-start.2 = (bf16[128,1664]{1,0:T(8,128)(2,1)S(1)}, bf16[128,1664]{1,0:T(8,128)(2,1)S(1)}, u32[]{:S(2)}, u32[]{:S(2)}) collective-permute-start(bf16[128,1664]{1,0:T(8,128)(2,1)S(1)} %get-tuple-element.17), channel_id=1, source_target_pairs={{0,4},{1,5},{2,6},{3,7},{4,0},{5,1},{6,2},{7,3},{8,12},{9,13},{10,... | collective-permute-start | bytes 1277960 | tf_op jit(solution)/shard_map/ppermute | solution.py:391
  8.3 2.6 %collective-permute-start = (bf16[64,1664]{1,0:T(8,128)(2,1)S(1)}, bf16[64,1664]{1,0:T(8,128)(2,1)S(1)}, u32[]{:S(2)}, u32[]{:S(2)}) collective-permute-start(bf16[64,1664]{1,0:T(8,128)(2,1)S(1)} %get-tuple-element.16), channel_id=1, source_target_pairs={{0,16},{1,17},{2,18},{3,19},{4,20},{5,21},{6,22},{7,23},{8,24},{9,... | collective-permute-start | bytes 638984 | tf_op jit(solution)/shard_map/ppermute | solution.py:391
  10.8 2.3 %shard_map.87.head = bf16[1536,1536]{1,0:T(8,128)(2,1)S(1)} custom-call(bf16[1536,1536]{1,0:T(8,128)(2,1)} %stored.1), custom_call_target="tpu_custom_call" | custom-call | bytes 9437184 | tf_op jit(solution)/shard_map/pallas_call | solution.py:104
  13.2 0.0 copy-done
  13.2 1.7 %collective-permute-done.1 = bf16[64,1664]{1,0:T(8,128)(2,1)S(1)} collective-permute-done((bf16[64,1664]{1,0:T(8,128)(2,1)S(1)}, bf16[64,1664]{1,0:T(8,128)(2,1)S(1)}, u32[]{:S(2)}, u32[]{:S(2)}) %collective-permute-start.1) | collective-permute-done | bytes 213024 | tf_op jit(solution)/shard_map/ppermute | solution.py:391
  14.9 3.0 %collective-permute-start.4 = (bf16[64,1664]{1,0:T(8,128)(2,1)S(1)}, bf16[64,1664]{1,0:T(8,128)(2,1)S(1)}, u32[]{:S(2)}, u32[]{:S(2)}) collective-permute-start(bf16[64,1664]{1,0:T(8,128)(2,1)S(1)} %collective-permute-done.1), channel_id=1, source_target_pairs={{0,4},{1,3},{2,6},{3,1},{4,0},{5,7},{6,2},{7,5},{8,12},{9,11},{10,... | collective-permute-start | bytes 638984 | tf_op jit(solution)/shard_map/ppermute | solution.py:391
  17.9 2.4 %collective-permute-done = bf16[64,1664]{1,0:T(8,128)(2,1)S(1)} collective-permute-done((bf16[64,1664]{1,0:T(8,128)(2,1)S(1)}, bf16[64,1664]{1,0:T(8,128)(2,1)S(1)}, u32[]{:S(2)}, u32[]{:S(2)}) %collective-permute-start) | collective-permute-done | bytes 213024 | tf_op jit(solution)/shard_map/ppermute | solution.py:391
  20.3 0.0 collective-permute-done.2.rest_1_
  20.3 0.0 collective-permute-start.8
  20.3 0.6 collective-permute-start.3
  20.9 0.8 %collective-permute-done.4 = bf16[64,1664]{1,0:T(8,128)(2,1)S(1)} collective-permute-done((bf16[64,1664]{1,0:T(8,128)(2,1)S(1)}, bf16[64,1664]{1,0:T(8,128)(2,1)S(1)}, u32[]{:S(2)}, u32[]{:S(2)}) %collective-permute-start.4) | collective-permute-done | bytes 213024 | tf_op jit(solution)/shard_map/ppermute | solution.py:391
  21.7 1.6 %collective-permute-start.5 = (bf16[128,1664]{1,0:T(8,128)(2,1)S(1)}, bf16[128,1664]{1,0:T(8,128)(2,1)S(1)}, u32[]{:S(2)}, u32[]{:S(2)}) collective-permute-start(bf16[128,1664]{1,0:T(8,128)(2,1)S(1)} %constant_dynamic-update-slice_fusion.rest_3_), channel_id=1, source_target_pairs={{0,2},{1,5},{2,0},{3,7},{4,6},{5,1},{6,4},{7,3},{8,10},{9,13},{10,... | collective-permute-start | bytes 1277960 | tf_op jit(solution)/shard_map/ppermute | solution.py:391
  23.3 0.0 collective-permute-start.12
  23.3 0.5 collective-permute-start.11
  23.8 2.3 %collective-permute-done.8 = bf16[64,1664]{1,0:T(8,128)(2,1)S(1)} collective-permute-done((bf16[64,1664]{1,0:T(8,128)(2,1)S(1)}, bf16[64,1664]{1,0:T(8,128)(2,1)S(1)}, u32[]{:S(2)}, u32[]{:S(2)}) %collective-permute-start.8) | collective-permute-done | bytes 213024 | tf_op jit(solution)/shard_map/ppermute | solution.py:391
  26.1 0.4 collective-permute-start.9
  26.6 1.9 %collective-permute-done.3 = bf16[64,1664]{1,0:T(8,128)(2,1)S(1)} collective-permute-done((bf16[64,1664]{1,0:T(8,128)(2,1)S(1)}, bf16[64,1664]{1,0:T(8,128)(2,1)S(1)}, u32[]{:S(2)}, u32[]{:S(2)}) %collective-permute-start.3) | collective-permute-done | bytes 213024 | tf_op jit(solution)/shard_map/ppermute | solution.py:391
  28.5 3.4 %collective-permute-done.9 = bf16[64,1664]{1,0:T(8,128)(2,1)S(1)} collective-permute-done((bf16[64,1664]{1,0:T(8,128)(2,1)S(1)}, bf16[64,1664]{1,0:T(8,128)(2,1)S(1)}, u32[]{:S(2)}, u32[]{:S(2)}) %collective-permute-start.9) | collective-permute-done | bytes 213024 | tf_op jit(solution)/shard_map/ppermute | solution.py:391
  32.0 0.1 collective-permute-start.15
  32.1 0.1 collective-permute-done.5.rest_5_
  32.2 0.4 collective-permute-start.14
  32.6 0.1 collective-permute-start.13
  32.7 0.0 collective-permute-done.12.rest_4_
  32.7 1.5 %collective-permute-start.10 = (bf16[128,1664]{1,0:T(8,128)(2,1)S(1)}, bf16[128,1664]{1,0:T(8,128)(2,1)S(1)}, u32[]{:S(2)}, u32[]{:S(2)}) collective-permute-start(bf16[128,1664]{1,0:T(8,128)(2,1)S(1)} %constant_dynamic-update-slice_fusion.2.rest_9_), channel_id=1, source_target_pairs={{0,2},{1,5},{2,0},{3,7},{4,6},{5,1},{6,4},{7,3},{8,10},{9,13},{10,... | collective-permute-start | bytes 1277960 | tf_op jit(solution)/shard_map/ppermute | solution.py:391
  34.2 0.0 collective-permute-done.11.rest_2_
  34.2 0.5 collective-permute-start.6
  34.8 0.0 collective-permute-done.15.rest_10_
  34.8 0.0 collective-permute-done.14.rest_8_
  34.8 0.3 collective-permute-done.13.rest_6_
  35.1 10.5 %shard_map.88 = (f32[8,2,8,128]{3,2,1,0:T(8,128)S(1)}, bf16[32,1664]{1,0:T(8,128)(2,1)S(1)}) custom-call(s32[18]{0:T(128)S(1)} %get-tuple-element.15.table, bf16[1536,1536]{1,0:T(8,128)(2,1)S(1)} %shard_map.87.head, bf16[256,1664]{1,0:T(8,128)(2,1)S(1)} %get-tuple-element.22.rest_0_, bf16[128,1664]{1,0:T(8,128)(2,1)S(1)} %collective-permute-done.2.rest_1_, ...), custom_call_target="tpu_custom_call" | custom-call | flops 7247757312 | bytes 9437184 | tf_op jit(solution)/shard_map/pallas_call | solution.py:310
  45.6 0.0 collective-permute-done.10.rest_2_
  45.6 0.2 collective-permute-start.16
  45.8 0.0 collective-permute-done.6.rest_0_
  45.8 0.4 collective-permute-start.7
  46.1 1.3 %collective-permute-done.16.rest_3_ = bf16[128,1664]{1,0:T(8,128)(2,1)S(1)} collective-permute-done((bf16[128,1664]{1,0:T(8,128)(2,1)S(1)}, bf16[128,1664]{1,0:T(8,128)(2,1)S(1)}, u32[]{:S(2)}, u32[]{:S(2)}) %collective-permute-start.16) | collective-permute-done | bytes 426016 | tf_op jit(solution)/shard_map/ppermute | solution.py:391
  47.4 0.6 collective-permute-done.7.rest_1_
  48.0 4.3 %shard_map.89 = f32[32,8,128]{2,1,0:T(8,128)S(1)} custom-call(s32[18]{0:T(128)S(1)} %get-tuple-element.15.table, bf16[1536,1536]{1,0:T(8,128)(2,1)S(1)} %shard_map.87.head, bf16[128,1664]{1,0:T(8,128)(2,1)S(1)} %collective-permute-done.6.rest_0_, bf16[128,1664]{1,0:T(8,128)(2,1)S(1)} %collective-permute-done.7.rest_1_, ...), custom_call_target="tpu_custom_call" | custom-call | flops 2415919104 | bytes 6291456 | tf_op jit(solution)/shard_map/pallas_call | solution.py:310
  52.3 12.6 %all_to_all.5.received = f32[32,8,128]{2,1,0:T(8,128)} all-to-all(f32[32,8,128]{2,1,0:T(8,128)S(1)} %shard_map.89), channel_id=1, replica_groups=mesh['tok'=8,'voc'=4] {'tok','voc'}, dimensions={0} | all-to-all | bytes 262144 | tf_op jit(solution)/shard_map/all_to_all | solution.py:457
  64.9 1.7 %shard_map.90 = (f32[2,128]{1,0:T(2,128)}, f32[2,128]{1,0:T(2,128)}) custom-call(s32[2]{0:T(128)} %copy-done, s32[8]{0:T(128)} %lengths.1, f32[32,8,128]{2,1,0:T(8,128)} %all_to_all.5.received), custom_call_target="tpu_custom_call" | custom-call | tf_op jit(solution)/shard_map/pallas_call | solution.py:365
  (5 shorter events, 0.1 us)
Async XLA Ops:
  0.7 12.5 %copy-start = (s32[2]{0:T(128)}, s32[2]{0:T(128)S(1)}, u32[]{:S(2)}) copy-start(s32[2]{0:T(128)S(1)} %pad_add_fusion.spot) | copy-start | bytes 28
  3.6 11.2 %collective-permute-start.1 = (bf16[64,1664]{1,0:T(8,128)(2,1)S(1)}, bf16[64,1664]{1,0:T(8,128)(2,1)S(1)}, u32[]{:S(2)}, u32[]{:S(2)}) collective-permute-start(bf16[64,1664]{1,0:T(8,128)(2,1)S(1)} %get-tuple-element.16), channel_id=1, source_target_pairs={{0,8},{1,9},{2,10},{3,11},{4,12},{5,13},{6,14},{7,15},{8,0},{9,1},... | collective-permute-start | bytes 638984 | tf_op jit(solution)/shard_map/ppermute | solution.py:391
  6.7 13.5 %collective-permute-start.2 = (bf16[128,1664]{1,0:T(8,128)(2,1)S(1)}, bf16[128,1664]{1,0:T(8,128)(2,1)S(1)}, u32[]{:S(2)}, u32[]{:S(2)}) collective-permute-start(bf16[128,1664]{1,0:T(8,128)(2,1)S(1)} %get-tuple-element.17), channel_id=1, source_target_pairs={{0,4},{1,5},{2,6},{3,7},{4,0},{5,1},{6,2},{7,3},{8,12},{9,13},{10,... | collective-permute-start | bytes 1277960 | tf_op jit(solution)/shard_map/ppermute | solution.py:391
  8.3 12.0 %collective-permute-start = (bf16[64,1664]{1,0:T(8,128)(2,1)S(1)}, bf16[64,1664]{1,0:T(8,128)(2,1)S(1)}, u32[]{:S(2)}, u32[]{:S(2)}) collective-permute-start(bf16[64,1664]{1,0:T(8,128)(2,1)S(1)} %get-tuple-element.16), channel_id=1, source_target_pairs={{0,16},{1,17},{2,18},{3,19},{4,20},{5,21},{6,22},{7,23},{8,24},{9,... | collective-permute-start | bytes 638984 | tf_op jit(solution)/shard_map/ppermute | solution.py:391
  14.9 6.9 %collective-permute-start.4 = (bf16[64,1664]{1,0:T(8,128)(2,1)S(1)}, bf16[64,1664]{1,0:T(8,128)(2,1)S(1)}, u32[]{:S(2)}, u32[]{:S(2)}) collective-permute-start(bf16[64,1664]{1,0:T(8,128)(2,1)S(1)} %collective-permute-done.1), channel_id=1, source_target_pairs={{0,4},{1,3},{2,6},{3,1},{4,0},{5,7},{6,2},{7,5},{8,12},{9,11},{10,... | collective-permute-start | bytes 638984 | tf_op jit(solution)/shard_map/ppermute | solution.py:391
  20.3 5.8 %collective-permute-start.8 = (bf16[64,1664]{1,0:T(8,128)(2,1)S(1)}, bf16[64,1664]{1,0:T(8,128)(2,1)S(1)}, u32[]{:S(2)}, u32[]{:S(2)}) collective-permute-start(bf16[64,1664]{1,0:T(8,128)(2,1)S(1)} %collective-permute-done), channel_id=1, source_target_pairs={{0,8},{1,9},{2,10},{3,11},{4,12},{5,13},{6,14},{7,15},{8,0},{9,1},... | collective-permute-start | bytes 638984 | tf_op jit(solution)/shard_map/ppermute | solution.py:391
  20.3 8.2 %collective-permute-start.3 = (bf16[64,1664]{1,0:T(8,128)(2,1)S(1)}, bf16[64,1664]{1,0:T(8,128)(2,1)S(1)}, u32[]{:S(2)}, u32[]{:S(2)}) collective-permute-start(bf16[64,1664]{1,0:T(8,128)(2,1)S(1)} %collective-permute-done), channel_id=1, source_target_pairs={{0,4},{1,3},{2,6},{3,1},{4,0},{5,7},{6,2},{7,5},{8,12},{9,11},{10,... | collective-permute-start | bytes 638984 | tf_op jit(solution)/shard_map/ppermute | solution.py:391
  21.7 10.5 %collective-permute-start.5 = (bf16[128,1664]{1,0:T(8,128)(2,1)S(1)}, bf16[128,1664]{1,0:T(8,128)(2,1)S(1)}, u32[]{:S(2)}, u32[]{:S(2)}) collective-permute-start(bf16[128,1664]{1,0:T(8,128)(2,1)S(1)} %constant_dynamic-update-slice_fusion.rest_3_), channel_id=1, source_target_pairs={{0,2},{1,5},{2,0},{3,7},{4,6},{5,1},{6,4},{7,3},{8,10},{9,13},{10,... | collective-permute-start | bytes 1277960 | tf_op jit(solution)/shard_map/ppermute | solution.py:391
  23.3 9.4 %collective-permute-start.12 = (bf16[128,1664]{1,0:T(8,128)(2,1)S(1)}, bf16[128,1664]{1,0:T(8,128)(2,1)S(1)}, u32[]{:S(2)}, u32[]{:S(2)}) collective-permute-start(bf16[128,1664]{1,0:T(8,128)(2,1)S(1)} %constant_dynamic-update-slice_fusion.rest_3_), channel_id=1, source_target_pairs={{0,1},{1,0},{2,3},{3,2},{4,5},{5,4},{6,7},{7,6},{8,9},{9,8},{10,11... | collective-permute-start | bytes 1277960 | tf_op jit(solution)/shard_map/ppermute | solution.py:391
  23.3 10.9 %collective-permute-start.11 = (bf16[128,1664]{1,0:T(8,128)(2,1)S(1)}, bf16[128,1664]{1,0:T(8,128)(2,1)S(1)}, u32[]{:S(2)}, u32[]{:S(2)}) collective-permute-start(bf16[128,1664]{1,0:T(8,128)(2,1)S(1)} %collective-permute-done.2.rest_1_), channel_id=1, source_target_pairs={{0,1},{1,0},{2,3},{3,2},{4,5},{5,4},{6,7},{7,6},{8,9},{9,8},{10,11... | collective-permute-start | bytes 1277960 | tf_op jit(solution)/shard_map/ppermute | solution.py:391
  26.1 5.8 %collective-permute-start.9 = (bf16[64,1664]{1,0:T(8,128)(2,1)S(1)}, bf16[64,1664]{1,0:T(8,128)(2,1)S(1)}, u32[]{:S(2)}, u32[]{:S(2)}) collective-permute-start(bf16[64,1664]{1,0:T(8,128)(2,1)S(1)} %collective-permute-done.8), channel_id=1, source_target_pairs={{0,4},{1,3},{2,6},{3,1},{4,0},{5,7},{6,2},{7,5},{8,12},{9,11},{10,... | collective-permute-start | bytes 638984 | tf_op jit(solution)/shard_map/ppermute | solution.py:391
  32.0 2.8 %collective-permute-start.15 = (bf16[128,1664]{1,0:T(8,128)(2,1)S(1)}, bf16[128,1664]{1,0:T(8,128)(2,1)S(1)}, u32[]{:S(2)}, u32[]{:S(2)}) collective-permute-start(bf16[128,1664]{1,0:T(8,128)(2,1)S(1)} %constant_dynamic-update-slice_fusion.2.rest_9_), channel_id=1, source_target_pairs={{0,1},{1,0},{2,3},{3,2},{4,5},{5,4},{6,7},{7,6},{8,9},{9,8},{10,11... | collective-permute-start | bytes 1277960 | tf_op jit(solution)/shard_map/ppermute | solution.py:391
  32.2 2.6 %collective-permute-start.14 = (bf16[128,1664]{1,0:T(8,128)(2,1)S(1)}, bf16[128,1664]{1,0:T(8,128)(2,1)S(1)}, u32[]{:S(2)}, u32[]{:S(2)}) collective-permute-start(bf16[128,1664]{1,0:T(8,128)(2,1)S(1)} %pad_maximum_fusion.rest_7_), channel_id=1, source_target_pairs={{0,1},{1,0},{2,3},{3,2},{4,5},{5,4},{6,7},{7,6},{8,9},{9,8},{10,11... | collective-permute-start | bytes 1277960 | tf_op jit(solution)/shard_map/ppermute | solution.py:391
  32.6 2.5 %collective-permute-start.13 = (bf16[128,1664]{1,0:T(8,128)(2,1)S(1)}, bf16[128,1664]{1,0:T(8,128)(2,1)S(1)}, u32[]{:S(2)}, u32[]{:S(2)}) collective-permute-start(bf16[128,1664]{1,0:T(8,128)(2,1)S(1)} %collective-permute-done.5.rest_5_), channel_id=1, source_target_pairs={{0,1},{1,0},{2,3},{3,2},{4,5},{5,4},{6,7},{7,6},{8,9},{9,8},{10,11... | collective-permute-start | bytes 1277960 | tf_op jit(solution)/shard_map/ppermute | solution.py:391
  32.7 12.9 %collective-permute-start.10 = (bf16[128,1664]{1,0:T(8,128)(2,1)S(1)}, bf16[128,1664]{1,0:T(8,128)(2,1)S(1)}, u32[]{:S(2)}, u32[]{:S(2)}) collective-permute-start(bf16[128,1664]{1,0:T(8,128)(2,1)S(1)} %constant_dynamic-update-slice_fusion.2.rest_9_), channel_id=1, source_target_pairs={{0,2},{1,5},{2,0},{3,7},{4,6},{5,1},{6,4},{7,3},{8,10},{9,13},{10,... | collective-permute-start | bytes 1277960 | tf_op jit(solution)/shard_map/ppermute | solution.py:391
  34.2 11.5 %collective-permute-start.6 = (bf16[128,1664]{1,0:T(8,128)(2,1)S(1)}, bf16[128,1664]{1,0:T(8,128)(2,1)S(1)}, u32[]{:S(2)}, u32[]{:S(2)}) collective-permute-start(bf16[128,1664]{1,0:T(8,128)(2,1)S(1)} %pad_maximum_fusion.rest_7_), channel_id=1, source_target_pairs={{0,2},{1,5},{2,0},{3,7},{4,6},{5,1},{6,4},{7,3},{8,10},{9,13},{10,... | collective-permute-start | bytes 1277960 | tf_op jit(solution)/shard_map/ppermute | solution.py:391
  45.6 1.8 %collective-permute-start.16 = (bf16[128,1664]{1,0:T(8,128)(2,1)S(1)}, bf16[128,1664]{1,0:T(8,128)(2,1)S(1)}, u32[]{:S(2)}, u32[]{:S(2)}) collective-permute-start(bf16[128,1664]{1,0:T(8,128)(2,1)S(1)} %collective-permute-done.10.rest_2_), channel_id=1, source_target_pairs={{0,1},{1,0},{2,3},{3,2},{4,5},{5,4},{6,7},{7,6},{8,9},{9,8},{10,11... | collective-permute-start | bytes 1277960 | tf_op jit(solution)/shard_map/ppermute | solution.py:391
  45.8 2.2 %collective-permute-start.7 = (bf16[128,1664]{1,0:T(8,128)(2,1)S(1)}, bf16[128,1664]{1,0:T(8,128)(2,1)S(1)}, u32[]{:S(2)}, u32[]{:S(2)}) collective-permute-start(bf16[128,1664]{1,0:T(8,128)(2,1)S(1)} %collective-permute-done.6.rest_0_), channel_id=1, source_target_pairs={{0,1},{1,0},{2,3},{3,2},{4,5},{5,4},{6,7},{7,6},{8,9},{9,8},{10,11... | collective-permute-start | bytes 1277960 | tf_op jit(solution)/shard_map/ppermute | solution.py:391
